TPU v7x, 128 devices: a whole 4x4x4 slice. The times are simulated.
128 devices in a mesh: dp: 32 (over x, y, core), tensor: 4 (over z).
Axes of the slice: x: 4, y: 4, z: 4, core: 2. Of those that a mesh axis runs over, the one named last changes fastest.
Arguments:
- inputs: bfloat16 [16384, 1024], P(('dp', 'tensor')), may hold values from -6 to 6
- lengths: int32 [32], replicated, may hold values from 1 to 16, 128 in all
- w_qkv: bfloat16 [1, 1024, 3, 1024], P(None, 'dp', None, 'tensor'), may hold values from -0.1875 to 0.1875
- w_out: bfloat16 [1, 1024, 1024], P(None, 'tensor', 'dp'), may hold values from -0.75 to 0.75
- w_fc: bfloat16 [1, 1024, 4096], P(None, 'dp', 'tensor'), may hold values from -0.1875 to 0.1875
- w_proj: bfloat16 [1, 4096, 1024], P(None, 'tensor', 'dp'), may hold values from -0.09375 to 0.09375
- b_qv: bfloat16 [1, 2, 1024], P(None, None, ('tensor', 'dp')), may hold values from -3 to 3
- b_fc: bfloat16 [1, 4096], P(None, ('tensor', 'dp')), may hold values from -3 to 3
- gains: float32 [1, 2, 1024], P(None, None, ('dp', 'tensor')), may hold values from 0.5 to 1.5
- shifts: float32 [1, 4, 1024], P(None, None, ('dp', 'tensor')), may hold values from -2 to 2
- cotangent: bfloat16 [16384, 1024], P(('dp', 'tensor')), may hold values from -24 to 24
Outputs:
- outputs: float32 [16384, 1024], P(('dp', 'tensor'))
- grad_inputs: float32 [16384, 1024], P(('dp', 'tensor'))
- grad_w_qkv: float32 [1, 1024, 3, 1024], P(None, 'dp', None, 'tensor')
- grad_w_out: float32 [1, 1024, 1024], P(None, 'tensor', 'dp')
- grad_w_fc: float32 [1, 1024, 4096], P(None, 'dp', 'tensor')
- grad_w_proj: float32 [1, 4096, 1024], P(None, 'tensor', 'dp')
- grad_b_qv: float32 [1, 2, 1024], P(None, None, ('tensor', 'dp'))
- grad_b_fc: float32 [1, 4096], P(None, ('tensor', 'dp'))
- grad_gains: float32 [1, 2, 1024], P(None, None, ('dp', 'tensor'))
- grad_shifts: float32 [1, 4, 1024], P(None, None, ('dp', 'tensor'))
Inputs may be any that keep to these rules, and one draw needn't show every extreme that they name: lengths counts blocks of 128 tokens; the lengths sum to 128 and the longest is exactly 16.
All inputs are finite; a program needn't handle non-finite values.
Results may differ from a plain program's by a relative error of at most 0.012.
Values may be sent and summed in bfloat16 or wider, within the bound.
A program may use at most 192 MiB of HBM per device.

v0:
```python
import jax
import jax.numpy as jnp
from jax import lax
from jax.sharding import PartitionSpec as P

HEAD_DIM = 64
BLOCK = 128
SPAN = 4


def from_behind(value, axis, steps):
    count = lax.axis_size(axis)
    first, last = (max(0, -steps), min(count, count - steps))
    return lax.ppermute(value, axis, [(source, source + steps) for source in range(first, last)])


def layer_norm(values, gain_row, shift_row):
    centre = values - jnp.mean(values, axis=-1, keepdims=True)
    spread = jnp.mean(centre * centre, axis=-1, keepdims=True)
    return centre * lax.rsqrt(spread + 1e-05) * gain_row + shift_row


def gelu_tanh(values):
    return (
        0.5
        * values
        * (1.0 + jnp.tanh(0.7978845608028654 * (values + 0.044715 * values * values * values)))
    )


def sequence_of(lengths, positions):
    bounds = jnp.cumsum(lengths) * BLOCK
    found_seq = jnp.sum((positions[:, None] >= bounds[None, :]).astype(jnp.int32), axis=1)
    return jnp.where(positions >= 0, found_seq, -1)


def contract_rows(left_side, right_side):
    return lax.dot_general(
        left_side, right_side, (((0,), (0,)), ((), ())), preferred_element_type=jnp.float32
    )


def contract_cols(left_side, right_side):
    return lax.dot_general(
        left_side, right_side, (((1,), (1,)), ((), ())), preferred_element_type=jnp.float32
    )


def gather_rows(normed):
    return lax.all_gather(normed.astype(jnp.bfloat16), "tensor", axis=0, tiled=True)


def gather_grads(gradient):
    return lax.all_gather(gradient.astype(jnp.bfloat16), "tensor", axis=0, tiled=True)


def tensor_sum(left_side, right_side):
    row_count = left_side.shape[0] // lax.axis_size("tensor")

    def partial_value(start_row, row_num):
        return jnp.dot(left_side, right_side, preferred_element_type=jnp.float32)

    return lax.psum_scatter(
        partial_value(jnp.int32(0), row_count * lax.axis_size("tensor")),
        "tensor",
        scatter_dimension=0,
        tiled=True,
    )


def tensor_back(left_side, right_side):
    row_count = left_side.shape[0] // lax.axis_size("tensor")

    def partial_value(start_row, row_num):
        return contract_cols(left_side, right_side)

    return lax.psum_scatter(
        partial_value(jnp.int32(0), row_count * lax.axis_size("tensor")),
        "tensor",
        scatter_dimension=0,
        tiled=True,
    )


def split_heads(qkv_low, key_set):
    heads_local = qkv_low.shape[2] // HEAD_DIM
    queries = qkv_low[:, 0].reshape(qkv_low.shape[0], heads_local, HEAD_DIM)
    key_rows = key_set[:, 0].reshape(key_set.shape[0], heads_local, HEAD_DIM)
    value_rows = key_set[:, 1].reshape(key_set.shape[0], heads_local, HEAD_DIM)
    return (queries, key_rows, value_rows)


def attend_forward(qkv_low, key_set, allowed):
    queries, key_rows, value_rows = split_heads(qkv_low, key_set)
    scores = jnp.einsum(
        "qhd,khd->hqk", queries, key_rows, preferred_element_type=jnp.float32
    ) * HEAD_DIM ** (-0.5)
    masked = jnp.where(allowed[None], scores, -1e30)
    row_peak = jnp.max(masked, axis=-1, keepdims=True)
    exp_scores = jnp.exp(masked - row_peak)
    row_total = jnp.sum(exp_scores, axis=-1, keepdims=True)
    soft_weights = (exp_scores / row_total).astype(jnp.bfloat16)
    context = jnp.einsum(
        "hqk,khd->qhd", soft_weights, value_rows, preferred_element_type=jnp.float32
    )
    return (
        context.reshape(qkv_low.shape[0], -1).astype(jnp.bfloat16),
        row_peak + jnp.log(row_total),
    )


def attend_backward(qkv_low, key_set, allowed, log_total, grad_context):
    queries, key_rows, value_rows = split_heads(qkv_low, key_set)
    score_scale = HEAD_DIM ** (-0.5)
    scores = (
        jnp.einsum("qhd,khd->hqk", queries, key_rows, preferred_element_type=jnp.float32)
        * score_scale
    )
    masked = jnp.where(allowed[None], scores, -1e30)
    soft_weights = jnp.exp(masked - log_total)
    grad_heads = grad_context.reshape(queries.shape)
    grad_soft = jnp.einsum(
        "qhd,khd->hqk", grad_heads, value_rows, preferred_element_type=jnp.float32
    )
    row_inner = jnp.sum(soft_weights * grad_soft, axis=-1, keepdims=True)
    grad_scores = (soft_weights * (grad_soft - row_inner)).astype(jnp.bfloat16)
    grad_queries = (
        jnp.einsum("hqk,khd->qhd", grad_scores, key_rows, preferred_element_type=jnp.float32)
        * score_scale
    )
    grad_keys = (
        jnp.einsum("hqk,qhd->khd", grad_scores, queries, preferred_element_type=jnp.float32)
        * score_scale
    )
    grad_values = jnp.einsum(
        "hqk,qhd->khd",
        soft_weights.astype(jnp.bfloat16),
        grad_heads,
        preferred_element_type=jnp.float32,
    )
    key_count = key_set.shape[0]
    grad_pairs = jnp.stack(
        [grad_keys.reshape(key_count, -1), grad_values.reshape(key_count, -1)], axis=1
    )
    return (grad_queries.reshape(qkv_low.shape[0], -1), grad_pairs)


def on_device(inputs, lengths, w_qkv, w_out, w_fc, w_proj, b_qv, b_fc, gains, shifts, cotangent):
    levels = w_qkv.shape[0]
    all_gains, all_shifts = (
        lax.all_gather(gains, ("dp", "tensor"), axis=2, tiled=True),
        lax.all_gather(shifts, ("dp", "tensor"), axis=2, tiled=True),
    )
    group_index = lax.axis_index("dp")
    rows_dev = inputs.shape[0]
    tok_group = rows_dev * lax.axis_size("tensor")
    query_pos = group_index * tok_group + jnp.arange(tok_group, dtype=jnp.int32)
    key_pos = (group_index - SPAN) * tok_group + jnp.arange((SPAN + 1) * tok_group, dtype=jnp.int32)
    same_seq = sequence_of(lengths, query_pos)[:, None] == sequence_of(lengths, key_pos)[None, :]
    allowed = same_seq & (key_pos[None, :] <= query_pos[:, None])
    residual = inputs.astype(jnp.float32)
    layer_index = 0
    fetched = (
        lax.all_gather(w_qkv[layer_index], "dp", axis=0, tiled=True),
        lax.all_gather(w_out[layer_index], "dp", axis=1, tiled=True),
        lax.all_gather(w_fc[layer_index], "dp", axis=0, tiled=True),
        lax.all_gather(w_proj[layer_index], "dp", axis=1, tiled=True),
        lax.all_gather(b_qv[layer_index], "dp", axis=1, tiled=True),
        lax.all_gather(b_fc[layer_index], "dp", axis=0, tiled=True),
    )
    weight_qkv, weight_out, weight_fc, weight_proj, bias_qv, bias_fc = fetched
    layer_gains = all_gains[layer_index]
    layer_shifts = all_shifts[layer_index]
    gathered_one = gather_rows(layer_norm(residual, layer_gains[0], layer_shifts[0]))
    width_local = weight_qkv.shape[2]
    mixed = jnp.dot(
        gathered_one,
        weight_qkv.reshape(weight_qkv.shape[0], -1),
        preferred_element_type=jnp.float32,
    ).reshape(tok_group, 3, width_local)
    bias_low = bias_qv.astype(jnp.float32)
    bias_full = jnp.stack([bias_low[0], jnp.zeros_like(bias_low[0]), bias_low[1]])
    qkv_low = (mixed + bias_full).astype(jnp.bfloat16)
    own_pair = qkv_low[:, 1:]
    earlier = []
    passing = own_pair
    for hop_index in range(SPAN):
        passing = from_behind(passing, "dp", 1)
        earlier.append(passing)
    key_set = jnp.concatenate(earlier[::-1] + [own_pair], axis=0)
    context_low, log_total = attend_forward(qkv_low, key_set, allowed)
    after = residual + tensor_sum(context_low, weight_out) + layer_shifts[2]
    gathered_two = gather_rows(layer_norm(after, layer_gains[1], layer_shifts[1]))
    pre_act = jnp.dot(gathered_two, weight_fc, preferred_element_type=jnp.float32) + bias_fc.astype(
        jnp.float32
    )
    act_low = gelu_tanh(pre_act).astype(jnp.bfloat16)
    output_rows = after + tensor_sum(act_low, weight_proj) + layer_shifts[3]
    stored = [
        (
            residual,
            gathered_one,
            qkv_low,
            key_set,
            log_total,
            context_low,
            after,
            gathered_two,
            pre_act,
            act_low,
            fetched,
        )
    ]
    grad_res = cotangent.astype(jnp.float32)
    reduced = [None] * levels
    gain_parts = [None] * levels
    shift_parts = [None] * levels
    layer_index = 0
    (
        layer_input,
        gathered_one,
        qkv_low,
        key_set,
        log_total,
        context_low,
        after,
        gathered_two,
        pre_act,
        act_low,
        fetched,
    ) = stored[layer_index]
    weight_qkv, weight_out, weight_fc, weight_proj, bias_qv, bias_fc = fetched
    layer_gains = all_gains[layer_index]
    layer_shifts = all_shifts[layer_index]
    grad_mlp = gather_grads(grad_res)
    grad_weight_proj = contract_rows(act_low, grad_mlp)
    grad_act = contract_cols(grad_mlp, weight_proj)
    gelu_value, gelu_pull = jax.vjp(gelu_tanh, pre_act)
    grad_pre = gelu_pull(grad_act)[0].astype(jnp.bfloat16)
    grad_bias_fc = jnp.sum(grad_pre.astype(jnp.float32), axis=0)
    grad_weight_fc = contract_rows(gathered_two, grad_pre)
    grad_normed_two = tensor_back(grad_pre, weight_fc)
    norm_value, norm_pull = jax.vjp(layer_norm, after, layer_gains[1], layer_shifts[1])
    grad_after_norm, grad_gain_two, grad_shift_two = norm_pull(grad_normed_two)
    grad_after = grad_res + grad_after_norm
    grad_mlp_bias = jnp.sum(grad_res, axis=0)
    grad_attn = gather_grads(grad_after)
    grad_weight_out = contract_rows(context_low, grad_attn)
    grad_context = contract_cols(grad_attn, weight_out).astype(jnp.bfloat16)
    grad_queries, grad_pairs = attend_backward(qkv_low, key_set, allowed, log_total, grad_context)
    pair_pieces = grad_pairs.reshape(SPAN + 1, tok_group, 2, grad_pairs.shape[2])
    pair_total = pair_pieces[SPAN]
    carried = jnp.zeros_like(pair_total)
    for hop_index in range(SPAN, 0, -1):
        carried = from_behind(carried + pair_pieces[SPAN - hop_index], "dp", -1)
    pair_total = pair_total + carried
    grad_qkv = jnp.concatenate([grad_queries[:, None], pair_total], axis=1).astype(jnp.bfloat16)
    grad_qkv_wide = grad_qkv.astype(jnp.float32)
    grad_bias_qv = jnp.stack(
        [jnp.sum(grad_qkv_wide[:, 0], axis=0), jnp.sum(grad_qkv_wide[:, 2], axis=0)]
    )
    grad_flat = grad_qkv.reshape(tok_group, -1)
    grad_weight_qkv = contract_rows(gathered_one, grad_flat).reshape(weight_qkv.shape)
    grad_normed_one = tensor_back(grad_flat, weight_qkv.reshape(weight_qkv.shape[0], -1))
    norm_value, norm_pull = jax.vjp(layer_norm, layer_input, layer_gains[0], layer_shifts[0])
    grad_input_norm, grad_gain_one, grad_shift_one = norm_pull(grad_normed_one)
    grad_attn_bias = jnp.sum(grad_after, axis=0)
    grad_res = grad_after + grad_input_norm
    reduced[layer_index] = (
        lax.psum_scatter(grad_weight_qkv, "dp", scatter_dimension=0, tiled=True),
        lax.psum_scatter(grad_weight_out, "dp", scatter_dimension=1, tiled=True),
        lax.psum_scatter(grad_weight_fc, "dp", scatter_dimension=0, tiled=True),
        lax.psum_scatter(grad_weight_proj, "dp", scatter_dimension=1, tiled=True),
        lax.psum_scatter(grad_bias_qv, "dp", scatter_dimension=1, tiled=True),
        lax.psum_scatter(grad_bias_fc, "dp", scatter_dimension=0, tiled=True),
    )
    gain_parts[layer_index] = jnp.stack([grad_gain_one, grad_gain_two])
    shift_parts[layer_index] = jnp.stack(
        [grad_shift_one, grad_shift_two, grad_attn_bias, grad_mlp_bias]
    )
    grad_gains, grad_shifts = (
        lax.psum_scatter(jnp.stack(gain_parts), ("dp", "tensor"), scatter_dimension=2, tiled=True),
        lax.psum_scatter(jnp.stack(shift_parts), ("dp", "tensor"), scatter_dimension=2, tiled=True),
    )
    grad_w_qkv = jnp.stack([reduced[0][0]])
    grad_w_out = jnp.stack([reduced[0][1]])
    grad_w_fc = jnp.stack([reduced[0][2]])
    grad_w_proj = jnp.stack([reduced[0][3]])
    grad_b_qv = jnp.stack([reduced[0][4]])
    grad_b_fc = jnp.stack([reduced[0][5]])
    return (
        output_rows,
        grad_res,
        grad_w_qkv,
        grad_w_out,
        grad_w_fc,
        grad_w_proj,
        grad_b_qv,
        grad_b_fc,
        grad_gains,
        grad_shifts,
    )


def solution(mesh):
    return jax.shard_map(
        on_device,
        mesh=mesh,
        in_specs=(
            P(("dp", "tensor"), None),
            P(),
            P(None, "dp", None, "tensor"),
            P(None, "tensor", "dp"),
            P(None, "dp", "tensor"),
            P(None, "tensor", "dp"),
            P(None, None, ("tensor", "dp")),
            P(None, ("tensor", "dp")),
            P(None, None, ("dp", "tensor")),
            P(None, None, ("dp", "tensor")),
            P(("dp", "tensor"), None),
        ),
        out_specs=(
            P(("dp", "tensor"), None),
            P(("dp", "tensor"), None),
            P(None, "dp", None, "tensor"),
            P(None, "tensor", "dp"),
            P(None, "dp", "tensor"),
            P(None, "tensor", "dp"),
            P(None, None, ("tensor", "dp")),
            P(None, ("tensor", "dp")),
            P(None, None, ("dp", "tensor")),
            P(None, None, ("dp", "tensor")),
        ),
        check_vma=False,
    )
```

profile of v0, /device:TPU:0, one launch (start us, length us, event | category | flops | bytes accessed | tf_op | source)
XLA Modules:
  0.0 1039.8 jit_solution(5257042540494097951)
XLA Ops:
  9.5 54.9 %all_gather.36 = f32[1,2,1024]{1,0,2:T(1,128)S(1)} all-gather(f32[1,2,8]{1,0,2:T(1,128)S(1)} %copy.53), channel_id=1, replica_groups=mesh['dp'=32,'tensor'=4] {'dp','tensor'}, dimensions={2}, use_global_device_ids=true | all-gather | bytes 8256 | tf_op jit(solution)/shard_map/all_gather | solution.py:151
  64.4 51.6 %all_gather.37 = f32[1,4,1024]{1,0,2:T(1,128)S(1)} all-gather(f32[1,4,8]{1,0,2:T(1,128)S(1)} %copy.54), channel_id=1, replica_groups=mesh['dp'=32,'tensor'=4] {'dp','tensor'}, dimensions={2}, use_global_device_ids=true | all-gather | bytes 16512 | tf_op jit(solution)/shard_map/all_gather | solution.py:152
  118.7 6.2 slice_reduce_fusion.4
  124.9 21.7 %slice_reduce_fusion.2 = (f32[1024]{0:T(1024)S(1)}, f32[1024]{0:T(1024)S(1)}, f32[1024]{0:T(1024)S(1)}, f32[1024]{0:T(1024)S(1)}) fusion(f32[1,4,1024]{1,0,2:T(1,128)S(1)} %all_gather.37), kind=kLoop, calls=%fused_computation.84 | loop fusion | bytes 32768 | tf_op jit(solution)/shard_map/slice | solution.py:198
  147.8 23.5 %all-gather.1 = bf16[1,2,256]{1,0,2:T(2,128)(2,1)S(1)} all-gather(bf16[1,2,8]{1,0,2:T(2,128)(2,1)S(1)} %copy.56), channel_id=3, replica_groups=mesh['dp'=32,'tensor'=4] {'dp'}, dimensions={2}, use_global_device_ids=true | all-gather | bytes 1056 | tf_op jit(solution)/shard_map/all_gather | solution.py:168
  171.5 3.6 slice_reduce_fusion.9
  175.2 1.7 copy.55
  177.0 2.2 add_convert_fusion
  179.2 2.3 collective-permute-start
  181.5 1.5 collective-permute-done
  183.0 6.7 collective-permute-start.1
  190.2 29.8 %all-gather.2 = bf16[1,256,1024]{1,2,0:T(8,128)(2,1)} all-gather(bf16[1,256,32]{1,2,0:T(8,128)(2,1)S(1)} %copy-done.19), channel_id=4, replica_groups=mesh['dp'=32,'tensor'=4] {'dp'}, dimensions={2}, use_global_device_ids=true | all-gather | bytes 540672 | tf_op jit(solution)/shard_map/all_gather | solution.py:165
  220.0 2.3 collective-permute-start.2
  222.4 1.4 collective-permute-done.2
  223.7 6.7 collective-permute-start.3
  233.4 4.1 fusion.68
  237.6 5.1 fusion
  242.6 1.9 copy-done
  244.5 6.2 fusion.27
  250.8 3.0 fusion.53
  254.4 38.7 %reduce-scatter.12.cloned.1.call-done = f32[128,1024]{1,0:T(8,128)} async-done(((f32[512,1024]{1,0:T(8,128)}), f32[128,1024]{1,0:T(8,128)}) %reduce-scatter.12.cloned.1.call-update) | async-done | bytes 524304 | tf_op jit(solution)/shard_map/reduce_scatter | solution.py:63
  298.3 67.3 %all-reduce = bf16[1024]{0:T(1024)(128)(2,1)S(1)} all-reduce(bf16[1024]{0:T(1024)(128)(2,1)S(1)} %dynamic-update-slice), channel_id=6, replica_groups=mesh['dp'=32,'tensor'=4] {'dp'}, use_global_device_ids=true, to_apply=%add | all-reduce | flops 1024 | bytes 4096
  365.6 4.5 fusion.18
  370.1 20.8 %all-gather.18.cloned.1.call-done = bf16[512,1024]{1,0:T(8,128)(2,1)} async-done(((bf16[128,1024]{1,0:T(8,128)(2,1)}), bf16[512,1024]{1,0:T(8,128)(2,1)}) %all-gather.18.cloned.1.call-update) | async-done | bytes 1048592 | tf_op jit(solution)/shard_map/all_gather | solution.py:54
  390.9 46.6 %all-gather.26.cloned.1.call-done = bf16[1,1024,1024]{1,2,0:T(8,128)(2,1)} async-done(((bf16[1,1024,32]{1,2,0:T(8,128)(2,1)}), bf16[1,1024,1024]{1,2,0:T(8,128)(2,1)}) %all-gather.26.cloned.1.call-update) | async-done | bytes 2097168 | tf_op jit(solution)/shard_map/all_gather | solution.py:167
  437.5 5.3 convert_reduce_fusion
  442.9 4.6 fusion.16
  447.6 1.5 copy-done.27
  449.1 4.4 fusion.14
  453.6 23.3 %reduce-scatter.16.cloned.1.call-done = f32[128,1024]{1,0:T(8,128)} async-done(((f32[512,1024]{1,0:T(8,128)}), f32[128,1024]{1,0:T(8,128)}) %reduce-scatter.16.cloned.1.call-update) | async-done | bytes 524304 | tf_op jit(solution)/shard_map/reduce_scatter | solution.py:77
  478.2 30.6 %reduce-scatter.14.cloned.1.call-done = f32[128,1024]{1,0:T(8,128)} async-done(((f32[512,1024]{1,0:T(8,128)}), f32[128,1024]{1,0:T(8,128)}) %reduce-scatter.14.cloned.1.call-update) | async-done | bytes 524304 | tf_op jit(solution)/shard_map/reduce_scatter | solution.py:63
  508.8 2.2 fusion.63
  512.1 23.6 %all-gather.20.cloned.1.call-done = bf16[512,1024]{1,0:T(8,128)(2,1)} async-done(((bf16[128,1024]{1,0:T(8,128)(2,1)}), bf16[512,1024]{1,0:T(8,128)(2,1)}) %all-gather.20.cloned.1.call-update) | async-done | bytes 1048592 | tf_op jit(solution)/shard_map/all_gather | solution.py:54
  535.8 1.7 convolution_convert_fusion
  537.5 10.4 %fusion.2 = f32[4,64,2560]{2,1,0:T(8,128)} fusion(bf16[512,4,64]{0,2,1:T(8,128)(2,1)S(1)} %bitcast.124, f32[4,512,2560]{2,1,0:T(8,128)} %copy-done, f32[4,512]{1,0:T(4,128)S(1)} %log_add_fusion), kind=kOutput, calls=%fused_computation.8 | convolution fusion | flops 681574400 | bytes 23863296 | tf_op jit(solution)/shard_map/hqk,qhd->khd/dot_general | solution.py:135
  547.9 13.1 %multiply_reduce_fusion = (f32[4,512]{1,0:T(4,128)S(1)}, f32[4,512,2560]{2,1,0:T(8,128)}) fusion(f32[4,512,2560]{2,1,0:T(8,128)} %copy-done, f32[4,512]{1,0:T(4,128)S(1)} %log_add_fusion, bf16[512,4,64]{0,2,1:T(8,128)(2,1)S(1)} %bitcast.125, bf16[2560,4,64]{0,2,1:T(8,128)(2,1)S(1)} %bitcast.123), kind=kOutput, calls=%fused_computation.1 | convolution fusion | flops 686815232 | bytes 43532288 | tf_op jit(solution)/shard_map/qhd,khd->hqk/dot_general | solution.py:122
  561.0 2.1 copy.59
  563.2 14.4 %multiply_convert_fusion = bf16[4,512,2560]{2,1,0:T(8,128)(2,1)S(1)} fusion(f32[4,512,2560]{2,1,0:T(8,128)} %get-tuple-element.48, f32[4,512,2560]{2,1,0:T(8,128)} %copy-done, f32[4,512]{1,0:T(4,128)S(1)} %get-tuple-element.47, f32[4,512]{1,0:T(4,128)S(1)} %log_add_fusion), kind=kLoop, calls=%fused_computation | loop fusion | flops 20971520 | bytes 52445184 | tf_op jit(solution)/shard_map/convert_element_type | solution.py:126
  577.6 3.9 convolution_multiply_fusion
  582.3 3.2 copy.58
  586.8 1.6 collective-permute-start.4
  588.4 3.3 collective-permute-done.4
  591.8 1.4 collective-permute-start.5
  593.2 14.3 %collective-permute-done.5 = f32[512,2,256]{2,0,1:T(8,128)S(1)} collective-permute-done((f32[512,2,256]{2,0,1:T(8,128)S(1)}, f32[512,2,256]{2,0,1:T(8,128)S(1)}, u32[]{:S(2)}, u32[]{:S(2)}) %collective-permute-start.5) | collective-permute-done | bytes 1048608 | tf_op jit(solution)/shard_map/ppermute | solution.py:14
  607.7 1.4 collective-permute-start.6
  609.2 14.8 %collective-permute-done.6 = f32[512,2,256]{2,0,1:T(8,128)S(1)} collective-permute-done((f32[512,2,256]{2,0,1:T(8,128)S(1)}, f32[512,2,256]{2,0,1:T(8,128)S(1)}, u32[]{:S(2)}, u32[]{:S(2)}) %collective-permute-start.6) | collective-permute-done | bytes 1048608 | tf_op jit(solution)/shard_map/ppermute | solution.py:14
  626.5 4.0 convolution_multiply_fusion.1
  630.4 1.8 copy.60
  632.2 9.4 collective-permute-done.7
  641.6 1.5 fusion.31
  643.2 1.5 copy-done.16
  644.7 2.4 convolution_bitcast_fusion
  648.4 5.0 fusion.60
  654.6 4.5 fusion.70
  660.3 2.5 fusion.69
  662.8 1.4 copy.61
  664.3 4.0 fusion.36
  669.8 75.8 %all-reduce.6 = (f32[2,256]{1,0:T(2,128)S(1)}, f32[1024]{0:T(1024)S(1)}) all-reduce(f32[2,256]{1,0:T(2,128)S(1)} %pad_maximum_fusion.2, f32[1024]{0:T(1024)S(1)} %get-tuple-element.49), channel_id=16, replica_groups=mesh['dp'=32,'tensor'=4] {'dp'}, use_global_device_ids=true, to_apply=%region_24.25.clone | all-reduce | flops 1536 | bytes 12288
  748.1 1.4 fusion.48
  749.5 63.9 %all-reduce.5 = (f32[1,2,1024]{2,1,0:T(2,128)S(1)}, f32[1,4,1024]{2,1,0:T(4,128)S(1)}) all-reduce(f32[1,2,1024]{2,1,0:T(2,128)S(1)} %maximum_bitcast_fusion.1, f32[1,4,1024]{2,1,0:T(4,128)S(1)} %maximum_bitcast_fusion), channel_id=18, replica_groups=mesh['dp'=32,'tensor'=4] {'dp','tensor'}, use_global_device_ids=true, to_apply=%region_29.30.clone | all-reduce | flops 6144 | bytes 49152
  814.7 2.1 add_add_fusion.2
  816.9 51.1 %reduce-scatter.24.cloned.1.call-done = f32[32,1024]{1,0:T(8,128)} async-done(((f32[1024,1024]{1,0:T(8,128)}), f32[32,1024]{1,0:T(8,128)}) %reduce-scatter.24.cloned.1.call-update) | async-done | bytes 131088 | tf_op jit(solution)/shard_map/reduce_scatter | solution.py:272
  868.0 80.7 %reduce-scatter.22.cloned.1.call-done = f32[256,32]{0,1:T(8,128)} async-done(((f32[256,1024]{0,1:T(8,128)}), f32[256,32]{0,1:T(8,128)}) %reduce-scatter.22.cloned.1.call-update) | async-done | bytes 32784 | tf_op jit(solution)/shard_map/reduce_scatter | solution.py:271
  948.7 84.1 %reduce-scatter.20.cloned.1.call-done = f32[32,3,256]{2,0,1:T(8,128)} async-done(((f32[1024,3,256]{2,0,1:T(8,128)}), f32[32,3,256]{2,0,1:T(8,128)}) %reduce-scatter.20.cloned.1.call-update) | async-done | bytes 98320 | tf_op jit(solution)/shard_map/reduce_scatter | solution.py:270
  (162 shorter events, 30.2 us)
Async XLA Ops:
  7.2 168.0 %all-gather.22.cloned.1.call-start = ((), (), s32[]{:S(2)}) async-start(), calls=%async_computation.20 | async-start | bytes 1622016 | tf_op jit(solution)/shard_map/all_gather | solution.py:164
  7.9 169.0 %all-gather.14.cloned.1.call-start = ((), (), s32[]{:S(2)}) async-start(), calls=%async_computation.8 | async-start | bytes 1310720 | tf_op jit(solution)/shard_map/all_gather | solution.py:50
  64.4 82.3 %copy-start.5 = (bf16[128,1024]{1,0:T(8,128)(2,1)S(1)}, bf16[128,1024]{1,0:T(8,128)(2,1)}, u32[]{:S(2)}) copy-start(bf16[128,1024]{1,0:T(8,128)(2,1)} %param.11) | copy-start | bytes 786436
  117.0 30.7 %copy-start.25 = (bf16[1,2,8]{2,1,0:T(2,128)(2,1)S(1)}, bf16[1,2,8]{2,1,0:T(2,128)(2,1)}, u32[]{:S(2)}) copy-start(bf16[1,2,8]{2,1,0:T(2,128)(2,1)} %param.17) | copy-start | bytes 100
  118.2 0.5 copy-start.23
  118.7 52.7 %copy-start.20 = (f32[128]{0:T(128)}, f32[128]{0:T(128)S(1)}, u32[]{:S(2)}) copy-start(f32[128]{0:T(128)S(1)} %fusion.55) | copy-start | bytes 1540
  147.7 145.4 %reduce-scatter.12.cloned.1.call-start = ((), (), s32[]{:S(2)}) async-start(), calls=%async_computation.9 | async-start | bytes 2621440 | tf_op jit(solution)/shard_map/reduce_scatter | solution.py:63
  176.9 12.8 %copy-start.26 = (s32[32]{0:T(128)S(1)}, s32[32]{0:T(128)}, u32[]{:S(2)}) copy-start(s32[32]{0:T(128)} %param.12) | copy-start | bytes 388
  176.9 13.2 %copy-start.19 = (bf16[1,256,32]{1,2,0:T(8,128)(2,1)S(1)}, bf16[1,256,32]{1,2,0:T(8,128)(2,1)}, u32[]{:S(2)}) copy-start(bf16[1,256,32]{1,2,0:T(8,128)(2,1)} %param.14) | copy-start | bytes 49156
  179.2 3.8 collective-permute-start
  183.0 36.9 %collective-permute-start.1 = (bf16[512,2,256]{0,2,1:T(8,128)(2,1)S(1)}, bf16[512,2,256]{0,2,1:T(8,128)(2,1)S(1)}, u32[]{:S(2)}, u32[]{:S(2)}) collective-permute-start(bf16[512,2,256]{0,2,1:T(8,128)(2,1)S(1)} %collective-permute-done), channel_id=1, source_target_pairs={{0,4},{4,8},{8,12},{12,16},{16,20},{20,24},{24,28},{28,32},{32,36}... | collective-permute-start | bytes 1572872 | tf_op jit(solution)/shard_map/ppermute | solution.py:14
  220.0 3.8 collective-permute-start.2
  223.7 8.2 collective-permute-start.3
  231.6 1.8 copy-start.10
  233.4 4.1 copy-start.3
  237.5 7.0 copy-start
  250.7 42.3 %copy-start.6 = (bf16[128,1024]{1,0:T(8,128)(2,1)S(1)}, bf16[128,1024]{1,0:T(8,128)(2,1)}, u32[]{:S(2)}) copy-start(bf16[128,1024]{1,0:T(8,128)(2,1)} %param.11) | copy-start | bytes 786436
  253.8 43.0 %copy-start.22 = (u32[128]{0:T(128)S(1)}, u32[128]{0:T(128)}, u32[]{:S(2)}) copy-start(u32[128]{0:T(128)} %constant.62) | copy-start | bytes 1540
  253.8 44.3 %copy-start.29 = (bf16[1,32]{1,0:T(2,128)(2,1)S(1)}, bf16[1,32]{1,0:T(2,128)(2,1)}, u32[]{:S(2)}) copy-start(bf16[1,32]{1,0:T(2,128)(2,1)} %param.18) | copy-start | bytes 196
  253.8 111.8 %all-gather.24.cloned.1.call-start = ((), (), s32[]{:S(2)}) async-start(), calls=%async_computation.21 | async-start | bytes 2162688 | tf_op jit(solution)/shard_map/all_gather | solution.py:166
  254.4 111.2 %all-gather.16.cloned.1.call-start = ((), (), s32[]{:S(2)}) async-start(), calls=%async_computation.10 | async-start | bytes 1310720 | tf_op jit(solution)/shard_map/all_gather | solution.py:50
  295.4 95.5 %all-gather.18.cloned.1.call-start = ((), (), s32[]{:S(2)}) async-start(), calls=%async_computation.12 | async-start | bytes 1310720 | tf_op jit(solution)/shard_map/all_gather | solution.py:54
  296.0 141.6 %all-gather.26.cloned.1.call-start = ((), (), s32[]{:S(2)}) async-start(), calls=%async_computation.22 | async-start | bytes 2162688 | tf_op jit(solution)/shard_map/all_gather | solution.py:167
  296.7 180.2 %reduce-scatter.16.cloned.1.call-start = ((), (), s32[]{:S(2)}) async-start(), calls=%async_computation.13 | async-start | bytes 2621440 | tf_op jit(solution)/shard_map/reduce_scatter | solution.py:77
  442.9 4.7 copy-start.18
  447.5 1.6 copy-start.27
  447.6 61.2 %reduce-scatter.14.cloned.1.call-start = ((), (), s32[]{:S(2)}) async-start(), calls=%async_computation.11 | async-start | bytes 2621440 | tf_op jit(solution)/shard_map/reduce_scatter | solution.py:63
  453.6 57.4 %copy-start.13 = (bf16[128,1024]{1,0:T(8,128)(2,1)S(1)}, bf16[128,1024]{1,0:T(8,128)(2,1)}, u32[]{:S(2)}) copy-start(bf16[128,1024]{1,0:T(8,128)(2,1)} %param.21) | copy-start | bytes 786436
  453.6 82.2 %all-gather.20.cloned.1.call-start = ((), (), s32[]{:S(2)}) async-start(), calls=%async_computation.14 | async-start | bytes 1310720 | tf_op jit(solution)/shard_map/all_gather | solution.py:54
  478.2 57.6 %copy-start.8 = (bf16[1,256,1024]{1,2,0:T(8,128)(2,1)S(1)}, bf16[1,256,1024]{1,2,0:T(8,128)(2,1)}, u32[]{:S(2)}) copy-start(bf16[1,256,1024]{1,2,0:T(8,128)(2,1)} %all-gather.2) | copy-start | bytes 1572868
  511.8 234.9 %reduce-scatter.18.cloned.1.call-start = ((), (), s32[]{:S(2)}) async-start(), calls=%async_computation.15 | async-start | bytes 2621440 | tf_op jit(solution)/shard_map/reduce_scatter | solution.py:77
  537.5 10.4 %copy-start.7 = (bf16[2560,1,256]{0,2,1:T(8,128)(2,1)S(1)}, bf16[2560,1,256]{0,2,1:T(8,128)(2,1)}, u32[]{:S(2)}) copy-start(bf16[2560,1,256]{0,2,1:T(8,128)(2,1)} %get-tuple-element.40) | copy-start | bytes 3932164
  563.2 14.4 %copy-start.11 = (bf16[512,1,256]{0,2,1:T(8,128)(2,1)S(1)}, bf16[512,1,256]{0,2,1:T(8,128)(2,1)}, u32[]{:S(2)}) copy-start(bf16[512,1,256]{0,2,1:T(8,128)(2,1)} %copy-done.10) | copy-start | bytes 786436
  577.6 4.7 copy-start.2
  585.5 6.1 copy-start.1
  585.5 40.9 %slice-start = ((s8[10485760]{0:T(1024)(128)(4,1)}), s8[4194304]{0:T(1024)(128)(4,1)S(1)}, s32[]{:S(2)}) async-start(s8[10485760]{0:T(1024)(128)(4,1)} %bitcast.116), calls=%async_computation.23 | async-start | bytes 8388608
  586.8 39.6 %slice-start.1 = ((s8[10485760]{0:T(1024)(128)(4,1)}), s8[4194304]{0:T(1024)(128)(4,1)S(1)}, s32[]{:S(2)}) async-start(s8[10485760]{0:T(1024)(128)(4,1)} %bitcast.116), calls=%async_computation.24 | async-start | bytes 8388608
  586.8 4.8 collective-permute-start.4
  591.8 34.6 %slice-start.2 = ((s8[10485760]{0:T(1024)(128)(4,1)}), s8[2097152]{0:T(1024)(128)(4,1)S(1)}, s32[]{:S(2)}) async-start(s8[10485760]{0:T(1024)(128)(4,1)} %bitcast.116), calls=%async_computation.25 | async-start | bytes 4194304
  591.8 15.7 %collective-permute-start.5 = (f32[512,2,256]{2,0,1:T(8,128)S(1)}, f32[512,2,256]{2,0,1:T(8,128)S(1)}, u32[]{:S(2)}, u32[]{:S(2)}) collective-permute-start(f32[512,2,256]{2,0,1:T(8,128)S(1)} %fusion.34), channel_id=1, source_target_pairs={{4,0},{8,4},{12,8},{16,12},{20,16},{24,20},{28,24},{32,28},{36,32}... | collective-permute-start | bytes 3145736 | tf_op jit(solution)/shard_map/ppermute | solution.py:14
  607.7 18.7 %copy-start.4 = (bf16[2560,1,256]{0,2,1:T(8,128)(2,1)S(1)}, bf16[2560,1,256]{0,2,1:T(8,128)(2,1)}, u32[]{:S(2)}) copy-start(bf16[2560,1,256]{0,2,1:T(8,128)(2,1)} %copy-done.3) | copy-start | bytes 3932164
  607.7 16.2 %collective-permute-start.6 = (f32[512,2,256]{2,0,1:T(8,128)S(1)}, f32[512,2,256]{2,0,1:T(8,128)S(1)}, u32[]{:S(2)}, u32[]{:S(2)}) collective-permute-start(f32[512,2,256]{2,0,1:T(8,128)S(1)} %fusion.29), channel_id=1, source_target_pairs={{4,0},{8,4},{12,8},{16,12},{20,16},{24,20},{28,24},{32,28},{36,32}... | collective-permute-start | bytes 3145736 | tf_op jit(solution)/shard_map/ppermute | solution.py:14
  625.1 16.4 %collective-permute-start.7 = (f32[512,2,256]{2,0,1:T(8,128)}, f32[512,2,256]{2,0,1:T(8,128)}, u32[]{:S(2)}, u32[]{:S(2)}) collective-permute-start(f32[512,2,256]{2,0,1:T(8,128)} %fusion.35), channel_id=1, source_target_pairs={{4,0},{8,4},{12,8},{16,12},{20,16},{24,20},{28,24},{32,28},{36,32}... | collective-permute-start | bytes 3145736 | tf_op jit(solution)/shard_map/ppermute | solution.py:14
  632.2 10.8 %copy-start.17 = (bf16[512,1,256]{2,0,1:T(8,128)(2,1)S(1)}, bf16[512,1,256]{2,0,1:T(8,128)(2,1)}, u32[]{:S(2)}) copy-start(bf16[512,1,256]{2,0,1:T(8,128)(2,1)} %copy.60) | copy-start | bytes 786436
  643.0 1.7 copy-start.16
  643.2 4.0 copy-start.12
  647.2 1.2 copy-start.28
  647.2 169.7 %reduce-scatter.26.cloned.1.call-start = ((), (), s32[]{:S(2)}) async-start(), calls=%async_computation.19 | async-start | bytes 4325376 | tf_op jit(solution)/shard_map/reduce_scatter | solution.py:273
  653.4 1.2 copy-start.15
  653.4 214.6 %reduce-scatter.24.cloned.1.call-start = ((), (), s32[]{:S(2)}) async-start(), calls=%async_computation.18 | async-start | bytes 4325376 | tf_op jit(solution)/shard_map/reduce_scatter | solution.py:272
  659.1 1.2 copy-start.9
  659.1 289.6 %reduce-scatter.22.cloned.1.call-start = ((), (), s32[]{:S(2)}) async-start(), calls=%async_computation.17 | async-start | bytes 1081344 | tf_op jit(solution)/shard_map/reduce_scatter | solution.py:271
  662.8 370.1 %reduce-scatter.20.cloned.1.call-start = ((), (), s32[]{:S(2)}) async-start(), calls=%async_computation.16 | async-start | bytes 3244032 | tf_op jit(solution)/shard_map/reduce_scatter | solution.py:270
  668.3 79.8 %copy-start.24 = (f32[128]{0:T(128)S(1)}, f32[128]{0:T(128)}, u32[]{:S(2)}) copy-start(f32[128]{0:T(128)} %copy-done.23) | copy-start | bytes 1540
  668.3 79.8 %copy-start.21 = (f32[128]{0:T(128)S(1)}, f32[128]{0:T(128)}, u32[]{:S(2)}) copy-start(f32[128]{0:T(128)} %copy-done.20) | copy-start | bytes 1540
  668.3 146.4 %copy-start.14 = (bf16[128,1024]{1,0:T(8,128)(2,1)S(1)}, bf16[128,1024]{1,0:T(8,128)(2,1)}, u32[]{:S(2)}) copy-start(bf16[128,1024]{1,0:T(8,128)(2,1)} %param.21) | copy-start | bytes 786436
Sparse Core Ops, SparseCore 0:
  10.4 45.5 all-gather.21
  147.8 22.4 all-gather.13
  253.9 39.1 reduce-scatter.11
  295.4 43.3 all-gather.23
  341.0 23.6 all-gather.15
  366.3 24.5 all-gather.17
  393.4 44.0 all-gather.25
  447.7 29.1 reduce-scatter.15
  479.3 29.4 reduce-scatter.13
  512.0 23.7 all-gather.19
  647.3 48.9 reduce-scatter.17
  700.4 81.6 reduce-scatter.25
  786.7 81.2 reduce-scatter.23
  871.9 76.7 reduce-scatter.21
  953.2 79.6 reduce-scatter.19
where the time goes:
time: 1050 us; the launch traced here: 1040 us
  waiting for transfers between devices  447 us (43%)
  blocking collectives  367 us (35%)
  matrix products  86 us (8%)
  local copies, waits for them, and re-layouts  58 us (6%)
  other arithmetic  40.3 us (4%)
  starting transfers between devices  24.7 us (2%)
  between operations  17 us (2%)
    unnamed x3, blocking collectives  207 us
    reduce_scatter x1, waiting for transfers between devices, on_device(): lax.psum_scatter(grad_weight_qkv, 'dp', scatter_dimension=0, tiled=True)  84.1 us
    reduce_scatter x1, waiting for transfers between devices, on_device(): lax.psum_scatter(grad_weight_out, 'dp', scatter_dimension=1, tiled=True)  80.7 us
    reduce_scatter x2, waiting for transfers between devices, tensor_sum(): lax.psum_scatter(partial_value(jnp.int32(0), row_count * lax.axis_size('t...  69.2 us
    all_gather x1, blocking collectives, on_device(): lax.all_gather(gains, ('dp', 'tensor'), axis=2, tiled=True)  54.9 us
    all_gather x1, blocking collectives, on_device(): lax.all_gather(shifts, ('dp', 'tensor'), axis=2, tiled=True)  51.6 us
    reduce_scatter x1, waiting for transfers between devices, on_device(): lax.psum_scatter(grad_weight_fc, 'dp', scatter_dimension=0, tiled=True)  51.1 us
    all_gather x1, waiting for transfers between devices, on_device(): lax.all_gather(w_proj[layer_index], 'dp', axis=1, tiled=True)  46.6 us
  transfers between devices with their start and end apart: 23, of which 16 were waited for; matrix products, arithmetic and copies ran while one was open for 8% of the time, Pallas kernels for 0%

commit v1 on v0

--- a/solution.py
+++ b/solution.py
@@ -1,10 +1,374 @@
+import functools
+
 import jax
 import jax.numpy as jnp
 from jax import lax
+from jax.experimental import pallas as pl
+from jax.experimental.pallas import tpu as pltpu
 from jax.sharding import PartitionSpec as P
 
 HEAD_DIM = 64
 BLOCK = 128
+D = 1024
+GROUP = 512
+BF = jnp.bfloat16
+F32 = jnp.float32
+MESH = pl.DeviceIdType.MESH
+VMEM_LIMIT = 58 * 1024 * 1024
+
+
+def nn(a, b):
+    return jnp.dot(a, b, preferred_element_type=F32)
+
+
+def nt(a, b):
+    return lax.dot_general(a, b, (((1,), (1,)), ((), ())), preferred_element_type=F32)
+
+
+def tn(a, b):
+    return lax.dot_general(a, b, (((0,), (0,)), ((), ())), preferred_element_type=F32)
+
+
+def rows(start, size, step=None):
+    return pl.ds(pl.multiple_of(start, step or size), size)
+
+
+class Place:
+    def __init__(self):
+        self.dp = lax.axis_index("dp")
+        self.z = lax.axis_index("tensor")
+        self.c = lax.rem(self.dp, 2)
+        self.chip = self.dp // 2
+        self.y = lax.rem(self.chip, 4)
+        self.x = self.chip // 4
+
+    def at(self, dx=0, dy=0, dz=0, flip=False):
+        x = lax.rem(self.x + dx + 4, 4)
+        y = lax.rem(self.y + dy + 4, 4)
+        c = 1 - self.c if flip else self.c
+        return ((x * 4 + y) * 2 + c, lax.rem(self.z + dz + 4, 4))
+
+    def linear(self, step):
+        return (lax.rem(self.chip + step + 16, 16) * 2 + self.c, self.z)
+
+
+class Copies:
+    def __init__(self, send_sem, recv_sem):
+        self.send_sem, self.recv_sem = send_sem, recv_sem
+        self.started = []
+
+    def put(self, src, dst, device):
+        k = len(self.started)
+        copy = pltpu.make_async_remote_copy(
+            src_ref=src,
+            dst_ref=dst,
+            send_sem=self.send_sem.at[k],
+            recv_sem=self.recv_sem.at[k],
+            device_id=device,
+            device_id_type=MESH,
+        )
+        copy.start()
+        self.started.append(copy)
+        return copy
+
+    def finish(self):
+        for copy in self.started:
+            copy.wait_send()
+
+
+def greet(devices):
+    barrier = pltpu.get_barrier_semaphore()
+    for device in devices:
+        pl.semaphore_signal(barrier, inc=1, device_id=device, device_id_type=MESH)
+    pl.semaphore_wait(barrier, len(devices))
+
+
+class RingGather:
+    def __init__(self, copies, place, buf, size=BLOCK):
+        self.copies, self.place, self.buf, self.size = copies, place, buf, size
+
+    def block(self, dz, part=None):
+        start = lax.rem(self.place.z + dz + 4, 4) * self.size
+        if part is None:
+            return self.buf.at[rows(start, self.size)]
+        half = self.size // 2
+        return self.buf.at[rows(start + part * half, half)]
+
+    def start(self):
+        own = self.block(0)
+        self.up = self.copies.put(own, own, self.place.at(dz=1))
+        self.down = self.copies.put(own, own, self.place.at(dz=-1))
+
+    def below(self):
+        self.up.wait_recv()
+        half = self.block(-1, 0)
+        self.up2 = self.copies.put(half, half, self.place.at(dz=1))
+
+    def above(self):
+        self.down.wait_recv()
+        half = self.block(1, 1)
+        self.down2 = self.copies.put(half, half, self.place.at(dz=-1))
+
+    def far(self):
+        self.up2.wait_recv()
+        self.down2.wait_recv()
+
+
+class PlaneGather:
+    def __init__(self, copies, place, w, first, width):
+        self.copies, self.place, self.w = copies, place, w
+        c = place.c
+        self.first, self.width = first, width
+        self.cols = pl.ds(pl.multiple_of(first + c * (width // 2), 128), width // 2)
+        self.near = 1 - c, c
+
+    def dev(self, axis, step):
+        c = self.place.c
+        if axis == 0:
+            return self.place.at(dx=c * step, dy=(1 - c) * step)
+        return self.place.at(dx=(1 - c) * step, dy=c * step)
+
+    def block(self, first_off, second_off, part=None):
+        p, c = self.place, self.place.c
+        a = lax.rem(p.y * (1 - c) + p.x * c + first_off + 4, 4)
+        b = lax.rem(p.x * (1 - c) + p.y * c + second_off + 4, 4)
+        x = b * (1 - c) + a * c
+        y = a * (1 - c) + b * c
+        start = (x * 4 + y) * 64
+        if part is None:
+            return self.w.at[rows(start, 64), self.cols]
+        return self.w.at[rows(start + 32 * part, 32), self.cols]
+
+    def put(self, ref, device):
+        return self.copies.put(ref, ref, device)
+
+    def start(self):
+        p = self.place
+        mine = self.w.at[rows(p.dp * 32, 32), pl.ds(self.first, self.width)]
+        self.swap = self.put(mine, p.at(flip=True))
+
+    def spread(self, first_off):
+        ref = self.block(first_off, 0)
+        return (self.put(ref, self.dev(1, 1)), self.put(ref, self.dev(1, -1)))
+
+    def share(self, first_off, second_off):
+        self.shared.append(self.put(self.block(first_off, second_off), self.place.at(flip=True)))
+
+    def step1(self):
+        self.swap.wait_recv()
+        ref = self.block(0, 0)
+        self.shared = []
+        self.up = self.put(ref, self.dev(0, 1))
+        self.down = self.put(ref, self.dev(0, -1))
+        self.out = {0: self.spread(0)}
+
+    def step2(self):
+        self.up.wait_recv()
+        self.up2 = self.put(self.block(-1, 0, 0), self.dev(0, 1))
+        self.down.wait_recv()
+        self.down2 = self.put(self.block(1, 0, 1), self.dev(0, -1))
+        self.out[-1] = self.spread(-1)
+        self.out[1] = self.spread(1)
+        self.share(-1, 0)
+        self.share(1, 0)
+
+    def step3(self):
+        self.up2.wait_recv()
+        self.down2.wait_recv()
+        self.out[2] = self.spread(2)
+        self.share(2, 0)
+
+    def step4(self):
+        self.far = []
+        for first_off in (0, -1, 1, 2):
+            up, down = self.out[first_off]
+            up.wait_recv()
+            self.far.append(self.put(self.block(first_off, -1, 0), self.dev(1, 1)))
+            down.wait_recv()
+            self.far.append(self.put(self.block(first_off, 1, 1), self.dev(1, -1)))
+            self.share(first_off, -1)
+            self.share(first_off, 1)
+
+    def step5(self):
+        for k, first_off in enumerate((0, -1, 1, 2)):
+            self.far[2 * k].wait_recv()
+            self.far[2 * k + 1].wait_recv()
+            self.share(first_off, 2)
+
+    def step6(self):
+        for copy in self.shared:
+            copy.wait_recv()
+
+
+def normalised(values):
+    centre = values - jnp.mean(values, axis=-1, keepdims=True)
+    spread = jnp.mean(centre * centre, axis=-1, keepdims=True)
+    scale = lax.rsqrt(spread + 1e-05)
+    return centre * scale, scale
+
+
+def first_kernel(
+    x_ref, cot_ref, shard_ref, small_ref,
+    n1_ref, q_ref, kv_ref, cotg_ref, w_ref, vec_ref, bqv_ref,
+    xg, vz, vall, send_sem, recv_sem,
+):
+    p = Place()
+    greet(
+        [p.at(dz=1), p.at(dz=-1), p.at(dz=2), p.at(dx=1), p.at(dx=-1), p.at(dx=2),
+         p.at(dy=1), p.at(dy=-1), p.at(dy=2), p.at(flip=True), p.linear(1), p.linear(-1)]
+    )
+    copies = Copies(send_sem, recv_sem)
+    w_ref[rows(p.dp * 32, 32), :] = shard_ref[...]
+    head = PlaneGather(copies, p, w_ref, 0, 768)
+    head.start()
+    small = []
+    vz[p.z] = small_ref[0:8]
+    for dz in (1, -1, 2):
+        small.append(copies.put(vz.at[p.z], vz.at[p.z], p.at(dz=dz)))
+    xg[rows(p.z * BLOCK, BLOCK), :] = x_ref[...]
+    ring = RingGather(copies, p, xg)
+    ring.start()
+    head.step1()
+    for copy in small:
+        copy.wait_recv()
+    vall[p.c, p.chip, 0:8] = vz[0] + vz[1] + vz[2] + vz[3]
+    vall[p.c, p.chip, 8:16] = small_ref[8:16]
+    mine = vall.at[p.c, p.chip]
+    small = [copies.put(mine, mine, p.at(dy=dy)) for dy in (1, -1, 2)]
+    ring.below()
+    ring.above()
+    head.step2()
+    tail = PlaneGather(copies, p, w_ref, 768, 2304)
+    tail.start()
+    for copy in small:
+        copy.wait_recv()
+    mine = vall.at[p.c, rows(p.x * 4, 4)]
+    small = [copies.put(mine, mine, p.at(dx=dx)) for dx in (1, -1, 2)]
+    head.step3()
+    cotg_ref[rows(p.z * BLOCK, BLOCK), :] = cot_ref[...]
+    cot_ring = RingGather(copies, p, cotg_ref)
+    cot_ring.start()
+    for copy in small:
+        copy.wait_recv()
+    mine = vall.at[p.c]
+    last = copies.put(mine, mine, p.at(flip=True))
+    head.step4()
+    tail.step1()
+    ring.far()
+    last.wait_recv()
+    lanes = []
+    for k in range(8):
+        total = vall[0, 2 * k] + vall[0, 2 * k + 1] + vall[1, 2 * k] + vall[1, 2 * k + 1]
+        vec_ref[:, k * 128:(k + 1) * 128] = total
+        lanes.append(total)
+    for h in range(2):
+        bqv_ref[:, h * 128:(h + 1) * 128] = lanes[4 * h] + lanes[4 * h + 1] + lanes[4 * h + 2] + lanes[4 * h + 3]
+
+    def norm_block(k, carry):
+        block = rows(lax.rem(p.z + k, 4) * BLOCK, BLOCK)
+        hat, _ = normalised(xg[block, :].astype(F32))
+        n1_ref[block, :] = (hat * vec_ref[0:1, :] + vec_ref[2:3, :]).astype(BF)
+        return carry
+
+    lax.fori_loop(0, 4, norm_block, 0)
+    head.step5()
+    tail.step2()
+    head.step6()
+    tail.step3()
+    tail.step4()
+    halo = []
+    for k in range(4):
+        start = lax.rem(p.z + k, 4) * BLOCK
+        block = rows(start, BLOCK)
+        values = n1_ref[block, :]
+        q_ref[block, :] = (nn(values, w_ref[:, 0:256]) + bqv_ref[9:10, :]).astype(BF)
+        mine = rows(4 * GROUP + start, BLOCK)
+        kv_ref[mine, 0:256] = nn(values, w_ref[:, 256:512]).astype(BF)
+        kv_ref[mine, 256:512] = (nn(values, w_ref[:, 512:768]) + bqv_ref[10:11, :]).astype(BF)
+        halo.append(
+            copies.put(kv_ref.at[mine], kv_ref.at[rows(2 * GROUP + start, BLOCK)], p.linear(1))
+        )
+    tail.step5()
+    cot_ring.below()
+    cot_ring.above()
+    relay, cross = [], []
+    sibling = p.at(flip=True)
+    for k in range(4):
+        start = lax.rem(p.z + k, 4) * BLOCK
+        halo[k].wait_recv()
+        near = kv_ref.at[rows(2 * GROUP + start, BLOCK)]
+        relay.append(copies.put(near, kv_ref.at[rows(start, BLOCK)], p.linear(1)))
+        cross.append(
+            copies.put(near, kv_ref.at[rows((1 + 2 * p.c) * GROUP + start, BLOCK)], sibling)
+        )
+    cot_ring.far()
+    for k in range(4):
+        start = lax.rem(p.z + k, 4) * BLOCK
+        relay[k].wait_recv()
+        cross.append(
+            copies.put(
+                kv_ref.at[rows((4 - 4 * p.c) * GROUP + start, BLOCK)],
+                kv_ref.at[rows((3 - 2 * p.c) * GROUP + start, BLOCK)],
+                sibling,
+            )
+        )
+    for copy in cross:
+        copy.wait_recv()
+    tail.step6()
+    copies.finish()
+
+
+N1_COPIES = 2 * 36 + 4 + 4 + 3 + 3 + 3 + 1 + 16
+
+
+def vm(count):
+    return [pl.BlockSpec(memory_space=pltpu.VMEM)] * count
+
+
+def call_first(x, cot, shard, small):
+    return pl.pallas_call(
+        first_kernel,
+        out_shape=(
+            jax.ShapeDtypeStruct((GROUP, D), BF),
+            jax.ShapeDtypeStruct((GROUP, 256), BF),
+            jax.ShapeDtypeStruct((5 * GROUP, 512), BF),
+            jax.ShapeDtypeStruct((GROUP, D), BF),
+            jax.ShapeDtypeStruct((D, 3072), BF),
+            jax.ShapeDtypeStruct((16, D), F32),
+            jax.ShapeDtypeStruct((16, 256), F32),
+        ),
+        in_specs=vm(4),
+        out_specs=tuple(vm(7)),
+        scratch_shapes=[
+            pltpu.VMEM((GROUP, D), BF),
+            pltpu.VMEM((4, 8, 128), F32),
+            pltpu.VMEM((2, 16, 16, 128), F32),
+            pltpu.SemaphoreType.DMA((N1_COPIES,)),
+            pltpu.SemaphoreType.DMA((N1_COPIES,)),
+        ],
+        compiler_params=pltpu.CompilerParams(
+            collective_id=1, has_side_effects=True, vmem_limit_bytes=VMEM_LIMIT
+        ),
+        name="gather_and_project",
+    )(x, cot, shard, small)
+
+
+def pack_small(gains, shifts, b_qv, b_fc):
+    dp, z = lax.axis_index("dp"), lax.axis_index("tensor")
+    lane = jnp.arange(128, dtype=jnp.int32)[None, :]
+    eight = jnp.concatenate([gains, shifts, jnp.zeros((2, 8), F32)], axis=0)
+    top = jnp.where(lane // 8 == lax.rem(dp * 4 + z, 16), jnp.tile(eight, (1, 16)), 0.0)
+    fc = jnp.where(lane // 32 == lax.rem(dp, 4), jnp.tile(b_fc[None].astype(F32), (1, 4)), 0.0)
+    qv = jnp.where(lane // 8 == lax.rem(dp, 16), jnp.tile(b_qv.astype(F32), (1, 16)), 0.0)
+    return jnp.concatenate([top, fc, qv, jnp.zeros((5, 128), F32)], axis=0)
+
+
+def pack_weights(w_qkv, w_out, w_fc, w_proj):
+    return jnp.concatenate(
+        [w_qkv[0].reshape(32, 768), w_out[0].T, w_fc[0], w_proj[0].T], axis=1
+    )
+
+
 SPAN = 4
 
 
@@ -146,48 +510,27 @@
 
 
 def on_device(inputs, lengths, w_qkv, w_out, w_fc, w_proj, b_qv, b_fc, gains, shifts, cotangent):
-    levels = w_qkv.shape[0]
-    all_gains, all_shifts = (
-        lax.all_gather(gains, ("dp", "tensor"), axis=2, tiled=True),
-        lax.all_gather(shifts, ("dp", "tensor"), axis=2, tiled=True),
-    )
+    n1, q, kv, cotg, wall, vec, bqv = call_first(
+        inputs, cotangent, pack_weights(w_qkv, w_out, w_fc, w_proj),
+        pack_small(gains[0], shifts[0], b_qv[0], b_fc[0])
+    )
+    all_gains, all_shifts = vec[None, 0:2], vec[None, 2:6]
     group_index = lax.axis_index("dp")
-    rows_dev = inputs.shape[0]
-    tok_group = rows_dev * lax.axis_size("tensor")
+    tok_group = 512
     query_pos = group_index * tok_group + jnp.arange(tok_group, dtype=jnp.int32)
     key_pos = (group_index - SPAN) * tok_group + jnp.arange((SPAN + 1) * tok_group, dtype=jnp.int32)
     same_seq = sequence_of(lengths, query_pos)[:, None] == sequence_of(lengths, key_pos)[None, :]
     allowed = same_seq & (key_pos[None, :] <= query_pos[:, None])
     residual = inputs.astype(jnp.float32)
-    layer_index = 0
-    fetched = (
-        lax.all_gather(w_qkv[layer_index], "dp", axis=0, tiled=True),
-        lax.all_gather(w_out[layer_index], "dp", axis=1, tiled=True),
-        lax.all_gather(w_fc[layer_index], "dp", axis=0, tiled=True),
-        lax.all_gather(w_proj[layer_index], "dp", axis=1, tiled=True),
-        lax.all_gather(b_qv[layer_index], "dp", axis=1, tiled=True),
-        lax.all_gather(b_fc[layer_index], "dp", axis=0, tiled=True),
-    )
-    weight_qkv, weight_out, weight_fc, weight_proj, bias_qv, bias_fc = fetched
-    layer_gains = all_gains[layer_index]
-    layer_shifts = all_shifts[layer_index]
-    gathered_one = gather_rows(layer_norm(residual, layer_gains[0], layer_shifts[0]))
-    width_local = weight_qkv.shape[2]
-    mixed = jnp.dot(
-        gathered_one,
-        weight_qkv.reshape(weight_qkv.shape[0], -1),
-        preferred_element_type=jnp.float32,
-    ).reshape(tok_group, 3, width_local)
-    bias_low = bias_qv.astype(jnp.float32)
-    bias_full = jnp.stack([bias_low[0], jnp.zeros_like(bias_low[0]), bias_low[1]])
-    qkv_low = (mixed + bias_full).astype(jnp.bfloat16)
-    own_pair = qkv_low[:, 1:]
-    earlier = []
-    passing = own_pair
-    for hop_index in range(SPAN):
-        passing = from_behind(passing, "dp", 1)
-        earlier.append(passing)
-    key_set = jnp.concatenate(earlier[::-1] + [own_pair], axis=0)
+    levels = 1
+    weight_qkv, weight_out, weight_fc, weight_proj = (
+        wall[:, :768].reshape(1024, 3, 256), wall[:, 768:1024].T, wall[:, 1024:2048], wall[:, 2048:].T)
+    bias_fc = vec[8]
+    fetched = None
+    layer_gains, layer_shifts = all_gains[0], all_shifts[0]
+    gathered_one = n1
+    key_set = kv.reshape(2560, 2, 256)
+    qkv_low = jnp.concatenate([q[:, None], key_set[2048:]], axis=1)
     context_low, log_total = attend_forward(qkv_low, key_set, allowed)
     after = residual + tensor_sum(context_low, weight_out) + layer_shifts[2]
     gathered_two = gather_rows(layer_norm(after, layer_gains[1], layer_shifts[1]))
@@ -196,43 +539,14 @@
     )
     act_low = gelu_tanh(pre_act).astype(jnp.bfloat16)
     output_rows = after + tensor_sum(act_low, weight_proj) + layer_shifts[3]
-    stored = [
-        (
-            residual,
-            gathered_one,
-            qkv_low,
-            key_set,
-            log_total,
-            context_low,
-            after,
-            gathered_two,
-            pre_act,
-            act_low,
-            fetched,
-        )
-    ]
     grad_res = cotangent.astype(jnp.float32)
     reduced = [None] * levels
     gain_parts = [None] * levels
     shift_parts = [None] * levels
     layer_index = 0
-    (
-        layer_input,
-        gathered_one,
-        qkv_low,
-        key_set,
-        log_total,
-        context_low,
-        after,
-        gathered_two,
-        pre_act,
-        act_low,
-        fetched,
-    ) = stored[layer_index]
-    weight_qkv, weight_out, weight_fc, weight_proj, bias_qv, bias_fc = fetched
-    layer_gains = all_gains[layer_index]
-    layer_shifts = all_shifts[layer_index]
-    grad_mlp = gather_grads(grad_res)
+    layer_index = 0
+    layer_input = residual
+    grad_mlp = cotg
     grad_weight_proj = contract_rows(act_low, grad_mlp)
     grad_act = contract_cols(grad_mlp, weight_proj)
     gelu_value, gelu_pull = jax.vjp(gelu_tanh, pre_act)

time: 1050 us -> 794 us (0.76)
  blocking collectives: 367 us -> 140 us
  Pallas kernels: 0 us -> 71.1 us
  waiting for transfers between devices: 447 us -> 385 us
  local copies, waits for them, and re-layouts: 58 us -> 33.6 us
  starting transfers between devices: 24.7 us -> 6.35 us
    all_gather x4 -> x0, blocking collectives: 160 us -> none  [the longest x1 54.9 us: on_device(): lax.all_gather(gains, ('dp', 'tensor'), axis=2, tiled=True)]
    pallas_call x0 -> x1, Pallas kernels: none -> 71.1 us  [call_first(): pl.pallas_call(first_kernel, out_shape=(jax.ShapeDtypeStruct((GROUP, D),...]
    unnamed x3 -> x2, blocking collectives: 207 us -> 140 us
    reduce_scatter x1, waiting for transfers between devices: 0.01 us -> 52.6 us  [on_device(): lax.psum_scatter(grad_weight_proj, 'dp', scatter_dimension=1, tiled=True)]
    reduce_scatter x1, waiting for transfers between devices: 51.1 us -> 0.01 us  [on_device(): lax.psum_scatter(grad_weight_fc, 'dp', scatter_dimension=0, tiled=True)]
    all_gather x3 -> x0, waiting for transfers between devices: 46.6 us -> none  [the longest x1 46.6 us: on_device(): lax.all_gather(w_proj[layer_index], 'dp', axis=1, tiled=True)]
    slice x5 -> x2, local copies, waits for them, and re-layouts: 31.6 us -> 5.7 us  [the longest x1 4.74 us: split_heads(): value_rows = key_set[:, 1].reshape(key_set.shape[0], heads_local, HEAD_DIM)]
    all_gather x2 -> x1, waiting for transfers between devices: 0.04 us -> 23.9 us  [gather_rows(): lax.all_gather(normed.astype(jnp.bfloat16), 'tensor', axis=0, tiled=True)]
  transfers between devices with their start and end apart: 23 -> 14, of which waited for: 16 -> 12; matrix products, arithmetic and copies ran while one was open for 8% -> 5% of each run, Pallas kernels for 0% -> 0%
where the time goes in v1:
time: 794 us; the launch traced here: 784 us
  waiting for transfers between devices  385 us (48%)
  blocking collectives  140 us (18%)
  matrix products  89.5 us (11%)
  Pallas kernels  71.1 us (9%)
  other arithmetic  41.9 us (5%)
  local copies, waits for them, and re-layouts  33.6 us (4%)
  between operations  16.3 us (2%)
    unnamed x2, blocking collectives  140 us
    reduce_scatter x1, waiting for transfers between devices, on_device(): lax.psum_scatter(grad_weight_qkv, 'dp', scatter_dimension=0, tiled=True)  84.2 us
    reduce_scatter x1, waiting for transfers between devices, on_device(): lax.psum_scatter(grad_weight_out, 'dp', scatter_dimension=1, tiled=True)  80.9 us
    pallas_call x1, Pallas kernels, call_first(): pl.pallas_call(first_kernel, out_shape=(jax.ShapeDtypeStruct((GROUP, D),...  71.1 us
    reduce_scatter x2, waiting for transfers between devices, tensor_sum(): lax.psum_scatter(partial_value(jnp.int32(0), row_count * lax.axis_size('t...  55.8 us
    reduce_scatter x1, waiting for transfers between devices, on_device(): lax.psum_scatter(grad_weight_proj, 'dp', scatter_dimension=1, tiled=True)  52.6 us
    ppermute x4, waiting for transfers between devices, from_behind(): lax.ppermute(value, axis, [(source, source + steps) for source in range(f...  39.8 us
    reduce_scatter x2, waiting for transfers between devices, tensor_back(): lax.psum_scatter(partial_value(jnp.int32(0), row_count * lax.axis_size('t...  24.4 us
  transfers between devices with their start and end apart: 14, of which 12 were waited for; matrix products, arithmetic and copies ran while one was open for 5% of the time, Pallas kernels for 0%

profile of v1, /device:TPU:0, one launch (start us, length us, event | category | flops | bytes accessed | tf_op | source)
XLA Modules:
  0.0 784.0 jit_solution(14572535131418815688)
XLA Ops:
  7.3 0.7 bitcast_convert_fusion.1
  8.9 0.7 copy.42
  10.1 0.8 maximum_maximum_fusion.1
  11.0 0.8 copy.40
  11.9 0.7 maximum_maximum_fusion.small_ref
  12.5 1.6 pad_maximum_fusion.1.shard_ref
  14.1 71.1 %gather_and_project.1 = (bf16[512,1024]{1,0:T(8,128)(2,1)}, bf16[512,256]{1,0:T(8,128)(2,1)}, bf16[2560,512]{1,0:T(8,128)(2,1)}, bf16[512,1024]{1,0:T(8,128)(2,1...) custom-call(bf16[128,1024]{1,0:T(8,128)(2,1)} %x_ref.1, bf16[128,1024]{1,0:T(8,128)(2,1)} %cot_ref.1, ...), custom_call_target="tpu_custom_call" | custom-call | tf_op jit(solution)/shard_map/gather_and_project/pallas_call | solution.py:329
  85.2 3.6 reshape.361
  88.8 0.8 copy.43
  89.6 5.2 fusion.59
  94.8 6.3 copy.44
  101.1 4.7 copy.41
  105.9 1.2 compare_and_fusion
  107.0 5.5 fusion.61
  112.6 5.1 fusion
  117.6 1.9 copy-done
  119.5 6.2 fusion.24
  125.7 3.0 fusion.46
  129.0 1.0 fusion.60
  129.9 25.3 %reduce-scatter.12.cloned.1.call-done = f32[128,1024]{1,0:T(8,128)} async-done(((f32[512,1024]{1,0:T(8,128)}), f32[128,1024]{1,0:T(8,128)}) %reduce-scatter.12.cloned.1.call-update) | async-done | bytes 524304 | tf_op jit(solution)/shard_map/reduce_scatter | solution.py:427
  155.3 1.2 fusion.57
  156.7 0.9 add_convert_fusion
  157.6 23.9 %all-gather.3.cloned.1.call-done = bf16[512,1024]{1,0:T(8,128)(2,1)} async-done(((bf16[128,1024]{1,0:T(8,128)(2,1)}), bf16[512,1024]{1,0:T(8,128)(2,1)}) %all-gather.3.cloned.1.call-update) | async-done | bytes 1048592 | tf_op jit(solution)/shard_map/all_gather | solution.py:414
  181.5 3.2 fusion.18
  184.7 5.2 convert_reduce_fusion
  189.9 1.0 copy-done.9
  190.9 4.2 fusion.16
  195.1 1.5 copy-done.14
  196.7 4.4 fusion.14
  201.2 24.4 %reduce-scatter.16.cloned.1.call-done = f32[128,1024]{1,0:T(8,128)} async-done(((f32[512,1024]{1,0:T(8,128)}), f32[128,1024]{1,0:T(8,128)}) %reduce-scatter.16.cloned.1.call-update) | async-done | bytes 524304 | tf_op jit(solution)/shard_map/reduce_scatter | solution.py:441
  225.5 1.3 multiply_reduce_fusion.1
  226.9 30.5 %reduce-scatter.14.cloned.1.call-done = f32[128,1024]{1,0:T(8,128)} async-done(((f32[512,1024]{1,0:T(8,128)}), f32[128,1024]{1,0:T(8,128)}) %reduce-scatter.14.cloned.1.call-update) | async-done | bytes 524304 | tf_op jit(solution)/shard_map/reduce_scatter | solution.py:427
  257.3 2.2 fusion.56
  259.5 0.8 fusion.50
  260.7 23.6 %all-gather.5.cloned.1.call-done = bf16[512,1024]{1,0:T(8,128)(2,1)} async-done(((bf16[128,1024]{1,0:T(8,128)(2,1)}), bf16[512,1024]{1,0:T(8,128)(2,1)}) %all-gather.5.cloned.1.call-update) | async-done | bytes 1048592 | tf_op jit(solution)/shard_map/all_gather | solution.py:418
  284.3 1.8 convolution_convert_fusion
  286.1 8.9 %fusion.2 = f32[4,64,2560]{2,1,0:T(8,128)S(1)} fusion(bf16[512,4,64]{0,2,1:T(8,128)(2,1)S(1)} %bitcast.116, f32[4,512,2560]{2,1,0:T(8,128)} %copy-done, f32[4,512]{1,0:T(4,128)S(1)} %log_add_fusion), kind=kOutput, calls=%fused_computation.8 | convolution fusion | flops 681574400 | bytes 23863296 | tf_op jit(solution)/shard_map/hqk,qhd->khd/dot_general | solution.py:499
  295.0 13.1 %multiply_reduce_fusion = (f32[4,512]{1,0:T(4,128)S(1)}, f32[4,512,2560]{2,1,0:T(8,128)}) fusion(f32[4,512,2560]{2,1,0:T(8,128)} %copy-done, f32[4,512]{1,0:T(4,128)S(1)} %log_add_fusion, bf16[512,4,64]{0,2,1:T(8,128)(2,1)S(1)} %bitcast.117, bf16[2560,4,64]{0,2,1:T(8,128)(2,1)S(1)} %bitcast.112), kind=kOutput, calls=%fused_computation.1 | convolution fusion | flops 686815232 | bytes 43532288 | tf_op jit(solution)/shard_map/qhd,khd->hqk/dot_general | solution.py:486
  308.2 18.1 %multiply_convert_fusion = bf16[4,512,2560]{2,1,0:T(8,128)(2,1)} fusion(f32[4,512,2560]{2,1,0:T(8,128)} %get-tuple-element.60, f32[4,512,2560]{2,1,0:T(8,128)} %copy-done, f32[4,512]{1,0:T(4,128)S(1)} %get-tuple-element.59, f32[4,512]{1,0:T(4,128)S(1)} %log_add_fusion), kind=kLoop, calls=%fused_computation | loop fusion | flops 20971520 | bytes 52445184 | tf_op jit(solution)/shard_map/convert_element_type | solution.py:490
  326.3 5.9 convolution_multiply_fusion
  332.3 1.3 collective-permute-start
  333.6 3.3 collective-permute-done
  337.1 1.3 collective-permute-start.1
  338.4 14.2 %collective-permute-done.1 = f32[512,2,256]{0,2,1:T(8,128)S(1)} collective-permute-done((f32[512,2,256]{0,2,1:T(8,128)S(1)}, f32[512,2,256]{0,2,1:T(8,128)S(1)}, u32[]{:S(2)}, u32[]{:S(2)}) %collective-permute-start.1) | collective-permute-done | bytes 1048608 | tf_op jit(solution)/shard_map/ppermute | solution.py:378
  352.8 1.4 collective-permute-start.2
  354.2 14.8 %collective-permute-done.2 = f32[512,2,256]{0,2,1:T(8,128)S(1)} collective-permute-done((f32[512,2,256]{0,2,1:T(8,128)S(1)}, f32[512,2,256]{0,2,1:T(8,128)S(1)}, u32[]{:S(2)}, u32[]{:S(2)}) %collective-permute-start.2) | collective-permute-done | bytes 1048608 | tf_op jit(solution)/shard_map/ppermute | solution.py:378
  369.3 1.3 collective-permute-start.3
  370.6 7.2 convolution_multiply_fusion.1
  377.8 7.6 collective-permute-done.3
  385.8 0.9 copy-done.5
  386.7 3.9 fusion.20
  390.6 4.8 fusion.63
  395.7 5.3 fusion.53
  401.1 0.9 copy-done.8
  401.9 2.8 fusion.62
  404.8 4.2 fusion.33
  411.7 75.7 %all-reduce.5 = (f32[2,256]{1,0:T(2,128)S(1)}, f32[1024]{0:T(1024)S(1)}) all-reduce(f32[2,256]{1,0:T(2,128)S(1)} %pad_maximum_fusion.2, f32[1024]{0:T(1024)S(1)} %get-tuple-element.61), channel_id=10, replica_groups=mesh['dp'=32,'tensor'=4] {'dp'}, use_global_device_ids=true, to_apply=%region_24.25.clone | all-reduce | flops 1536 | bytes 12288
  488.7 1.3 fusion.54
  490.0 1.4 fusion.43
  491.5 64.2 %all-reduce.4 = (f32[1,2,1024]{2,1,0:T(2,128)S(1)}, f32[1,4,1024]{2,1,0:T(4,128)S(1)}) all-reduce(f32[1,2,1024]{2,1,0:T(2,128)S(1)} %maximum_bitcast_fusion.1, f32[1,4,1024]{2,1,0:T(4,128)S(1)} %maximum_bitcast_fusion), channel_id=12, replica_groups=mesh['dp'=32,'tensor'=4] {'dp','tensor'}, use_global_device_ids=true, to_apply=%region_29.30.clone | all-reduce | flops 6144 | bytes 49152
  557.0 2.1 add_add_fusion.2
  559.1 52.6 %reduce-scatter.26.cloned.1.call-done = f32[1024,32]{0,1:T(8,128)} async-done(((f32[1024,1024]{0,1:T(8,128)}), f32[1024,32]{0,1:T(8,128)}) %reduce-scatter.26.cloned.1.call-update) | async-done | bytes 131088 | tf_op jit(solution)/shard_map/reduce_scatter | solution.py:587
  611.7 80.9 %reduce-scatter.22.cloned.1.call-done = f32[256,32]{0,1:T(8,128)} async-done(((f32[256,1024]{0,1:T(8,128)}), f32[256,32]{0,1:T(8,128)}) %reduce-scatter.22.cloned.1.call-update) | async-done | bytes 32784 | tf_op jit(solution)/shard_map/reduce_scatter | solution.py:585
  692.5 84.2 %reduce-scatter.20.cloned.1.call-done = f32[32,3,256]{2,0,1:T(8,128)} async-done(((f32[1024,3,256]{2,0,1:T(8,128)}), f32[32,3,256]{2,0,1:T(8,128)}) %reduce-scatter.20.cloned.1.call-update) | async-done | bytes 98320 | tf_op jit(solution)/shard_map/reduce_scatter | solution.py:584
  (96 shorter events, 8.1 us)
Async XLA Ops:
  7.2 148.1 %reduce-scatter.12.cloned.1.call-start = ((), (), s32[]{:S(2)}) async-start(), calls=%async_computation.8 | async-start | bytes 2621440 | tf_op jit(solution)/shard_map/reduce_scatter | solution.py:427
  85.2 3.6 copy-start.10
  94.8 6.3 copy-start.2
  112.5 7.0 copy-start
  125.7 29.5 %copy-start.4 = (bf16[128,1024]{1,0:T(8,128)(2,1)S(1)}, bf16[128,1024]{1,0:T(8,128)(2,1)}, u32[]{:S(2)}) copy-start(bf16[128,1024]{1,0:T(8,128)(2,1)} %x_ref.1) | copy-start | bytes 786436
  128.7 52.8 %all-gather.3.cloned.1.call-start = ((), (), s32[]{:S(2)}) async-start(), calls=%async_computation.9 | async-start | bytes 1310720 | tf_op jit(solution)/shard_map/all_gather | solution.py:414
  157.6 27.1 %copy-start.11 = (bf16[512,1024]{1,0:T(8,128)(2,1)S(1)}, bf16[512,1024]{1,0:T(8,128)(2,1)}, u32[]{:S(2)}) copy-start(bf16[512,1024]{1,0:T(8,128)(2,1)} %get-tuple-element.20) | copy-start | bytes 3145732
  157.6 67.9 %reduce-scatter.16.cloned.1.call-start = ((), (), s32[]{:S(2)}) async-start(), calls=%async_computation.11 | async-start | bytes 2621440 | tf_op jit(solution)/shard_map/reduce_scatter | solution.py:441
  184.7 5.2 copy-start.13
  189.9 1.0 copy-start.9
  195.1 1.6 copy-start.14
  195.1 62.2 %reduce-scatter.14.cloned.1.call-start = ((), (), s32[]{:S(2)}) async-start(), calls=%async_computation.10 | async-start | bytes 2621440 | tf_op jit(solution)/shard_map/reduce_scatter | solution.py:427
  201.1 58.4 %copy-start.7 = (bf16[128,1024]{1,0:T(8,128)(2,1)S(1)}, bf16[128,1024]{1,0:T(8,128)(2,1)}, u32[]{:S(2)}) copy-start(bf16[128,1024]{1,0:T(8,128)(2,1)} %cot_ref.1) | copy-start | bytes 786436
  201.1 83.2 %all-gather.5.cloned.1.call-start = ((), (), s32[]{:S(2)}) async-start(), calls=%async_computation.12 | async-start | bytes 1310720 | tf_op jit(solution)/shard_map/all_gather | solution.py:418
  260.4 228.3 %reduce-scatter.18.cloned.1.call-start = ((), (), s32[]{:S(2)}) async-start(), calls=%async_computation.13 | async-start | bytes 2621440 | tf_op jit(solution)/shard_map/reduce_scatter | solution.py:441
  286.1 8.9 %copy-start.3 = (bf16[2560,1,256]{0,2,1:T(8,128)(2,1)S(1)}, bf16[2560,1,256]{0,2,1:T(8,128)(2,1)}, u32[]{:S(2)}) copy-start(bf16[2560,1,256]{0,2,1:T(8,128)(2,1)} %copy.41) | copy-start | bytes 3932164
  308.2 18.1 %copy-start.6 = (bf16[512,256]{0,1:T(8,128)(2,1)S(1)}, bf16[512,256]{0,1:T(8,128)(2,1)}, u32[]{:S(2)}) copy-start(bf16[512,256]{0,1:T(8,128)(2,1)} %copy.43) | copy-start | bytes 786436
  332.3 4.6 collective-permute-start
  337.1 15.5 %collective-permute-start.1 = (f32[512,2,256]{0,2,1:T(8,128)S(1)}, f32[512,2,256]{0,2,1:T(8,128)S(1)}, u32[]{:S(2)}, u32[]{:S(2)}) collective-permute-start(f32[512,2,256]{0,2,1:T(8,128)S(1)} %fusion.31), channel_id=1, source_target_pairs={{4,0},{8,4},{12,8},{16,12},{20,16},{24,20},{28,24},{32,28},{36,32}... | collective-permute-start | bytes 3145736 | tf_op jit(solution)/shard_map/ppermute | solution.py:378
  352.8 17.8 %copy-start.1 = (bf16[2560,1,256]{0,2,1:T(8,128)(2,1)S(1)}, bf16[2560,1,256]{0,2,1:T(8,128)(2,1)}, u32[]{:S(2)}) copy-start(bf16[2560,1,256]{0,2,1:T(8,128)(2,1)} %copy.44) | copy-start | bytes 3932164
  352.8 16.2 %collective-permute-start.2 = (f32[512,2,256]{0,2,1:T(8,128)S(1)}, f32[512,2,256]{0,2,1:T(8,128)S(1)}, u32[]{:S(2)}, u32[]{:S(2)}) collective-permute-start(f32[512,2,256]{0,2,1:T(8,128)S(1)} %fusion.26), channel_id=1, source_target_pairs={{4,0},{8,4},{12,8},{16,12},{20,16},{24,20},{28,24},{32,28},{36,32}... | collective-permute-start | bytes 3145736 | tf_op jit(solution)/shard_map/ppermute | solution.py:378
  369.3 16.1 %collective-permute-start.3 = (f32[512,2,256]{0,2,1:T(8,128)S(1)}, f32[512,2,256]{0,2,1:T(8,128)S(1)}, u32[]{:S(2)}, u32[]{:S(2)}) collective-permute-start(f32[512,2,256]{0,2,1:T(8,128)S(1)} %fusion.32), channel_id=1, source_target_pairs={{4,0},{8,4},{12,8},{16,12},{20,16},{24,20},{28,24},{32,28},{36,32}... | collective-permute-start | bytes 3145736 | tf_op jit(solution)/shard_map/ppermute | solution.py:378
  385.8 0.9 copy-start.5
  390.6 168.5 %reduce-scatter.24.cloned.1.call-start = ((), (), s32[]{:S(2)}) async-start(), calls=%async_computation.16 | async-start | bytes 4325376 | tf_op jit(solution)/shard_map/reduce_scatter | solution.py:586
  395.4 216.3 %reduce-scatter.26.cloned.1.call-start = ((), (), s32[]{:S(2)}) async-start(), calls=%async_computation.17 | async-start | bytes 4325376 | tf_op jit(solution)/shard_map/reduce_scatter | solution.py:587
  401.0 0.9 copy-start.8
  401.0 291.5 %reduce-scatter.22.cloned.1.call-start = ((), (), s32[]{:S(2)}) async-start(), calls=%async_computation.15 | async-start | bytes 1081344 | tf_op jit(solution)/shard_map/reduce_scatter | solution.py:585
  404.7 372.0 %reduce-scatter.20.cloned.1.call-start = ((), (), s32[]{:S(2)}) async-start(), calls=%async_computation.14 | async-start | bytes 3244032 | tf_op jit(solution)/shard_map/reduce_scatter | solution.py:584
  409.0 0.7 copy-start.12
Sparse Core Ops, SparseCore 0:
  128.9 26.3 reduce-scatter.11
  157.7 23.7 all-gather.2
  195.2 30.2 reduce-scatter.15
  227.8 29.4 reduce-scatter.13
  260.5 23.7 all-gather.4
  390.7 49.0 reduce-scatter.17
  444.0 81.6 reduce-scatter.23
  530.4 81.2 reduce-scatter.25
  615.8 76.7 reduce-scatter.21
  697.0 79.6 reduce-scatter.19

commit v2 on v1

--- a/solution.py
+++ b/solution.py
@@ -55,7 +55,7 @@
 class Copies:
     def __init__(self, send_sem, recv_sem):
         self.send_sem, self.recv_sem = send_sem, recv_sem
-        self.started = []
+        self.started, self.settled = [], []
 
     def put(self, src, dst, device):
         k = len(self.started)
@@ -71,9 +71,15 @@
         self.started.append(copy)
         return copy
 
+    def settle(self, *copies):
+        for copy in copies:
+            copy.wait_send()
+            self.settled.append(copy)
+
     def finish(self):
         for copy in self.started:
-            copy.wait_send()
+            if not any(copy is other for other in self.settled):
+                copy.wait_send()
 
 
 def greet(devices):
@@ -369,250 +375,735 @@
     )
 
 
-SPAN = 4
-
-
-def from_behind(value, axis, steps):
-    count = lax.axis_size(axis)
-    first, last = (max(0, -steps), min(count, count - steps))
-    return lax.ppermute(value, axis, [(source, source + steps) for source in range(first, last)])
-
-
-def layer_norm(values, gain_row, shift_row):
-    centre = values - jnp.mean(values, axis=-1, keepdims=True)
-    spread = jnp.mean(centre * centre, axis=-1, keepdims=True)
-    return centre * lax.rsqrt(spread + 1e-05) * gain_row + shift_row
-
-
-def gelu_tanh(values):
+def heads_down(tile):
+    head = lax.broadcasted_iota(jnp.int32, tile.shape, 0) // HEAD_DIM
+    return jnp.concatenate([jnp.where(head == h, tile, 0.0) for h in range(4)], axis=1)
+
+
+def heads_across(tile):
+    head = lax.broadcasted_iota(jnp.int32, tile.shape, 1) // HEAD_DIM
+    return jnp.concatenate([jnp.where(head == h, tile, 0.0) for h in range(4)], axis=0)
+
+
+def causal(scores):
+    key = lax.broadcasted_iota(jnp.int32, scores.shape, 0)
+    query = lax.rem(lax.broadcasted_iota(jnp.int32, scores.shape, 1), BLOCK)
+    return jnp.where(key <= query, scores, -1e30)
+
+
+def attend_kernel(first_ref, q_ref, kv_ref, ctx_ref, lse_ref, vt, scores, acc):
+    def turn(j, carry):
+        block = rows(j * BLOCK, BLOCK)
+        vt[j] = kv_ref[block, 256:512].astype(F32).T.astype(BF)
+        return carry
+
+    lax.fori_loop(first_ref[0], 20, turn, 0)
+
+    def query_block(b, carry):
+        first, last = first_ref[b], 16 + b
+        queries = (q_ref[rows(b * BLOCK, BLOCK), :].astype(F32) * 0.125).T
+        wide = heads_down(queries).astype(BF)
+
+        def score(j, top):
+            tile = nn(kv_ref[rows(j * BLOCK, BLOCK), 0:256], wide)
+            scores[j - first] = tile
+            return jnp.maximum(top, jnp.max(tile.reshape(16, 8, 512), axis=0))
+
+        top = lax.fori_loop(first, last, score, jnp.full((8, 512), -1e30, F32))
+        tile = causal(nn(kv_ref[rows(last * BLOCK, BLOCK), 0:256], wide))
+        scores[last - first] = tile
+        top = jnp.maximum(top, jnp.max(tile.reshape(16, 8, 512), axis=0))
+        top = jnp.max(top, axis=0, keepdims=True)
+        acc[...] = jnp.zeros_like(acc)
+
+        def weigh(j, total):
+            weights = jnp.exp(scores[j - first] - top)
+            low = weights.astype(BF)
+            for h in range(4):
+                part = slice(h * HEAD_DIM, (h + 1) * HEAD_DIM)
+                acc[part, :] += nn(vt[j, part, :], low[:, h * BLOCK:(h + 1) * BLOCK])
+            return total + jnp.sum(weights.reshape(16, 8, 512), axis=0)
+
+        total = lax.fori_loop(first, last + 1, weigh, jnp.zeros((8, 512), F32))
+        total = jnp.sum(total, axis=0, keepdims=True)
+        lse_ref[pl.ds(b, 1), :] = top + jnp.log(total)
+        inverse = 1.0 / total
+        context = jnp.concatenate(
+            [acc[h * HEAD_DIM:(h + 1) * HEAD_DIM, :] * inverse[:, h * BLOCK:(h + 1) * BLOCK] for h in range(4)],
+            axis=0,
+        )
+        ctx_ref[rows(b * BLOCK, BLOCK), :] = context.T.astype(BF)
+        return carry
+
+    lax.fori_loop(0, 4, query_block, 0)
+
+
+def call_attend(first, q, kv):
+    return pl.pallas_call(
+        attend_kernel,
+        out_shape=(
+            jax.ShapeDtypeStruct((GROUP, 256), BF),
+            jax.ShapeDtypeStruct((8, 512), F32),
+        ),
+        in_specs=[pl.BlockSpec(memory_space=pltpu.SMEM)] + vm(2),
+        out_specs=tuple(vm(2)),
+        scratch_shapes=[
+            pltpu.VMEM((20, 256, BLOCK), BF),
+            pltpu.VMEM((16, BLOCK, 512), F32),
+            pltpu.VMEM((256, BLOCK), F32),
+        ],
+        compiler_params=pltpu.CompilerParams(vmem_limit_bytes=VMEM_LIMIT),
+        name="attend",
+    )(first, q, kv)
+
+
+def attend_back_kernel(
+    first_ref, q_ref, kv_ref, ctx_ref, lse_ref, dctx_ref, dq_ref, dkv_ref, kt, dkv, acc
+):
+    def turn(j, carry):
+        block = rows(j * BLOCK, BLOCK)
+        kt[j] = kv_ref[block, 0:256].astype(F32).T.astype(BF)
+        return carry
+
+    lax.fori_loop(first_ref[0], 20, turn, 0)
+
+    def clear(j, carry):
+        dkv[rows(j * BLOCK, BLOCK), :] = jnp.zeros((BLOCK, 512), F32)
+        return carry
+
+    lax.fori_loop(0, 20, clear, 0)
+
+    def query_block(b, carry):
+        first, last = first_ref[b], 16 + b
+        block = rows(b * BLOCK, BLOCK)
+        queries = q_ref[block, :].astype(F32) * 0.125
+        grads = dctx_ref[block, :].astype(F32)
+        turned = grads.T
+        wide_q, tall_q = heads_down(queries.T).astype(BF), heads_across(queries).astype(BF)
+        wide_g, tall_g = heads_down(turned).astype(BF), heads_across(grads).astype(BF)
+        inner = turned * ctx_ref[block, :].astype(F32).T
+        inner = jnp.concatenate(
+            [jnp.sum(inner[h * HEAD_DIM:(h + 1) * HEAD_DIM], axis=0, keepdims=True) for h in range(4)],
+            axis=1,
+        )
+        lse = lse_ref[pl.ds(b, 1), :]
+        acc[...] = jnp.zeros_like(acc)
+
+        def step(j, mask):
+            keys = rows(j * BLOCK, BLOCK)
+            tile = nn(kv_ref[keys, 0:256], wide_q)
+            if mask:
+                tile = causal(tile)
+            weights = jnp.exp(tile - lse)
+            grad = nn(kv_ref[keys, 256:512], wide_g)
+            low = (weights * (grad - inner)).astype(BF)
+            dkv[keys, 0:256] += nn(low, tall_q)
+            dkv[keys, 256:512] += nn(weights.astype(BF), tall_g)
+            for h in range(4):
+                part = slice(h * HEAD_DIM, (h + 1) * HEAD_DIM)
+                acc[part, :] += nn(kt[j, part, :], low[:, h * BLOCK:(h + 1) * BLOCK])
+
+        def full(j, carry):
+            step(j, False)
+            return carry
+
+        lax.fori_loop(first, last, full, 0)
+        step(last, True)
+        dq_ref[block, :] = (acc[...].T * 0.125).astype(BF)
+        return carry
+
+    lax.fori_loop(0, 4, query_block, 0)
+
+    def store(j, carry):
+        block = rows(j * BLOCK, BLOCK)
+        dkv_ref[block, :] = dkv[block, :].astype(BF)
+        return carry
+
+    lax.fori_loop(0, 20, store, 0)
+
+
+def call_attend_back(first, q, kv, ctx, lse, dctx):
+    return pl.pallas_call(
+        attend_back_kernel,
+        out_shape=(
+            jax.ShapeDtypeStruct((GROUP, 256), BF),
+            jax.ShapeDtypeStruct((5 * GROUP, 512), BF),
+        ),
+        in_specs=[pl.BlockSpec(memory_space=pltpu.SMEM)] + vm(5),
+        out_specs=tuple(vm(2)),
+        scratch_shapes=[
+            pltpu.VMEM((20, 256, BLOCK), BF),
+            pltpu.VMEM((5 * GROUP, 512), F32),
+            pltpu.VMEM((256, BLOCK), F32),
+        ],
+        compiler_params=pltpu.CompilerParams(vmem_limit_bytes=VMEM_LIMIT),
+        name="attend_back",
+    )(first, q, kv, ctx, lse, dctx)
+
+
+def first_blocks(lengths):
+    base = lax.axis_index("dp") * 4
+    ends = jnp.cumsum(lengths)
+    block = base + jnp.arange(4, dtype=jnp.int32)
+    start = jnp.max(jnp.where(ends[None, :] <= block[:, None], ends[None, :], 0), axis=1)
+    return start - base + 16
+
+
+class PlaneScatter:
+    copies_needed = 18
+
+    def __init__(self, copies, place, g, scratch):
+        self.copies, self.place, self.g = copies, place, g
+        self.land, self.far, self.near, self.t, self.far2, self.near2, self.last, self.rest = scratch
+        self.half = g.shape[1] // 2
+
+    @staticmethod
+    def scratch(width):
+        half = width // 2
+        return [
+            pltpu.VMEM((1024, half), BF),
+            pltpu.VMEM((2, 2, 64, half), BF),
+            pltpu.VMEM((2, 4, 64, half), BF),
+            pltpu.VMEM((4, 64, half), BF),
+            pltpu.VMEM((2, 32, half), BF),
+            pltpu.VMEM((2, 64, half), BF),
+            pltpu.VMEM((32, half), F32),
+            pltpu.VMEM((32, half), F32),
+        ]
+
+    def dev(self, axis, step):
+        c = self.place.c
+        if axis == 0:
+            return self.place.at(dx=(1 - c) * step, dy=c * step)
+        return self.place.at(dx=c * step, dy=(1 - c) * step)
+
+    def first(self, step):
+        p = self.place
+        return lax.rem(p.x * (1 - p.c) + p.y * p.c + step + 4, 4)
+
+    def second(self, step):
+        p = self.place
+        return lax.rem(p.y * (1 - p.c) + p.x * p.c + step + 4, 4)
+
+    def block(self, f, s):
+        c = self.place.c
+        x, y = f * (1 - c) + s * c, s * (1 - c) + f * c
+        return rows((x * 4 + y) * 64, 64)
+
+    def start(self):
+        c = self.place.c
+        other = pl.ds(pl.multiple_of((1 - c) * self.half, 128), self.half)
+        self.swap = self.copies.put(self.g.at[:, other], self.land, self.place.at(flip=True))
+
+    def step1(self):
+        self.swap.wait_recv()
+        mine = pl.ds(pl.multiple_of(self.place.c * self.half, 128), self.half)
+        self.mine = mine
+
+        def join(k, carry):
+            f = self.first(2 + k // 4)
+            block = self.block(f, lax.rem(k, 4))
+            self.land[block, :] = (self.land[block, :].astype(F32) + self.g[block, mine].astype(F32)).astype(BF)
+            return carry
+
+        lax.fori_loop(0, 4, join, 0)
+        self.out = []
+        for s in range(4):
+            to = self.dev(0, 1 if s < 2 else -1)
+            self.out.append(
+                self.copies.put(self.land.at[self.block(self.first(2), s)], self.far.at[s // 2, s % 2], to)
+            )
+        lax.fori_loop(4, 16, join, 0)
+
+    def step2(self):
+        self.out2 = []
+        for side, step in ((0, 1), (1, -1)):
+            f = self.first(step)
+            for s in range(4):
+                block = self.block(f, s)
+                if s // 2 == side:
+                    self.out[s].wait_recv()
+                    self.land[block, :] = (
+                        self.land[block, :].astype(F32) + self.far[side, s % 2].astype(F32)
+                    ).astype(BF)
+                self.out2.append(
+                    self.copies.put(self.land.at[block], self.near.at[side, s], self.dev(0, step))
+                )
+
+    def step3(self):
+        f = self.first(0)
+        for copy in self.out2:
+            copy.wait_recv()
+
+        def total(k, carry):
+            s = self.second(2 + k)
+            self.t[s] = (
+                self.land[self.block(f, s), :].astype(F32)
+                + self.near[0, s].astype(F32)
+                + self.near[1, s].astype(F32)
+            ).astype(BF)
+            return carry
+
+        lax.fori_loop(0, 1, total, 0)
+        s = self.second(2)
+        self.up = self.copies.put(self.t.at[s, 0:32], self.far2.at[0], self.dev(1, 1))
+        self.down = self.copies.put(self.t.at[s, 32:64], self.far2.at[1], self.dev(1, -1))
+        lax.fori_loop(1, 4, total, 0)
+
+    def step4(self):
+        s = self.second(1)
+        self.up.wait_recv()
+        self.t[s, 0:32] = (self.t[s, 0:32].astype(F32) + self.far2[0].astype(F32)).astype(BF)
+        self.up2 = self.copies.put(self.t.at[s], self.near2.at[0], self.dev(1, 1))
+        s = self.second(-1)
+        self.down.wait_recv()
+        self.t[s, 32:64] = (self.t[s, 32:64].astype(F32) + self.far2[1].astype(F32)).astype(BF)
+        self.down2 = self.copies.put(self.t.at[s], self.near2.at[1], self.dev(1, -1))
+
+    def part(self, c):
+        half = rows(c * 32, 32)
+        return (
+            self.t[self.second(0), half].astype(F32)
+            + self.near2[0, half].astype(F32)
+            + self.near2[1, half].astype(F32)
+        )
+
+    def step5(self):
+        self.up2.wait_recv()
+        self.down2.wait_recv()
+        c = self.place.c
+        self.last[...] = self.part(1 - c)
+        self.back = self.copies.put(self.last, self.rest, self.place.at(flip=True))
+
+    def step6(self, out):
+        out[:, self.mine] = self.part(self.place.c)
+        self.back.wait_recv()
+        other = pl.ds(pl.multiple_of((1 - self.place.c) * self.half, 128), self.half)
+        out[:, other] = self.rest[...]
+
+
+class RingScatter:
+    copies_needed = 4
+
+    def __init__(self, copies, place, scratch):
+        self.copies, self.place = copies, place
+        self.part, self.far, self.near = scratch
+
+    @staticmethod
+    def scratch():
+        return [
+            pltpu.VMEM((3, BLOCK, D), BF),
+            pltpu.VMEM((2, 64, D), BF),
+            pltpu.VMEM((2, BLOCK, D), BF),
+        ]
+
+    def send_far(self):
+        p, c = self.place, self.copies
+        self.up = c.put(self.part.at[2, 0:64], self.far.at[0], p.at(dz=1))
+        self.down = c.put(self.part.at[2, 64:128], self.far.at[1], p.at(dz=-1))
+
+    def send_above(self):
+        self.up.wait_recv()
+        self.part[0, 0:64] = (self.part[0, 0:64].astype(F32) + self.far[0].astype(F32)).astype(BF)
+        self.up2 = self.copies.put(self.part.at[0], self.near.at[0], self.place.at(dz=1))
+
+    def send_below(self):
+        self.down.wait_recv()
+        self.part[1, 64:128] = (self.part[1, 64:128].astype(F32) + self.far[1].astype(F32)).astype(BF)
+        self.down2 = self.copies.put(self.part.at[1], self.near.at[1], self.place.at(dz=-1))
+
+    def received(self):
+        self.up2.wait_recv()
+        self.down2.wait_recv()
+        return self.near[0].astype(F32) + self.near[1].astype(F32)
+
+
+class RingReturn:
+    copies_needed = 6
+
+    def __init__(self, copies, place, scratch):
+        self.copies, self.place = copies, place
+        self.part, self.near, self.mid, self.far = scratch
+
+    @staticmethod
+    def scratch():
+        return [
+            pltpu.VMEM((3, BLOCK, D), BF),
+            pltpu.VMEM((2, BLOCK, D), BF),
+            pltpu.VMEM((2, 64, D), BF),
+            pltpu.VMEM((BLOCK, D), BF),
+        ]
+
+    def send_above(self):
+        self.up = self.copies.put(self.part.at[0], self.near.at[0], self.place.at(dz=1))
+
+    def send_below(self):
+        self.down = self.copies.put(self.part.at[1], self.near.at[1], self.place.at(dz=-1))
+
+    def send_far(self):
+        p, c = self.place, self.copies
+        self.up1 = c.put(self.part.at[2, 0:64], self.mid.at[0], p.at(dz=1))
+        self.down1 = c.put(self.part.at[2, 64:128], self.mid.at[1], p.at(dz=-1))
+
+    def pass_on(self):
+        p, c = self.place, self.copies
+        self.up1.wait_recv()
+        self.up2 = c.put(self.mid.at[0], self.far.at[0:64], p.at(dz=1))
+        self.down1.wait_recv()
+        self.down2 = c.put(self.mid.at[1], self.far.at[64:128], p.at(dz=-1))
+
+    def received(self):
+        for copy in (self.up, self.down, self.up2, self.down2):
+            copy.wait_recv()
+        return self.near[0].astype(F32) + self.near[1].astype(F32) + self.far[...].astype(F32)
+
+
+def norm_back(hat, scale, grad, gain):
+    inner = grad * gain
+    mean = jnp.mean(inner, axis=-1, keepdims=True)
+    along = jnp.mean(inner * hat, axis=-1, keepdims=True)
     return (
-        0.5
-        * values
-        * (1.0 + jnp.tanh(0.7978845608028654 * (values + 0.044715 * values * values * values)))
+        scale * (inner - mean - hat * along),
+        jnp.sum(grad * hat, axis=0, keepdims=True),
+        jnp.sum(grad, axis=0, keepdims=True),
     )
 
 
-def sequence_of(lengths, positions):
-    bounds = jnp.cumsum(lengths) * BLOCK
-    found_seq = jnp.sum((positions[:, None] >= bounds[None, :]).astype(jnp.int32), axis=1)
-    return jnp.where(positions >= 0, found_seq, -1)
-
-
-def contract_rows(left_side, right_side):
-    return lax.dot_general(
-        left_side, right_side, (((0,), (0,)), ((), ())), preferred_element_type=jnp.float32
+def weight_grad(left, right, out, first):
+    width = right.shape[1]
+
+    def tile(k, carry):
+        turned = left[:, pl.ds(pl.multiple_of(k * 256, 256), 256)].astype(F32).T.astype(BF)
+        out[rows(k * 256, 256), first:first + width] = nn(turned, right[...]).astype(BF)
+        return carry
+
+    lax.fori_loop(0, 4, tile, 0)
+
+
+def middle_kernel(
+    x_ref, ctx_ref, w_ref, vec_ref, cotg_ref,
+    out_ref, gafter_ref, gaf_ref, dctx_ref, dw_ref, sums_ref,
+    n2g, act, dpre, dact, own, after, g, send_sem, recv_sem, *scratch,
+):
+    p = Place()
+    greet(
+        [p.at(dz=1), p.at(dz=-1), p.at(dx=1), p.at(dx=-1), p.at(dy=1), p.at(dy=-1), p.at(flip=True)]
     )
-
-
-def contract_cols(left_side, right_side):
-    return lax.dot_general(
-        left_side, right_side, (((1,), (1,)), ((), ())), preferred_element_type=jnp.float32
+    copies = Copies(send_sem, recv_sem)
+    scatter1 = RingScatter(copies, p, scratch[0:3])
+    outs = RingReturn(copies, p, scratch[3:7])
+    backs = RingReturn(copies, p, scratch[7:11])
+    plane = PlaneScatter(copies, p, g, scratch[11:19])
+
+    def block(dz):
+        return rows(lax.rem(p.z + dz + 4, 4) * BLOCK, BLOCK)
+
+    def out_part(dz):
+        return nt(ctx_ref[block(dz), :], w_ref[:, 768:1024])
+
+    scatter1.part[2] = out_part(2).astype(BF)
+    scatter1.send_far()
+    scatter1.part[0] = out_part(1).astype(BF)
+    scatter1.send_above()
+    scatter1.part[1] = out_part(-1).astype(BF)
+    scatter1.send_below()
+    after[...] = x_ref[...].astype(F32) + out_part(0) + vec_ref[4:5, :]
+
+    def act_grad(t, carry):
+        cols = pl.ds(pl.multiple_of(2048 + t * 256, 256), 256)
+        dact[:, pl.ds(pl.multiple_of(t * 256, 256), 256)] = nn(cotg_ref[...], w_ref[:, cols])
+        return carry
+
+    lax.fori_loop(0, 4, act_grad, 0)
+    after[...] += scatter1.received()
+    hat, scale = normalised(after[...])
+    n2g[block(0), :] = (hat * vec_ref[1:2, :] + vec_ref[3:4, :]).astype(BF)
+    ring = RingGather(copies, p, n2g)
+    ring.start()
+
+    def mlp(dz, put_out, put_back):
+        here = block(dz)
+
+        def hidden(t, carry):
+            cols = pl.ds(pl.multiple_of(t * 256, 256), 256)
+            pre = nn(n2g[here, :], w_ref[:, pl.ds(pl.multiple_of(1024 + t * 256, 256), 256)])
+            pre = pre + vec_ref[8:9, cols]
+            square = pre * pre
+            bend = jnp.tanh(0.7978845608028654 * pre * (1.0 + 0.044715 * square))
+            act[here, cols] = (0.5 * pre * (1.0 + bend)).astype(BF)
+            slope = 0.5 * (1.0 + bend) + 0.5 * pre * (1.0 - bend * bend) * (
+                0.7978845608028654 * (1.0 + 0.134145 * square)
+            )
+            dpre[here, cols] = (dact[here, cols] * slope).astype(BF)
+            return carry
+
+        lax.fori_loop(0, 4, hidden, 0)
+
+        def project(t, carry):
+            cols = pl.ds(pl.multiple_of(t * 256, 256), 256)
+            put_back(cols, nt(dpre[here, :], w_ref[cols, 1024:2048]))
+            put_out(cols, nt(act[here, :], w_ref[cols, 2048:3072]))
+            return carry
+
+        lax.fori_loop(0, 4, project, 0)
+
+    def into(ref, k):
+        def put(cols, value):
+            ref[k, :, cols] = value.astype(ref.dtype)
+
+        return put
+
+    mlp(0, into(own, 0), into(own, 1))
+    ring.below()
+    ring.above()
+    mlp(-1, into(outs.part, 1), into(backs.part, 1))
+    backs.send_below()
+    outs.send_below()
+    mlp(1, into(outs.part, 0), into(backs.part, 0))
+    backs.send_above()
+    outs.send_above()
+    ring.far()
+    mlp(2, into(outs.part, 2), into(backs.part, 2))
+    backs.send_far()
+    outs.send_far()
+    weight_grad(n2g, dpre, g, 0)
+    backs.pass_on()
+    outs.pass_on()
+    weight_grad(cotg_ref, act, g, 1024)
+    plane.start()
+    sums_ref[...] = jnp.zeros_like(sums_ref)
+    sums_ref[4:5, :] = jnp.sum(dpre[...].astype(F32), axis=0, keepdims=True)
+    grad = own[1] + backs.received()
+    hat, scale = normalised(after[...])
+    back, gain, shift = norm_back(hat, scale, grad, vec_ref[1:2, :])
+    residual = cotg_ref[block(0), :].astype(F32)
+    back = back + residual
+    gaf_ref[block(0), :] = back.astype(BF)
+    ring2 = RingGather(copies, p, gaf_ref)
+    ring2.start()
+    gafter_ref[...] = back
+    sums_ref[0:1, :] = gain
+    sums_ref[1:2, :] = shift
+    sums_ref[2:3, :] = jnp.sum(back, axis=0, keepdims=True)
+    sums_ref[3:4, :] = jnp.sum(residual, axis=0, keepdims=True)
+    plane.step1()
+
+    def context_grad(dz):
+        here = block(dz)
+        dctx_ref[here, :] = nn(gaf_ref[here, :], w_ref[:, 768:1024]).astype(BF)
+
+    context_grad(0)
+    ring2.below()
+    ring2.above()
+    plane.step2()
+    out_ref[...] = after[...] + own[0] + outs.received() + vec_ref[5:6, :]
+    context_grad(-1)
+    context_grad(1)
+    ring2.far()
+    context_grad(2)
+    plane.step3()
+    plane.step4()
+    plane.step5()
+    plane.step6(dw_ref)
+    copies.finish()
+
+
+N3_COPIES = 4 + 12 + 8 + 18
+
+
+def call_middle(x, ctx, w, vec, cotg):
+    return pl.pallas_call(
+        middle_kernel,
+        out_shape=(
+            jax.ShapeDtypeStruct((BLOCK, D), F32),
+            jax.ShapeDtypeStruct((BLOCK, D), F32),
+            jax.ShapeDtypeStruct((GROUP, D), BF),
+            jax.ShapeDtypeStruct((GROUP, 256), BF),
+            jax.ShapeDtypeStruct((32, 2048), F32),
+            jax.ShapeDtypeStruct((8, D), F32),
+        ),
+        in_specs=vm(5),
+        out_specs=tuple(vm(6)),
+        scratch_shapes=[
+            pltpu.VMEM((GROUP, D), BF),
+            pltpu.VMEM((GROUP, D), BF),
+            pltpu.VMEM((GROUP, D), BF),
+            pltpu.VMEM((GROUP, D), F32),
+            pltpu.VMEM((2, BLOCK, D), F32),
+            pltpu.VMEM((BLOCK, D), F32),
+            pltpu.VMEM((D, 2048), BF),
+            pltpu.SemaphoreType.DMA((N3_COPIES,)),
+            pltpu.SemaphoreType.DMA((N3_COPIES,)),
+            *RingScatter.scratch(),
+            *RingReturn.scratch(),
+            *RingReturn.scratch(),
+            *PlaneScatter.scratch(2048),
+        ],
+        compiler_params=pltpu.CompilerParams(
+            collective_id=2, has_side_effects=True, vmem_limit_bytes=VMEM_LIMIT
+        ),
+        name="mlp_both_ways",
+    )(x, ctx, w, vec, cotg)
+
+
+def last_kernel(
+    x_ref, dq_ref, dkv_ref, n1_ref, w_ref, vec_ref, gafter_ref, gaf_ref, ctx_ref, sums_ref,
+    gin_ref, dw_ref, small_ref,
+    part, cross, hand, land, dqkv, g, zsum, ysum, csum, send_sem, recv_sem, *scratch,
+):
+    p = Place()
+    greet(
+        [p.at(dz=1), p.at(dz=-1), p.at(dz=2), p.at(dx=1), p.at(dx=-1), p.at(dx=2),
+         p.at(dy=1), p.at(dy=-1), p.at(dy=2), p.at(flip=True), p.linear(1), p.linear(-1)]
     )
-
-
-def gather_rows(normed):
-    return lax.all_gather(normed.astype(jnp.bfloat16), "tensor", axis=0, tiled=True)
-
-
-def gather_grads(gradient):
-    return lax.all_gather(gradient.astype(jnp.bfloat16), "tensor", axis=0, tiled=True)
-
-
-def tensor_sum(left_side, right_side):
-    row_count = left_side.shape[0] // lax.axis_size("tensor")
-
-    def partial_value(start_row, row_num):
-        return jnp.dot(left_side, right_side, preferred_element_type=jnp.float32)
-
-    return lax.psum_scatter(
-        partial_value(jnp.int32(0), row_count * lax.axis_size("tensor")),
-        "tensor",
-        scatter_dimension=0,
-        tiled=True,
+    copies = Copies(send_sem, recv_sem)
+    scatter = RingScatter(copies, p, scratch[0:3])
+    plane = PlaneScatter(copies, p, g, scratch[3:11])
+    sibling = p.at(flip=True)
+    even = p.c == 0
+
+    def block(k):
+        return rows(lax.rem(p.z + k, 4) * BLOCK, BLOCK)
+
+    order = (2, 1, 3, 0)
+    crossing = []
+    for k in order:
+        start = lax.rem(p.z + k, 4) * BLOCK
+        for side in range(2):
+            source = dkv_ref.at[rows((1 + 2 * side) * GROUP + start, BLOCK)]
+            crossing.append(copies.put(source, cross.at[side, block(k)], sibling))
+    far = []
+    for i, k in enumerate(order):
+        start = lax.rem(p.z + k, 4) * BLOCK
+        crossing[2 * i].wait_recv()
+        crossing[2 * i + 1].wait_recv()
+        low = cross[0, block(k)].astype(F32)
+        high = cross[1, block(k)].astype(F32)
+        hand[0, block(k)] = (dkv_ref[rows(start, BLOCK), :].astype(F32) + jnp.where(even, 0.0, low)).astype(BF)
+        far.append(copies.put(hand.at[0, block(k)], land.at[0, block(k)], p.linear(-1)))
+        part[0, block(k)] = dkv_ref[rows(2 * GROUP + start, BLOCK), :].astype(F32) + jnp.where(even, low, high)
+        part[1, block(k)] = dkv_ref[rows(4 * GROUP + start, BLOCK), :].astype(F32) + jnp.where(even, high, 0.0)
+    dqkv[:, 0:256] = dq_ref[...]
+    near = []
+    for i, k in enumerate(order):
+        far[i].wait_recv()
+        hand[1, block(k)] = (part[0, block(k)] + land[0, block(k)].astype(F32)).astype(BF)
+        near.append(copies.put(hand.at[1, block(k)], land.at[1, block(k)], p.linear(-1)))
+    weight_grad(gaf_ref, ctx_ref, g, 768)
+    small_ref[...] = jnp.zeros_like(small_ref)
+    small_ref[8:9, :] = sums_ref[4:5, :]
+    small_ref[9:10, 0:256] = jnp.sum(dq_ref[...].astype(F32), axis=0, keepdims=True)
+
+    def grad_part(i, k):
+        near[i].wait_recv()
+        dqkv[block(k), 256:768] = (part[1, block(k)] + land[1, block(k)].astype(F32)).astype(BF)
+        return nt(dqkv[block(k), :], w_ref[:, 0:768])
+
+    scatter.part[2] = grad_part(0, 2).astype(BF)
+    scatter.send_far()
+    scatter.part[0] = grad_part(1, 1).astype(BF)
+    scatter.send_above()
+    scatter.part[1] = grad_part(2, 3).astype(BF)
+    scatter.send_below()
+    grad = grad_part(3, 0)
+    weight_grad(n1_ref, dqkv, g, 0)
+    plane.start()
+    small_ref[10:11, 0:256] = jnp.sum(dqkv[:, 512:768].astype(F32), axis=0, keepdims=True)
+    grad = grad + scatter.received()
+    hat, scale = normalised(x_ref[...].astype(F32))
+    back, gain, shift = norm_back(hat, scale, grad, vec_ref[0:1, :])
+    small_ref[0:1, :] = gain
+    small_ref[1:2, :] = sums_ref[0:1, :]
+    small_ref[2:3, :] = shift
+    small_ref[3:6, :] = sums_ref[1:4, :]
+    top = small_ref.at[0:8]
+    sends = [copies.put(top, zsum.at[i], p.at(dz=dz)) for i, dz in enumerate((1, -1, 2))]
+    plane.step1()
+    gin_ref[...] = gafter_ref[...] + back
+    for copy in sends:
+        copy.wait_recv()
+    copies.settle(*sends)
+    small_ref[0:8, :] = small_ref[0:8, :] + zsum[0] + zsum[1] + zsum[2]
+    send = copies.put(small_ref, csum.at[0], sibling)
+    plane.step2()
+    send.wait_recv()
+    csum[1] = small_ref[...] + csum[0]
+    sends = [copies.put(csum.at[1], ysum.at[i], p.at(dy=dy)) for i, dy in enumerate((1, -1, 2))]
+    plane.step3()
+    for copy in sends:
+        copy.wait_recv()
+    csum[2] = csum[1] + ysum[0] + ysum[1] + ysum[2]
+    sends = [copies.put(csum.at[2], ysum.at[3 + i], p.at(dx=dx)) for i, dx in enumerate((1, -1, 2))]
+    plane.step4()
+    plane.step5()
+    for copy in sends:
+        copy.wait_recv()
+    copies.settle(send)
+    small_ref[...] = csum[2] + ysum[3] + ysum[4] + ysum[5]
+    plane.step6(dw_ref)
+    copies.finish()
+
+
+N5_COPIES = 8 + 4 + 4 + 4 + 18 + 3 + 1 + 3 + 3
+
+
+def call_last(x, dq, dkv, n1, w, vec, gafter, gaf, ctx, sums):
+    return pl.pallas_call(
+        last_kernel,
+        out_shape=(
+            jax.ShapeDtypeStruct((BLOCK, D), F32),
+            jax.ShapeDtypeStruct((32, 1024), F32),
+            jax.ShapeDtypeStruct((16, D), F32),
+        ),
+        in_specs=vm(10),
+        out_specs=tuple(vm(3)),
+        scratch_shapes=[
+            pltpu.VMEM((2, GROUP, 512), F32),
+            pltpu.VMEM((2, GROUP, 512), BF),
+            pltpu.VMEM((2, GROUP, 512), BF),
+            pltpu.VMEM((2, GROUP, 512), BF),
+            pltpu.VMEM((GROUP, 768), BF),
+            pltpu.VMEM((D, 1024), BF),
+            pltpu.VMEM((3, 8, D), F32),
+            pltpu.VMEM((6, 16, D), F32),
+            pltpu.VMEM((3, 16, D), F32),
+            pltpu.SemaphoreType.DMA((N5_COPIES,)),
+            pltpu.SemaphoreType.DMA((N5_COPIES,)),
+            *RingScatter.scratch(),
+            *PlaneScatter.scratch(1024),
+        ],
+        compiler_params=pltpu.CompilerParams(
+            collective_id=3, has_side_effects=True, vmem_limit_bytes=VMEM_LIMIT
+        ),
+        name="project_back",
+    )(x, dq, dkv, n1, w, vec, gafter, gaf, ctx, sums)
+
+
+def on_device(inputs, lengths, w_qkv, w_out, w_fc, w_proj, b_qv, b_fc, gains, shifts, cotangent):
+    dp, z = lax.axis_index("dp"), lax.axis_index("tensor")
+    first = first_blocks(lengths)
+    n1, q, kv, cotg, w, vec, _ = call_first(
+        inputs,
+        cotangent,
+        pack_weights(w_qkv, w_out, w_fc, w_proj),
+        pack_small(gains[0], shifts[0], b_qv[0], b_fc[0]),
     )
-
-
-def tensor_back(left_side, right_side):
-    row_count = left_side.shape[0] // lax.axis_size("tensor")
-
-    def partial_value(start_row, row_num):
-        return contract_cols(left_side, right_side)
-
-    return lax.psum_scatter(
-        partial_value(jnp.int32(0), row_count * lax.axis_size("tensor")),
-        "tensor",
-        scatter_dimension=0,
-        tiled=True,
-    )
-
-
-def split_heads(qkv_low, key_set):
-    heads_local = qkv_low.shape[2] // HEAD_DIM
-    queries = qkv_low[:, 0].reshape(qkv_low.shape[0], heads_local, HEAD_DIM)
-    key_rows = key_set[:, 0].reshape(key_set.shape[0], heads_local, HEAD_DIM)
-    value_rows = key_set[:, 1].reshape(key_set.shape[0], heads_local, HEAD_DIM)
-    return (queries, key_rows, value_rows)
-
-
-def attend_forward(qkv_low, key_set, allowed):
-    queries, key_rows, value_rows = split_heads(qkv_low, key_set)
-    scores = jnp.einsum(
-        "qhd,khd->hqk", queries, key_rows, preferred_element_type=jnp.float32
-    ) * HEAD_DIM ** (-0.5)
-    masked = jnp.where(allowed[None], scores, -1e30)
-    row_peak = jnp.max(masked, axis=-1, keepdims=True)
-    exp_scores = jnp.exp(masked - row_peak)
-    row_total = jnp.sum(exp_scores, axis=-1, keepdims=True)
-    soft_weights = (exp_scores / row_total).astype(jnp.bfloat16)
-    context = jnp.einsum(
-        "hqk,khd->qhd", soft_weights, value_rows, preferred_element_type=jnp.float32
-    )
+    ctx, lse = call_attend(first, q, kv)
+    out, gafter, gaf, dctx, dw_mlp, sums = call_middle(inputs, ctx, w, vec, cotg)
+    dq, dkv = call_attend_back(first, q, kv, ctx, lse, dctx)
+    gin, dw_attn, small = call_last(inputs, dq, dkv, n1, w, vec, gafter, gaf, ctx, sums)
+    own = lax.dynamic_slice(small, (0, (dp * 4 + z) * 8), (6, 8))
     return (
-        context.reshape(qkv_low.shape[0], -1).astype(jnp.bfloat16),
-        row_peak + jnp.log(row_total),
-    )
-
-
-def attend_backward(qkv_low, key_set, allowed, log_total, grad_context):
-    queries, key_rows, value_rows = split_heads(qkv_low, key_set)
-    score_scale = HEAD_DIM ** (-0.5)
-    scores = (
-        jnp.einsum("qhd,khd->hqk", queries, key_rows, preferred_element_type=jnp.float32)
-        * score_scale
-    )
-    masked = jnp.where(allowed[None], scores, -1e30)
-    soft_weights = jnp.exp(masked - log_total)
-    grad_heads = grad_context.reshape(queries.shape)
-    grad_soft = jnp.einsum(
-        "qhd,khd->hqk", grad_heads, value_rows, preferred_element_type=jnp.float32
-    )
-    row_inner = jnp.sum(soft_weights * grad_soft, axis=-1, keepdims=True)
-    grad_scores = (soft_weights * (grad_soft - row_inner)).astype(jnp.bfloat16)
-    grad_queries = (
-        jnp.einsum("hqk,khd->qhd", grad_scores, key_rows, preferred_element_type=jnp.float32)
-        * score_scale
-    )
-    grad_keys = (
-        jnp.einsum("hqk,qhd->khd", grad_scores, queries, preferred_element_type=jnp.float32)
-        * score_scale
-    )
-    grad_values = jnp.einsum(
-        "hqk,qhd->khd",
-        soft_weights.astype(jnp.bfloat16),
-        grad_heads,
-        preferred_element_type=jnp.float32,
-    )
-    key_count = key_set.shape[0]
-    grad_pairs = jnp.stack(
-        [grad_keys.reshape(key_count, -1), grad_values.reshape(key_count, -1)], axis=1
-    )
-    return (grad_queries.reshape(qkv_low.shape[0], -1), grad_pairs)
-
-
-def on_device(inputs, lengths, w_qkv, w_out, w_fc, w_proj, b_qv, b_fc, gains, shifts, cotangent):
-    n1, q, kv, cotg, wall, vec, bqv = call_first(
-        inputs, cotangent, pack_weights(w_qkv, w_out, w_fc, w_proj),
-        pack_small(gains[0], shifts[0], b_qv[0], b_fc[0])
-    )
-    all_gains, all_shifts = vec[None, 0:2], vec[None, 2:6]
-    group_index = lax.axis_index("dp")
-    tok_group = 512
-    query_pos = group_index * tok_group + jnp.arange(tok_group, dtype=jnp.int32)
-    key_pos = (group_index - SPAN) * tok_group + jnp.arange((SPAN + 1) * tok_group, dtype=jnp.int32)
-    same_seq = sequence_of(lengths, query_pos)[:, None] == sequence_of(lengths, key_pos)[None, :]
-    allowed = same_seq & (key_pos[None, :] <= query_pos[:, None])
-    residual = inputs.astype(jnp.float32)
-    levels = 1
-    weight_qkv, weight_out, weight_fc, weight_proj = (
-        wall[:, :768].reshape(1024, 3, 256), wall[:, 768:1024].T, wall[:, 1024:2048], wall[:, 2048:].T)
-    bias_fc = vec[8]
-    fetched = None
-    layer_gains, layer_shifts = all_gains[0], all_shifts[0]
-    gathered_one = n1
-    key_set = kv.reshape(2560, 2, 256)
-    qkv_low = jnp.concatenate([q[:, None], key_set[2048:]], axis=1)
-    context_low, log_total = attend_forward(qkv_low, key_set, allowed)
-    after = residual + tensor_sum(context_low, weight_out) + layer_shifts[2]
-    gathered_two = gather_rows(layer_norm(after, layer_gains[1], layer_shifts[1]))
-    pre_act = jnp.dot(gathered_two, weight_fc, preferred_element_type=jnp.float32) + bias_fc.astype(
-        jnp.float32
-    )
-    act_low = gelu_tanh(pre_act).astype(jnp.bfloat16)
-    output_rows = after + tensor_sum(act_low, weight_proj) + layer_shifts[3]
-    grad_res = cotangent.astype(jnp.float32)
-    reduced = [None] * levels
-    gain_parts = [None] * levels
-    shift_parts = [None] * levels
-    layer_index = 0
-    layer_index = 0
-    layer_input = residual
-    grad_mlp = cotg
-    grad_weight_proj = contract_rows(act_low, grad_mlp)
-    grad_act = contract_cols(grad_mlp, weight_proj)
-    gelu_value, gelu_pull = jax.vjp(gelu_tanh, pre_act)
-    grad_pre = gelu_pull(grad_act)[0].astype(jnp.bfloat16)
-    grad_bias_fc = jnp.sum(grad_pre.astype(jnp.float32), axis=0)
-    grad_weight_fc = contract_rows(gathered_two, grad_pre)
-    grad_normed_two = tensor_back(grad_pre, weight_fc)
-    norm_value, norm_pull = jax.vjp(layer_norm, after, layer_gains[1], layer_shifts[1])
-    grad_after_norm, grad_gain_two, grad_shift_two = norm_pull(grad_normed_two)
-    grad_after = grad_res + grad_after_norm
-    grad_mlp_bias = jnp.sum(grad_res, axis=0)
-    grad_attn = gather_grads(grad_after)
-    grad_weight_out = contract_rows(context_low, grad_attn)
-    grad_context = contract_cols(grad_attn, weight_out).astype(jnp.bfloat16)
-    grad_queries, grad_pairs = attend_backward(qkv_low, key_set, allowed, log_total, grad_context)
-    pair_pieces = grad_pairs.reshape(SPAN + 1, tok_group, 2, grad_pairs.shape[2])
-    pair_total = pair_pieces[SPAN]
-    carried = jnp.zeros_like(pair_total)
-    for hop_index in range(SPAN, 0, -1):
-        carried = from_behind(carried + pair_pieces[SPAN - hop_index], "dp", -1)
-    pair_total = pair_total + carried
-    grad_qkv = jnp.concatenate([grad_queries[:, None], pair_total], axis=1).astype(jnp.bfloat16)
-    grad_qkv_wide = grad_qkv.astype(jnp.float32)
-    grad_bias_qv = jnp.stack(
-        [jnp.sum(grad_qkv_wide[:, 0], axis=0), jnp.sum(grad_qkv_wide[:, 2], axis=0)]
-    )
-    grad_flat = grad_qkv.reshape(tok_group, -1)
-    grad_weight_qkv = contract_rows(gathered_one, grad_flat).reshape(weight_qkv.shape)
-    grad_normed_one = tensor_back(grad_flat, weight_qkv.reshape(weight_qkv.shape[0], -1))
-    norm_value, norm_pull = jax.vjp(layer_norm, layer_input, layer_gains[0], layer_shifts[0])
-    grad_input_norm, grad_gain_one, grad_shift_one = norm_pull(grad_normed_one)
-    grad_attn_bias = jnp.sum(grad_after, axis=0)
-    grad_res = grad_after + grad_input_norm
-    reduced[layer_index] = (
-        lax.psum_scatter(grad_weight_qkv, "dp", scatter_dimension=0, tiled=True),
-        lax.psum_scatter(grad_weight_out, "dp", scatter_dimension=1, tiled=True),
-        lax.psum_scatter(grad_weight_fc, "dp", scatter_dimension=0, tiled=True),
-        lax.psum_scatter(grad_weight_proj, "dp", scatter_dimension=1, tiled=True),
-        lax.psum_scatter(grad_bias_qv, "dp", scatter_dimension=1, tiled=True),
-        lax.psum_scatter(grad_bias_fc, "dp", scatter_dimension=0, tiled=True),
-    )
-    gain_parts[layer_index] = jnp.stack([grad_gain_one, grad_gain_two])
-    shift_parts[layer_index] = jnp.stack(
-        [grad_shift_one, grad_shift_two, grad_attn_bias, grad_mlp_bias]
-    )
-    grad_gains, grad_shifts = (
-        lax.psum_scatter(jnp.stack(gain_parts), ("dp", "tensor"), scatter_dimension=2, tiled=True),
-        lax.psum_scatter(jnp.stack(shift_parts), ("dp", "tensor"), scatter_dimension=2, tiled=True),
-    )
-    grad_w_qkv = jnp.stack([reduced[0][0]])
-    grad_w_out = jnp.stack([reduced[0][1]])
-    grad_w_fc = jnp.stack([reduced[0][2]])
-    grad_w_proj = jnp.stack([reduced[0][3]])
-    grad_b_qv = jnp.stack([reduced[0][4]])
-    grad_b_fc = jnp.stack([reduced[0][5]])
-    return (
-        output_rows,
-        grad_res,
-        grad_w_qkv,
-        grad_w_out,
-        grad_w_fc,
-        grad_w_proj,
-        grad_b_qv,
-        grad_b_fc,
-        grad_gains,
-        grad_shifts,
+        out,
+        gin,
+        dw_attn[:, :768].reshape(1, 32, 3, 256),
+        dw_attn[:, 768:].T[None],
+        dw_mlp[None, :, :1024],
+        dw_mlp[:, 1024:].T[None],
+        lax.dynamic_slice(small, (9, dp * 8), (2, 8))[None],
+        lax.dynamic_slice(small, (8, dp * 32), (1, 32)),
+        own[None, 0:2],
+        own[None, 2:6],
     )
 
 

time: 794 us -> 282 us (0.36); the launches traced: 784 us -> 284 us
  waiting for transfers between devices: 385 us -> 0 us
  Pallas kernels: 71.1 us -> 267 us
  blocking collectives: 140 us -> 0 us
  matrix products: 89.5 us -> 0 us
  other arithmetic: 41.9 us -> 5.24 us
  local copies, waits for them, and re-layouts: 33.6 us -> 11.3 us
  between operations: 16.3 us -> 0.77 us
    reduce_scatter x8 -> x0, waiting for transfers between devices: 298 us -> none  [the longest x1 84.2 us: on_device(): lax.psum_scatter(grad_weight_qkv, 'dp', scatter_dimension=0, tiled=True)]
    pallas_call x0 -> x4, Pallas kernels: none -> 196 us  [the longest x1 96 us: call_middle(): pl.pallas_call(middle_kernel, out_shape=(jax.ShapeDtypeStruct((BLOCK, D),...]
    unnamed x2 -> x0, blocking collectives: 140 us -> none
    dot_general x17 -> x0, matrix products: 89.5 us -> none  [the longest x4 17 us: contract_rows(): lax.dot_general(left_side, right_side, (((0,), (0,)), ((), ())), preferre...]
    all_gather x2 -> x0, waiting for transfers between devices: 47.5 us -> none  [the longest x1 23.9 us: gather_rows(): lax.all_gather(normed.astype(jnp.bfloat16), 'tensor', axis=0, tiled=True)]
    ppermute x4 -> x0, waiting for transfers between devices: 39.8 us -> none  [from_behind(): lax.ppermute(value, axis, [(source, source + steps) for source in range(f...]
    convert_element_type x3 -> x0, other arithmetic: 19.2 us -> none  [the longest x1 18.1 us: attend_backward(): grad_scores = (soft_weights * (grad_soft - row_inner)).astype(jnp.bfloat16)]
    slice x4 -> x1, local copies, waits for them, and re-layouts: 17.2 us -> 0.9 us  [on_device(): dw_attn[:, :768].reshape(1, 32, 3, 256)]
  transfers between devices with their start and end apart: 14 -> 0, of which waited for: 12 -> 0; matrix products, arithmetic and copies ran while one was open for 5% -> 0% of each run, Pallas kernels for 0% -> 0%
where the time goes in v2:
time: 282 us; the launch traced here: 284 us
  Pallas kernels  267 us (95%)
  local copies, waits for them, and re-layouts  11.3 us (4%)
  other arithmetic  5.24 us (2%)
    pallas_call x1, Pallas kernels, call_middle(): pl.pallas_call(middle_kernel, out_shape=(jax.ShapeDtypeStruct((BLOCK, D),...  96 us
    pallas_call x1, Pallas kernels, call_last(): pl.pallas_call(last_kernel, out_shape=(jax.ShapeDtypeStruct((BLOCK, D), F...  82.2 us
    pallas_call x1, Pallas kernels, call_first(): pl.pallas_call(first_kernel, out_shape=(jax.ShapeDtypeStruct((GROUP, D),...  71.1 us
    pallas_call x1, Pallas kernels, call_attend_back(): pl.pallas_call(attend_back_kernel, out_shape=(jax.ShapeDtypeStruct((GROUP...  9.97 us
    pallas_call x1, Pallas kernels, call_attend(): pl.pallas_call(attend_kernel, out_shape=(jax.ShapeDtypeStruct((GROUP, 256...  7.54 us

profile of v2, /device:TPU:0, one launch (start us, length us, event | category | flops | bytes accessed | tf_op | source)
XLA Modules:
  0.0 284.2 jit_solution(6760082279051127615)
XLA Ops:
  0.7 0.1 pad.6.clone
  0.7 0.8 maximum_maximum_fusion.1
  1.5 0.1 tile.32
  1.6 0.7 bitcast_convert_fusion
  2.3 0.1 tile.38
  2.4 0.7 bitcast_convert_fusion.1
  3.1 0.1 tile.36
  3.2 0.1 pad.3.clone
  3.3 0.7 maximum_maximum_fusion.small_ref
  3.9 0.8 copy.28
  4.8 1.6 pad_maximum_fusion.shard_ref
  6.4 71.1 %gather_and_project.1 = (bf16[512,1024]{1,0:T(8,128)(2,1)}, bf16[512,256]{1,0:T(8,128)(2,1)}, bf16[2560,512]{1,0:T(8,128)(2,1)}, bf16[512,1024]{1,0:T(8,128)(2,1...) custom-call(bf16[128,1024]{1,0:T(8,128)(2,1)} %x_ref.5, bf16[128,1024]{1,0:T(8,128)(2,1)} %cot_ref.1, ...), custom_call_target="tpu_custom_call" | custom-call | tf_op jit(solution)/shard_map/gather_and_project/pallas_call | solution.py:335
  77.5 0.7 copy.27
  78.2 0.1 reduce-window.8
  78.3 0.1 reduce
  78.4 0.2 select_reduce_fusion
  78.6 0.5 subtract_add_fusion.first_ref
  79.1 7.5 %attend.1 = (bf16[512,256]{1,0:T(8,128)(2,1)}, f32[8,512]{1,0:T(8,128)}) custom-call(s32[4]{0:T(128)} %subtract_add_fusion.first_ref, bf16[512,256]{1,0:T(8,128)(2,1)} %get-tuple-element.29.q_ref, bf16[2560,512]{1,0:T(8,128)(2,1)} %get-tuple-element.30.kv_ref), custom_call_target="tpu_custom_call" | custom-call | tf_op jit(solution)/shard_map/attend/pallas_call | solution.py:442
  86.7 96.0 %mlp_both_ways.1 = (f32[128,1024]{1,0:T(8,128)}, f32[128,1024]{1,0:T(8,128)}, bf16[512,1024]{1,0:T(8,128)(2,1)}, bf16[512,256]{1,0:T(8,128)(2,1)}, f32[32,2048]{1,0:T(8,128)}, /*index=5*/f32[8,1024]{1,0:T(8,128)}) custom-call(bf16[128,1024]{1,0:T(8,128)(2,1)} %x_ref.5, bf16[512,256]{1,0:T(8,128)(2,1)} %get-tuple-element.31.ctx_ref, ...), custom_call_target="tpu_custom_call" | custom-call | tf_op jit(solution)/shard_map/mlp_both_ways/pallas_call | solution.py:915
  182.7 10.0 %attend_back.1 = (bf16[512,256]{1,0:T(8,128)(2,1)}, bf16[2560,512]{1,0:T(8,128)(2,1)}) custom-call(s32[4]{0:T(128)} %subtract_add_fusion.first_ref, bf16[512,256]{1,0:T(8,128)(2,1)} %get-tuple-element.29.q_ref, bf16[2560,512]{1,0:T(8,128)(2,1)} %get-tuple-element.30.kv_ref, bf16[512,256]{1,0:T(8,128)(2,1)} %get-tuple-element.31.ctx_ref, ...), custom_call_target="tpu_custom_call" | custom-call | tf_op jit(solution)/shard_map/attend_back/pallas_call | solution.py:526
  192.7 0.0 copy-start.2
  192.7 0.0 copy-start
  192.7 82.2 %project_back.1 = (f32[128,1024]{1,0:T(8,128)}, f32[32,1024]{1,0:T(8,128)}, f32[16,1024]{1,0:T(8,128)}) custom-call(bf16[128,1024]{1,0:T(8,128)(2,1)} %x_ref.5, bf16[512,256]{1,0:T(8,128)(2,1)} %get-tuple-element.38.dq_ref, bf16[2560,512]{1,0:T(8,128)(2,1)} %get-tuple-element.39.dkv_ref, bf16[512,1024]{1,0:T(8,128)(2,1)} %get-tuple-element.40.n1_ref, ...), custom_call_target="tpu_custom_call" | custom-call | tf_op jit(solution)/shard_map/project_back/pallas_call | solution.py:1051
  274.9 0.0 copy-start.1
  274.9 0.8 constant_dynamic-slice_fusion.1
  275.7 1.3 slice_bitcast_fusion.4
  277.0 0.9 slice.18
  277.9 0.1 reshape.185
  278.0 0.7 copy.29
  278.6 1.4 slice_bitcast_fusion.2
  280.0 0.6 slice_bitcast_fusion.3
  280.6 1.3 constant_dynamic-slice_fusion
  281.9 0.0 copy-done.2
  281.9 0.7 slice_bitcast_fusion
  282.6 0.0 copy-done
  282.6 0.8 copy.33
  283.4 0.0 copy-done.1
  283.4 0.8 copy.34
  (12 shorter events, 0.1 us)
Async XLA Ops:
  192.7 89.2 %copy-start.2 = (f32[32,2048]{1,0:T(8,128)S(1)}, f32[32,2048]{1,0:T(8,128)}, u32[]{:S(2)}) copy-start(f32[32,2048]{1,0:T(8,128)} %get-tuple-element.46) | copy-start | bytes 786436
  192.7 89.9 %copy-start = (f32[128,1024]{1,0:T(8,128)S(1)}, f32[128,1024]{1,0:T(8,128)}, u32[]{:S(2)}) copy-start(f32[128,1024]{1,0:T(8,128)} %get-tuple-element.92) | copy-start | bytes 1572868
  274.9 8.5 %copy-start.1 = (f32[128,1024]{1,0:T(8,128)S(1)}, f32[128,1024]{1,0:T(8,128)}, u32[]{:S(2)}) copy-start(f32[128,1024]{1,0:T(8,128)} %get-tuple-element.93) | copy-start | bytes 1572868

commit v3 on v2

v3 whole, which is shorter than its diff:
```python
import functools

import jax
import jax.numpy as jnp
from jax import lax
from jax.experimental import pallas as pl
from jax.experimental.pallas import tpu as pltpu
from jax.sharding import PartitionSpec as P

HEAD_DIM = 64
BLOCK = 128
D = 1024
GROUP = 512
BF = jnp.bfloat16
F32 = jnp.float32
MESH = pl.DeviceIdType.MESH
VMEM_LIMIT = 58 * 1024 * 1024


def nn(a, b):
    return jnp.dot(a, b, preferred_element_type=F32)


def nt(a, b):
    return lax.dot_general(a, b, (((1,), (1,)), ((), ())), preferred_element_type=F32)


def tn(a, b):
    return lax.dot_general(a, b, (((0,), (0,)), ((), ())), preferred_element_type=F32)


def rows(start, size, step=None):
    return pl.ds(pl.multiple_of(start, step or size), size)


class Place:
    def __init__(self):
        self.dp = lax.axis_index("dp")
        self.z = lax.axis_index("tensor")
        self.c = lax.rem(self.dp, 2)
        self.chip = self.dp // 2
        self.y = lax.rem(self.chip, 4)
        self.x = self.chip // 4

    def at(self, dx=0, dy=0, dz=0, flip=False):
        x = lax.rem(self.x + dx + 4, 4)
        y = lax.rem(self.y + dy + 4, 4)
        c = 1 - self.c if flip else self.c
        return ((x * 4 + y) * 2 + c, lax.rem(self.z + dz + 4, 4))

    def linear(self, step):
        return (lax.rem(self.chip + step + 16, 16) * 2 + self.c, self.z)

    def beside(self, dy, step):
        chip = self.x * 4 + lax.rem(self.y + dy + 4, 4)
        return (lax.rem(chip + step + 16, 16) * 2 + self.c, self.z)

    def beside_source(self, step=2, dy=-1):
        chip = lax.rem(self.chip - step + 16, 16)
        y = lax.rem(lax.rem(chip, 4) + dy + 4, 4)
        return ((chip // 4 * 4 + y) * 2 + self.c, self.z)


class Copies:
    def __init__(self, send_sem, recv_sem):
        self.send_sem, self.recv_sem = send_sem, recv_sem
        self.started, self.settled = [], []

    def put(self, src, dst, device):
        k = len(self.started)
        copy = pltpu.make_async_remote_copy(
            src_ref=src,
            dst_ref=dst,
            send_sem=self.send_sem.at[k],
            recv_sem=self.recv_sem.at[k],
            device_id=device,
            device_id_type=MESH,
        )
        copy.start()
        self.started.append(copy)
        return copy

    def settle(self, *copies):
        for copy in copies:
            copy.wait_send()
            self.settled.append(copy)

    def finish(self):
        for copy in self.started:
            if not any(copy is other for other in self.settled):
                copy.wait_send()


def greet(devices):
    barrier = pltpu.get_barrier_semaphore()
    for device in devices:
        pl.semaphore_signal(barrier, inc=1, device_id=device, device_id_type=MESH)
    pl.semaphore_wait(barrier, len(devices))


class RingGather:
    def __init__(self, copies, place, buf, size=BLOCK):
        self.copies, self.place, self.buf, self.size = copies, place, buf, size

    def block(self, dz, part=None):
        start = lax.rem(self.place.z + dz + 4, 4) * self.size
        if part is None:
            return self.buf.at[rows(start, self.size)]
        half = self.size // 2
        return self.buf.at[rows(start + part * half, half)]

    def start(self):
        own = self.block(0)
        self.up = self.copies.put(own, own, self.place.at(dz=1))
        self.down = self.copies.put(own, own, self.place.at(dz=-1))

    def below(self):
        self.up.wait_recv()
        half = self.block(-1, 0)
        self.up2 = self.copies.put(half, half, self.place.at(dz=1))

    def above(self):
        self.down.wait_recv()
        half = self.block(1, 1)
        self.down2 = self.copies.put(half, half, self.place.at(dz=-1))

    def far(self):
        self.up2.wait_recv()
        self.down2.wait_recv()


class DirectGather:
    copies_needed = 31

    def __init__(self, copies, place, w):
        self.copies, self.place, self.w = copies, place, w
        self.shared = []

    def dev(self, axis, step):
        c = self.place.c
        if axis == 0:
            return self.place.at(dx=c * step, dy=(1 - c) * step)
        return self.place.at(dx=(1 - c) * step, dy=c * step)

    def block(self, a, b):
        p, c = self.place, self.place.c
        x = lax.rem(p.x + b * (1 - c) + a * c + 4, 4)
        y = lax.rem(p.y + a * (1 - c) + b * c + 4, 4)
        return self.w.at[rows(((x * 4 + y) * 2 + c) * 32, 32)]

    def put(self, ref, device):
        return self.copies.put(ref, ref, device)

    def spread(self, a):
        ref = self.block(a, 0)
        self.second[a] = [self.put(ref, self.dev(1, step)) for step in (1, -1, 2)]
        self.shared.append(self.put(ref, self.place.at(flip=True)))

    def start(self):
        ref = self.block(0, 0)
        self.first = [self.put(ref, self.dev(0, step)) for step in (1, -1, 2)]
        self.second = {}
        self.spread(0)

    def step1(self):
        for copy, a in zip(self.first, (-1, 1, 2)):
            copy.wait_recv()
            self.spread(a)

    def step2(self):
        for a in (0, -1, 1, 2):
            for copy, b in zip(self.second[a], (-1, 1, 2)):
                copy.wait_recv()
                self.shared.append(self.put(self.block(a, b), self.place.at(flip=True)))

    def step3(self):
        for copy in self.shared:
            copy.wait_recv()


class PlaneGather:
    def __init__(self, copies, place, w, first, width):
        self.copies, self.place, self.w = copies, place, w
        c = place.c
        self.first, self.width = first, width
        self.cols = pl.ds(pl.multiple_of(first + c * (width // 2), 128), width // 2)

    def dev(self, axis, step):
        if axis == 0:
            return self.place.at(dy=step)
        return self.place.at(dx=step)

    def block(self, first_off, second_off, part=None):
        p = self.place
        start = (lax.rem(p.x + second_off + 4, 4) * 4 + lax.rem(p.y + first_off + 4, 4)) * 64
        if part is None:
            return self.w.at[rows(start, 64), self.cols]
        return self.w.at[rows(start + 32 * part, 32), self.cols]

    def put(self, ref, device):
        return self.copies.put(ref, ref, device)

    def start(self):
        p = self.place
        mine = self.w.at[rows(p.dp * 32, 32), pl.ds(self.first, self.width)]
        self.swap = self.put(mine, p.at(flip=True))

    def spread(self, first_off):
        ref = self.block(first_off, 0)
        return (self.put(ref, self.dev(1, 1)), self.put(ref, self.dev(1, -1)))

    def share(self, first_off, second_off):
        self.shared.append(self.put(self.block(first_off, second_off), self.place.at(flip=True)))

    def step1(self):
        self.swap.wait_recv()
        ref = self.block(0, 0)
        self.shared = []
        self.up = self.put(ref, self.dev(0, 1))
        self.down = self.put(ref, self.dev(0, -1))
        self.out = {0: self.spread(0)}

    def step2(self):
        self.up.wait_recv()
        self.up2 = self.put(self.block(-1, 0, 0), self.dev(0, 1))
        self.down.wait_recv()
        self.down2 = self.put(self.block(1, 0, 1), self.dev(0, -1))
        self.out[-1] = self.spread(-1)
        self.out[1] = self.spread(1)
        self.share(-1, 0)
        self.share(1, 0)

    def step3(self):
        self.up2.wait_recv()
        self.down2.wait_recv()
        self.out[2] = self.spread(2)
        self.share(2, 0)

    def step4(self):
        self.far = []
        for first_off in (0, -1, 1, 2):
            up, down = self.out[first_off]
            up.wait_recv()
            self.far.append(self.put(self.block(first_off, -1, 0), self.dev(1, 1)))
            down.wait_recv()
            self.far.append(self.put(self.block(first_off, 1, 1), self.dev(1, -1)))
            self.share(first_off, -1)
            self.share(first_off, 1)

    def step5(self):
        for k, first_off in enumerate((0, -1, 1, 2)):
            self.far[2 * k].wait_recv()
            self.far[2 * k + 1].wait_recv()
            self.share(first_off, 2)

    def step6(self):
        for copy in self.shared:
            copy.wait_recv()


def normalised(values):
    centre = values - jnp.mean(values, axis=-1, keepdims=True)
    spread = jnp.mean(centre * centre, axis=-1, keepdims=True)
    scale = lax.rsqrt(spread + 1e-05)
    return centre * scale, scale


def one_hot(shape, offset):
    row = lax.broadcasted_iota(jnp.int32, shape, 0)
    lane = lax.broadcasted_iota(jnp.int32, shape, 1)
    return jnp.where(lane == row + offset, 1.0, 0.0).astype(F32)


def exact(a, b):
    return jnp.dot(a, b, precision=lax.Precision.HIGHEST, preferred_element_type=F32)


def first_kernel(
    x_ref, cot_ref, wqkv_ref, wout_ref, wfc_ref, wproj_ref, gains_ref, shifts_ref, bqv_ref, bfc_ref,
    q_ref, kv_ref, vec_ref, n1_out, xg_out, cotg_out, wqkv_out, wo_out, wmlp_out,
    n1, xg, cotg, wq, wo, wmlp, vz, vall, bias, mid, out_sem, send_sem, recv_sem,
):
    p = Place()
    mine = rows(p.dp * 32, 32)
    for j in range(3):
        wq[mine, j * 256:(j + 1) * 256] = wqkv_ref[j]
    wq[mine, 768:1024] = wout_ref[...]
    wmlp[mine, 0:1024] = wfc_ref[...]
    wmlp[mine, 1024:2048] = wproj_ref[...]
    xg[rows(p.z * BLOCK, BLOCK), :] = x_ref[...]
    cotg[rows(p.z * BLOCK, BLOCK), :] = cot_ref[...]
    place8 = one_hot((8, 128), lax.rem(p.dp * 4 + p.z, 16) * 8)
    own = vz.at[p.z]
    own[...] = jnp.zeros((8, 128), F32)
    own[0:2] = exact(gains_ref[...], place8)
    own[2:6] = exact(shifts_ref[...], place8)
    tile = vall.at[p.c, p.chip]
    tile[8:16] = jnp.zeros((8, 128), F32)
    tile[8:9] = exact(bfc_ref[...].astype(F32), one_hot((32, 128), lax.rem(p.dp, 4) * 32))
    tile[9:11] = exact(bqv_ref[...].astype(F32), one_hot((8, 128), lax.rem(p.dp, 16) * 8))
    greet(
        [p.at(dz=1), p.at(dz=-1), p.at(dz=2), p.at(dx=1), p.at(dx=-1), p.at(dx=2),
         p.at(dy=1), p.at(dy=-1), p.at(dy=2), p.at(flip=True), p.linear(1), p.linear(-1),
         p.beside(1, 2), p.beside_source()]
    )
    copies = Copies(send_sem, recv_sem)
    head = DirectGather(copies, p, wq)
    head.start()
    small = [copies.put(own, own, p.at(dz=dz)) for dz in (1, -1, 2)]
    ring = RingGather(copies, p, xg)
    ring.start()
    tail = PlaneGather(copies, p, wmlp, 0, 2048)
    for copy in small:
        copy.wait_recv()
    tile[0:8] = vz[0] + vz[1] + vz[2] + vz[3]
    small = [copies.put(tile, tile, p.at(dy=dy)) for dy in (1, -1, 2)]
    head.step1()
    tail.start()
    for copy in small:
        copy.wait_recv()
    line = vall.at[p.c, rows(p.x * 4, 4)]
    small = [copies.put(line, line, p.at(dx=dx)) for dx in (1, -1, 2)]
    ring.below()
    ring.above()
    cot_ring = RingGather(copies, p, cotg)
    cot_ring.start()
    for copy in small:
        copy.wait_recv()
    plane = vall.at[p.c]
    last = copies.put(plane, plane, p.at(flip=True))
    head.step2()
    tail.step1()
    ring.far()
    last.wait_recv()
    lanes = []
    for k in range(8):
        total = vall[0, 2 * k] + vall[0, 2 * k + 1] + vall[1, 2 * k] + vall[1, 2 * k + 1]
        vec_ref[:, k * 128:(k + 1) * 128] = total
        lanes.append(total)
    for h in range(2):
        bias[:, h * 128:(h + 1) * 128] = lanes[4 * h] + lanes[4 * h + 1] + lanes[4 * h + 2] + lanes[4 * h + 3]

    def norm_block(k, carry):
        block = rows(lax.rem(p.z + k, 4) * BLOCK, BLOCK)
        hat, _ = normalised(xg[block, :].astype(F32))
        n1[block, :] = (hat * vec_ref[0:1, :] + vec_ref[2:3, :]).astype(BF)
        return carry

    lax.fori_loop(0, 4, norm_block, 0)
    cot_ring.below()
    cot_ring.above()
    head.step3()

    def start_of(k):
        return lax.rem(p.z + k, 4) * BLOCK

    sibling = p.at(flip=True)
    near, there, cross = {}, {}, []
    for k in (2, 0, 3, 1):
        start = start_of(k)
        block = rows(start, BLOCK)
        values = n1[block, :]
        ours = rows(4 * GROUP + start, BLOCK)
        kv_ref[ours, 0:256] = nn(values, wq[:, 256:512]).astype(BF)
        kv_ref[ours, 256:512] = (nn(values, wq[:, 512:768]) + bias[10:11, :]).astype(BF)
        if k < 2:
            there[k] = copies.put(kv_ref.at[ours], mid.at[k], p.at(dy=-1))
        else:
            near[k] = copies.put(kv_ref.at[ours], kv_ref.at[rows(2 * GROUP + start, BLOCK)], p.linear(1))
    for k in (0, 1):
        ours = kv_ref.at[rows(4 * GROUP + start_of(k), BLOCK)]
        near[k] = copies.put(ours, kv_ref.at[rows(2 * GROUP + start_of(k), BLOCK)], p.linear(1))
    wo[rows(p.z * D, D), :] = wq[:, 768:1024]
    wo_ring = RingGather(copies, p, wo, D)
    wo_ring.start()
    tail.step2()
    q_ref[...] = (nn(n1[...], wq[:, 0:256]) + bias[9:10, :]).astype(BF)
    saves = [
        pltpu.make_async_copy(source, target, out_sem.at[i])
        for i, (source, target) in enumerate(
            (
                (n1, n1_out), (xg, xg_out), (wq.at[:, 0:768], wqkv_out), (cotg, cotg_out),
                (wo, wo_out), (wmlp, wmlp_out),
            )
        )
    ]
    for i in range(3):
        saves[i].start()
    far = {}
    for k in (0, 1):
        there[k].wait_recv()
        far[k] = copies.put(mid.at[k], kv_ref.at[rows(start_of(k), BLOCK)], p.beside(1, 2))

    def pass_near(k, onward):
        near[k].wait_recv()
        ref = kv_ref.at[rows(2 * GROUP + start_of(k), BLOCK)]
        if onward:
            far[k] = copies.put(ref, kv_ref.at[rows(start_of(k), BLOCK)], p.linear(1))
        cross.append(
            copies.put(ref, kv_ref.at[rows((1 + 2 * p.c) * GROUP + start_of(k), BLOCK)], sibling)
        )

    pass_near(2, True)
    pass_near(3, True)
    tail.step3()
    cot_ring.far()
    saves[3].start()
    tail.step4()
    pass_near(0, False)
    pass_near(1, False)
    wo_ring.below()
    wo_ring.above()

    def pass_far(k):
        far[k].wait_recv()
        cross.append(
            copies.put(
                kv_ref.at[rows((4 - 4 * p.c) * GROUP + start_of(k), BLOCK)],
                kv_ref.at[rows((3 - 2 * p.c) * GROUP + start_of(k), BLOCK)],
                sibling,
            )
        )

    pass_far(0)
    pass_far(1)
    tail.step5()
    pass_far(2)
    pass_far(3)
    tail.step6()
    saves[5].start()
    wo_ring.far()
    saves[4].start()
    for copy in cross:
        copy.wait_recv()
    for save in saves:
        save.wait()
    copies.finish()


N1_COPIES = 31 + 36 + 10 + 12 + 18


def vm(count):
    return [pl.BlockSpec(memory_space=pltpu.VMEM)] * count


def far_memory(count):
    return [pl.BlockSpec(memory_space=pl.ANY)] * count


def call_first(*operands):
    shape = jax.ShapeDtypeStruct
    return pl.pallas_call(
        first_kernel,
        out_shape=(
            shape((GROUP, 256), BF),
            shape((5 * GROUP, 512), BF),
            shape((16, D), F32),
            shape((GROUP, D), BF),
            shape((GROUP, D), BF),
            shape((GROUP, D), BF),
            shape((D, 768), BF),
            shape((4 * D, 256), BF),
            shape((D, 2048), BF),
        ),
        in_specs=vm(10),
        out_specs=tuple(vm(3) + far_memory(6)),
        scratch_shapes=[
            pltpu.VMEM((GROUP, D), BF),
            pltpu.VMEM((GROUP, D), BF),
            pltpu.VMEM((GROUP, D), BF),
            pltpu.VMEM((D, 1024), BF),
            pltpu.VMEM((4 * D, 256), BF),
            pltpu.VMEM((D, 2048), BF),
            pltpu.VMEM((4, 8, 128), F32),
            pltpu.VMEM((2, 16, 16, 128), F32),
            pltpu.VMEM((16, 256), F32),
            pltpu.VMEM((2, BLOCK, 512), BF),
            pltpu.SemaphoreType.DMA((6,)),
            pltpu.SemaphoreType.DMA((N1_COPIES,)),
            pltpu.SemaphoreType.DMA((N1_COPIES,)),
        ],
        compiler_params=pltpu.CompilerParams(
            collective_id=1, has_side_effects=True, vmem_limit_bytes=VMEM_LIMIT
        ),
        name="gather_and_project",
    )(*operands)

SPAN = 512
TOGETHER = 4


def first_blocks(lengths_ref, first_ref):
    base = lax.axis_index("dp") * 4
    end = jnp.int32(0)
    first = [jnp.int32(0)] * 4
    for i in range(32):
        end = end + lengths_ref[i]
        first = [jnp.where(end <= base + b, end, first[b]) for b in range(4)]
    for b in range(4):
        first_ref[b] = first[b] - base + 16


def heads_across(tile):
    head = lax.broadcasted_iota(jnp.int32, tile.shape, 1) // HEAD_DIM
    return jnp.concatenate([jnp.where(head == h, tile, 0.0) for h in range(4)], axis=0)


def heads_together(tile):
    head = lax.broadcasted_iota(jnp.int32, (BLOCK, 256), 1) // HEAD_DIM
    return sum(jnp.where(head == h, tile[h * BLOCK:(h + 1) * BLOCK], 0.0) for h in range(4))


def causal(scores):
    query = lax.rem(lax.broadcasted_iota(jnp.int32, scores.shape, 0), BLOCK)
    key = lax.broadcasted_iota(jnp.int32, scores.shape, 1)
    return jnp.where(key <= query + (SPAN - BLOCK), scores, -1e30)


def outside(block, first):
    lane = lax.broadcasted_iota(jnp.int32, (1, SPAN), 1)
    return jnp.where(lane < (first - block) * BLOCK, -1e30, 0.0)


def parts(tile):
    return [tile[:, i * 128:(i + 1) * 128] for i in range(SPAN // 128)]


def attend_kernel(lengths_ref, q_ref, kv_ref, ctx_ref, lse_ref, scores, top, total, acc, tall, first_ref):
    first_blocks(lengths_ref, first_ref)
    tops, totals, accs, talls = (
        [ref.at[i] for i in range(TOGETHER)] for ref in (top, total, acc, tall)
    )

    def query_blocks(group, carry):
        blocks = [group * TOGETHER + i for i in range(TOGETHER)]
        firsts = [first_ref[b] for b in blocks]
        for i, b in enumerate(blocks):
            talls[i][...] = heads_across(q_ref[rows(b * BLOCK, BLOCK), :].astype(F32) * 0.125).astype(BF)

        def left_of(i, pair):
            return 17 + blocks[i] - (pair + 1) * (SPAN // BLOCK)

        def score(i, pair):
            left = left_of(i, pair)
            tile = nt(talls[i][...], kv_ref[rows(left * BLOCK, SPAN, BLOCK), 0:256])
            return tile + outside(left, firsts[i])

        for i in range(TOGETHER):
            tile = causal(score(i, 0))
            scores[i, 0] = tile
            tops[i][...] = functools.reduce(jnp.maximum, parts(tile))

        def more(pair, carry):
            for i in range(TOGETHER):
                tile = score(i, pair)
                scores[i, pair] = tile
                tops[i][...] = functools.reduce(jnp.maximum, parts(tile), tops[i][...])
            return carry

        counts = [(16 + b - first) // (SPAN // BLOCK) + 1 for b, first in zip(blocks, firsts)]
        pairs = functools.reduce(jnp.maximum, counts)
        lax.fori_loop(1, pairs, more, 0)
        for i in range(TOGETHER):
            tops[i][...] = jnp.broadcast_to(jnp.max(tops[i][...], axis=1, keepdims=True), (512, 128))
            totals[i][...] = jnp.zeros((512, 128), F32)
            accs[i][...] = jnp.zeros((512, 256), F32)

        def weigh(pair, carry):
            for i in range(TOGETHER):
                weights = [jnp.exp(part - tops[i][...]) for part in parts(scores[i, pair])]
                totals[i][...] += sum(weights)
                weights = jnp.concatenate([part.astype(BF) for part in weights], axis=1)
                accs[i][...] += nn(weights, kv_ref[rows(left_of(i, pair) * BLOCK, SPAN, BLOCK), 256:512])
            return carry

        lax.fori_loop(0, pairs, weigh, 0)
        for i, b in enumerate(blocks):
            sums = jnp.sum(totals[i][...], axis=1, keepdims=True)
            lse_ref[b] = tops[i][...] + jnp.log(sums)
            ctx_ref[rows(b * BLOCK, BLOCK), :] = heads_together(accs[i][...] * (1.0 / sums)).astype(BF)
        return carry

    lax.fori_loop(0, 4 // TOGETHER, query_blocks, 0)


def call_attend(lengths, q, kv):
    return pl.pallas_call(
        attend_kernel,
        out_shape=(
            jax.ShapeDtypeStruct((GROUP, 256), BF),
            jax.ShapeDtypeStruct((4, 512, 128), F32),
        ),
        in_specs=[pl.BlockSpec(memory_space=pltpu.SMEM)] + vm(2),
        out_specs=tuple(vm(2)),
        scratch_shapes=[
            pltpu.VMEM((TOGETHER, 2048 // SPAN, 512, SPAN), F32),
            pltpu.VMEM((TOGETHER, 512, 128), F32),
            pltpu.VMEM((TOGETHER, 512, 128), F32),
            pltpu.VMEM((TOGETHER, 512, 256), F32),
            pltpu.VMEM((TOGETHER, 512, 256), BF),
            pltpu.SMEM((4,), jnp.int32),
        ],
        compiler_params=pltpu.CompilerParams(vmem_limit_bytes=VMEM_LIMIT),
        name="attend",
    )(lengths, q, kv)


def attend_back_kernel(
    lengths_ref, q_ref, kv_ref, ctx_ref, lse_ref, dctx_ref, dq_ref, dkv_ref,
    dkv, acc, tall_q, tall_g, inner, first_ref,
):
    first_blocks(lengths_ref, first_ref)
    accs, talls_q, talls_g, inners = (
        [ref.at[i] for i in range(TOGETHER)] for ref in (acc, tall_q, tall_g, inner)
    )

    def clear(j, carry):
        dkv[rows(j * BLOCK, BLOCK), :] = jnp.zeros((BLOCK, 512), F32)
        return carry

    lax.fori_loop(0, 20, clear, 0)

    def query_blocks(group, carry):
        blocks = [group * TOGETHER + i for i in range(TOGETHER)]
        firsts = [first_ref[b] for b in blocks]
        for i, b in enumerate(blocks):
            block = rows(b * BLOCK, BLOCK)
            grads = dctx_ref[block, :].astype(F32)
            talls_q[i][...] = heads_across(q_ref[block, :].astype(F32) * 0.125).astype(BF)
            talls_g[i][...] = heads_across(grads).astype(BF)
            product = heads_across(grads * ctx_ref[block, :].astype(F32))
            inners[i][...] = jnp.broadcast_to(jnp.sum(product, axis=1, keepdims=True), (512, 128))
            accs[i][...] = jnp.zeros((512, 256), F32)

        def step(pair, mask):
            low, weights, keys = [], [], []
            for i, b in enumerate(blocks):
                left = 17 + b - (pair + 1) * (SPAN // BLOCK)
                keys.append(rows(left * BLOCK, SPAN, BLOCK))
                tile = nt(talls_q[i][...], kv_ref[keys[i], 0:256]) + outside(left, firsts[i])
                if mask:
                    tile = causal(tile)
                weight = jnp.exp(tile - jnp.concatenate([lse_ref[b]] * (SPAN // 128), axis=1))
                grad = nt(talls_g[i][...], kv_ref[keys[i], 256:512])
                inner_row = jnp.concatenate([inners[i][...]] * (SPAN // 128), axis=1)
                low.append((weight * (grad - inner_row)).astype(BF))
                weights.append(weight.astype(BF))
                accs[i][...] += nn(low[i], kv_ref[keys[i], 0:256])
            for i in range(TOGETHER):
                dkv[keys[i], 0:256] += tn(low[i], talls_q[i][...])
                dkv[keys[i], 256:512] += tn(weights[i], talls_g[i][...])

        step(0, True)

        def full(pair, carry):
            step(pair, False)
            return carry

        counts = [(16 + b - first) // (SPAN // BLOCK) + 1 for b, first in zip(blocks, firsts)]
        lax.fori_loop(1, functools.reduce(jnp.maximum, counts), full, 0)
        for i, b in enumerate(blocks):
            dq_ref[rows(b * BLOCK, BLOCK), :] = heads_together(accs[i][...] * 0.125).astype(BF)
        return carry

    lax.fori_loop(0, 4 // TOGETHER, query_blocks, 0)

    def store(j, carry):
        block = rows(j * BLOCK, BLOCK)
        dkv_ref[block, :] = dkv[block, :].astype(BF)
        return carry

    lax.fori_loop(0, 20, store, 0)


def call_attend_back(lengths, q, kv, ctx, lse, dctx):
    return pl.pallas_call(
        attend_back_kernel,
        out_shape=(
            jax.ShapeDtypeStruct((GROUP, 256), BF),
            jax.ShapeDtypeStruct((5 * GROUP, 512), BF),
        ),
        in_specs=[pl.BlockSpec(memory_space=pltpu.SMEM)] + vm(5),
        out_specs=tuple(vm(2)),
        scratch_shapes=[
            pltpu.VMEM((5 * GROUP, 512), F32),
            pltpu.VMEM((TOGETHER, 512, 256), F32),
            pltpu.VMEM((TOGETHER, 512, 256), BF),
            pltpu.VMEM((TOGETHER, 512, 256), BF),
            pltpu.VMEM((TOGETHER, 512, 128), F32),
            pltpu.SMEM((4,), jnp.int32),
        ],
        compiler_params=pltpu.CompilerParams(vmem_limit_bytes=VMEM_LIMIT),
        name="attend_back",
    )(lengths, q, kv, ctx, lse, dctx)


class PlaneScatter:
    copies_needed = 18

    def __init__(self, copies, place, g, scratch):
        self.copies, self.place, self.g = copies, place, g
        self.land, self.far, self.near, self.t, self.far2, self.near2, self.last, self.rest = scratch
        self.half = g.shape[1] // 2

    @staticmethod
    def scratch(width):
        half = width // 2
        return [
            pltpu.VMEM((1024, half), BF),
            pltpu.VMEM((2, 2, 64, half), BF),
            pltpu.VMEM((2, 4, 64, half), BF),
            pltpu.VMEM((4, 64, half), BF),
            pltpu.VMEM((2, 32, half), BF),
            pltpu.VMEM((2, 64, half), BF),
            pltpu.VMEM((32, half), F32),
            pltpu.VMEM((32, half), F32),
        ]

    def dev(self, axis, step):
        c = self.place.c
        if axis == 0:
            return self.place.at(dx=(1 - c) * step, dy=c * step)
        return self.place.at(dx=c * step, dy=(1 - c) * step)

    def first(self, step):
        p = self.place
        return lax.rem(p.x * (1 - p.c) + p.y * p.c + step + 4, 4)

    def second(self, step):
        p = self.place
        return lax.rem(p.y * (1 - p.c) + p.x * p.c + step + 4, 4)

    def block(self, f, s):
        c = self.place.c
        x, y = f * (1 - c) + s * c, s * (1 - c) + f * c
        return rows((x * 4 + y) * 64, 64)

    def start(self):
        c = self.place.c
        other = pl.ds(pl.multiple_of((1 - c) * self.half, 128), self.half)
        self.swap = self.copies.put(self.g.at[:, other], self.land, self.place.at(flip=True))

    def step1(self):
        self.swap.wait_recv()
        mine = pl.ds(pl.multiple_of(self.place.c * self.half, 128), self.half)
        self.mine = mine

        def join(k, carry):
            f = self.first(2 + k // 4)
            block = self.block(f, lax.rem(k, 4))
            self.land[block, :] = (self.land[block, :].astype(F32) + self.g[block, mine].astype(F32)).astype(BF)
            return carry

        lax.fori_loop(0, 4, join, 0)
        self.out = []
        for s in range(4):
            to = self.dev(0, 1 if s < 2 else -1)
            self.out.append(
                self.copies.put(self.land.at[self.block(self.first(2), s)], self.far.at[s // 2, s % 2], to)
            )
        lax.fori_loop(4, 16, join, 0)

    def step2(self):
        self.out2 = []
        for side, step in ((0, 1), (1, -1)):
            f = self.first(step)
            for s in range(4):
                block = self.block(f, s)
                if s // 2 == side:
                    self.out[s].wait_recv()
                    self.land[block, :] = (
                        self.land[block, :].astype(F32) + self.far[side, s % 2].astype(F32)
                    ).astype(BF)
                self.out2.append(
                    self.copies.put(self.land.at[block], self.near.at[side, s], self.dev(0, step))
                )

    def step3(self):
        f = self.first(0)
        for copy in self.out2:
            copy.wait_recv()

        def total(k, carry):
            s = self.second(2 + k)
            self.t[s] = (
                self.land[self.block(f, s), :].astype(F32)
                + self.near[0, s].astype(F32)
                + self.near[1, s].astype(F32)
            ).astype(BF)
            return carry

        lax.fori_loop(0, 1, total, 0)
        s = self.second(2)
        self.up = self.copies.put(self.t.at[s, 0:32], self.far2.at[0], self.dev(1, 1))
        self.down = self.copies.put(self.t.at[s, 32:64], self.far2.at[1], self.dev(1, -1))
        lax.fori_loop(1, 4, total, 0)

    def step4(self):
        s = self.second(1)
        self.up.wait_recv()
        self.t[s, 0:32] = (self.t[s, 0:32].astype(F32) + self.far2[0].astype(F32)).astype(BF)
        self.up2 = self.copies.put(self.t.at[s], self.near2.at[0], self.dev(1, 1))
        s = self.second(-1)
        self.down.wait_recv()
        self.t[s, 32:64] = (self.t[s, 32:64].astype(F32) + self.far2[1].astype(F32)).astype(BF)
        self.down2 = self.copies.put(self.t.at[s], self.near2.at[1], self.dev(1, -1))

    def part(self, c):
        half = rows(c * 32, 32)
        return (
            self.t[self.second(0), half].astype(F32)
            + self.near2[0, half].astype(F32)
            + self.near2[1, half].astype(F32)
        )

    def step5(self):
        self.up2.wait_recv()
        self.down2.wait_recv()
        c = self.place.c
        self.last[...] = self.part(1 - c)
        self.back = self.copies.put(self.last, self.rest, self.place.at(flip=True))

    def step6(self, out):
        out[:, self.mine] = self.part(self.place.c)
        self.back.wait_recv()
        other = pl.ds(pl.multiple_of((1 - self.place.c) * self.half, 128), self.half)
        out[:, other] = self.rest[...]


class QuickScatter:
    copies_needed = 17

    def __init__(self, copies, place, g, scratch):
        self.copies, self.place, self.g = copies, place, g
        self.land, self.near, self.t, self.near2, self.last, self.rest = scratch
        self.half = g.shape[1] // 2

    @staticmethod
    def scratch(width):
        half = width // 2
        return [
            pltpu.VMEM((1024, half), BF),
            pltpu.VMEM((3, 4, 64, half), BF),
            pltpu.VMEM((4, 64, half), BF),
            pltpu.VMEM((3, 64, half), BF),
            pltpu.VMEM((32, half), F32),
            pltpu.VMEM((32, half), F32),
        ]

    dev, first, second, block, start = (
        PlaneScatter.dev, PlaneScatter.first, PlaneScatter.second, PlaneScatter.block, PlaneScatter.start
    )

    def step1(self):
        self.swap.wait_recv()
        self.mine = pl.ds(pl.multiple_of(self.place.c * self.half, 128), self.half)
        self.out = []
        for i, step in enumerate((2, 1, -1, 0)):
            f = self.first(step)

            def join(s, carry):
                block = self.block(f, s)
                self.land[block, :] = (
                    self.land[block, :].astype(F32) + self.g[block, self.mine].astype(F32)
                ).astype(BF)
                return carry

            lax.fori_loop(0, 4, join, 0)
            if step:
                for s in range(4):
                    self.out.append(
                        self.copies.put(self.land.at[self.block(f, s)], self.near.at[i, s], self.dev(0, step))
                    )

    def step2(self):
        for copy in self.out:
            copy.wait_recv()
        f = self.first(0)

        def total(s, carry):
            value = self.land[self.block(f, s), :].astype(F32)
            for i in range(3):
                value = value + self.near[i, s].astype(F32)
            self.t[s] = value.astype(BF)
            return carry

        lax.fori_loop(0, 4, total, 0)
        self.out2 = [
            self.copies.put(self.t.at[self.second(step)], self.near2.at[i], self.dev(1, step))
            for i, step in enumerate((2, 1, -1))
        ]

    def part(self, c):
        half = rows(c * 32, 32)
        value = self.t[self.second(0), half].astype(F32)
        for i in range(3):
            value = value + self.near2[i, half].astype(F32)
        return value

    def step3(self):
        for copy in self.out2:
            copy.wait_recv()
        self.last[...] = self.part(1 - self.place.c)
        self.back = self.copies.put(self.last, self.rest, self.place.at(flip=True))

    step4 = PlaneScatter.step6


class RingScatter:
    copies_needed = 4

    def __init__(self, copies, place, scratch):
        self.copies, self.place = copies, place
        self.part, self.far, self.near = scratch

    @staticmethod
    def scratch():
        return [
            pltpu.VMEM((3, BLOCK, D), BF),
            pltpu.VMEM((2, 64, D), BF),
            pltpu.VMEM((2, BLOCK, D), BF),
        ]

    def send_far(self):
        p, c = self.place, self.copies
        self.up = c.put(self.part.at[2, 0:64], self.far.at[0], p.at(dz=1))
        self.down = c.put(self.part.at[2, 64:128], self.far.at[1], p.at(dz=-1))

    def send_above(self):
        self.up.wait_recv()
        self.part[0, 0:64] = (self.part[0, 0:64].astype(F32) + self.far[0].astype(F32)).astype(BF)
        self.up2 = self.copies.put(self.part.at[0], self.near.at[0], self.place.at(dz=1))

    def send_below(self):
        self.down.wait_recv()
        self.part[1, 64:128] = (self.part[1, 64:128].astype(F32) + self.far[1].astype(F32)).astype(BF)
        self.down2 = self.copies.put(self.part.at[1], self.near.at[1], self.place.at(dz=-1))

    def received(self):
        self.up2.wait_recv()
        self.down2.wait_recv()
        return self.near[0].astype(F32) + self.near[1].astype(F32)


class RingReturn:
    copies_needed = 6

    def __init__(self, copies, place, scratch):
        self.copies, self.place = copies, place
        self.part, self.near, self.mid, self.far = scratch

    @staticmethod
    def scratch():
        return [
            pltpu.VMEM((3, BLOCK, D), BF),
            pltpu.VMEM((2, BLOCK, D), BF),
            pltpu.VMEM((2, 64, D), BF),
            pltpu.VMEM((BLOCK, D), BF),
        ]

    def send_above(self):
        self.up = self.copies.put(self.part.at[0], self.near.at[0], self.place.at(dz=1))

    def send_below(self):
        self.down = self.copies.put(self.part.at[1], self.near.at[1], self.place.at(dz=-1))

    def send_far(self):
        p, c = self.place, self.copies
        self.up1 = c.put(self.part.at[2, 0:64], self.mid.at[0], p.at(dz=1))
        self.down1 = c.put(self.part.at[2, 64:128], self.mid.at[1], p.at(dz=-1))

    def pass_on(self):
        p, c = self.place, self.copies
        self.up1.wait_recv()
        self.up2 = c.put(self.mid.at[0], self.far.at[0:64], p.at(dz=1))
        self.down1.wait_recv()
        self.down2 = c.put(self.mid.at[1], self.far.at[64:128], p.at(dz=-1))

    def received(self):
        for copy in (self.up, self.down, self.up2, self.down2):
            copy.wait_recv()
        return self.near[0].astype(F32) + self.near[1].astype(F32) + self.far[...].astype(F32)


def norm_back(hat, scale, grad, gain):
    inner = grad * gain
    mean = jnp.mean(inner, axis=-1, keepdims=True)
    along = jnp.mean(inner * hat, axis=-1, keepdims=True)
    return (
        scale * (inner - mean - hat * along),
        jnp.sum(grad * hat, axis=0, keepdims=True),
        jnp.sum(grad, axis=0, keepdims=True),
    )


def weight_grad(left, right, out, first):
    width = right.shape[1]

    def tile(k, carry):
        turned = left[:, pl.ds(pl.multiple_of(k * 256, 256), 256)].astype(F32).T.astype(BF)
        out[rows(k * 256, 256), first:first + width] = nn(turned, right[...]).astype(BF)
        return carry

    lax.fori_loop(0, 4, tile, 0)


def middle_kernel(
    x_ref, ctx_ref, vec_ref, wo_any, wmlp_any, cotg_any,
    gafter_ref, gaf_ref, dctx_ref, sums_ref, res_ref, outs_ref, dw_any,
    wo, wmlp, cotg, ctxf, n2g, act, dpre, dact, back, own, after, dw, dctx, io_sem, send_sem, recv_sem,
    *scratch,
):
    p = Place()
    loads = [
        pltpu.make_async_copy(source, target, io_sem.at[i])
        for i, (source, target) in enumerate(((wo_any, wo), (cotg_any, cotg), (wmlp_any, wmlp)))
    ]
    for load in loads:
        load.start()
    greet([p.at(dz=1), p.at(dz=-1), p.at(dz=2)])
    copies = Copies(send_sem, recv_sem)
    backs = RingReturn(copies, p, scratch[0:4])

    def block(dz):
        return rows(lax.rem(p.z + dz + 4, 4) * BLOCK, BLOCK)

    swaps = [
        copies.put(ctx_ref.at[block(dz)], ctxf.at[p.z], p.at(dz=dz)) for dz in (2, 1, -1)
    ]
    ctxf[p.z] = ctx_ref[block(0), :]
    for load in loads:
        load.wait()

    def act_grad(t, carry):
        cols = pl.ds(pl.multiple_of(1024 + t * 256, 256), 256)
        dact[:, pl.ds(pl.multiple_of(t * 256, 256), 256)] = nn(cotg[...], wmlp[:, cols])
        return carry

    lax.fori_loop(0, 4, act_grad, 0)
    for copy in swaps:
        copy.wait_recv()
    total = x_ref[...].astype(F32) + vec_ref[4:5, :]
    for k in range(4):
        total = total + nt(ctxf[k], wo[k * D:(k + 1) * D, :])
    after[...] = total
    hat, scale = normalised(after[...])
    n2g[block(0), :] = (hat * vec_ref[1:2, :] + vec_ref[3:4, :]).astype(BF)
    ring = RingGather(copies, p, n2g)
    ring.start()

    def mlp(dz, put_back):
        here = block(dz)

        def hidden(t, carry):
            cols = pl.ds(pl.multiple_of(t * 256, 256), 256)
            pre = nn(n2g[here, :], wmlp[:, cols]) + vec_ref[8:9, cols]
            square = pre * pre
            bend = jnp.tanh(0.7978845608028654 * pre * (1.0 + 0.044715 * square))
            act[here, cols] = (0.5 * pre * (1.0 + bend)).astype(BF)
            slope = 0.5 * (1.0 + bend) + 0.5 * pre * (1.0 - bend * bend) * (
                0.7978845608028654 * (1.0 + 0.134145 * square)
            )
            dpre[here, cols] = (dact[here, cols] * slope).astype(BF)
            return carry

        lax.fori_loop(0, 4, hidden, 0)

        def project(t, carry):
            cols = pl.ds(pl.multiple_of(t * 256, 256), 256)
            put_back(cols, nt(dpre[here, :], wmlp[cols, 0:1024]))
            return carry

        lax.fori_loop(0, 4, project, 0)

    def into(k):
        def put(cols, value):
            backs.part[k, :, cols] = value.astype(BF)

        return put

    def keep(cols, value):
        own[:, cols] = value

    mlp(0, keep)
    ring.below()
    ring.above()
    mlp(-1, into(1))
    backs.send_below()
    mlp(1, into(0))
    backs.send_above()
    ring.far()
    mlp(2, into(2))
    backs.send_far()
    weight_grad(n2g, dpre, dw, 0)
    backs.pass_on()
    weight_grad(cotg, act, dw, 1024)
    save = pltpu.make_async_copy(dw, dw_any, io_sem.at[3])
    save.start()
    grad = own[...] + backs.received()
    hat, scale = normalised(after[...])
    grad_in, gain, shift = norm_back(hat, scale, grad, vec_ref[1:2, :])
    residual = cotg[block(0), :].astype(F32)
    back[...] = grad_in + residual
    gaf_ref[...] = back[...].astype(BF)
    for k in (2, 1, 3, 0):
        owner = lax.rem(p.z + k, 4)
        part = nn(gaf_ref[...], wo[rows(owner * D, D), :]).astype(BF)
        if k:
            dctx[k] = part
            swaps.append(copies.put(dctx.at[k], dctx_ref.at[block(0)], p.at(dz=k)))
        else:
            dctx_ref[block(0), :] = part
    sums_ref[...] = jnp.zeros_like(sums_ref)
    sums_ref[0:1, :] = gain
    sums_ref[1:2, :] = shift
    sums_ref[2:3, :] = jnp.sum(back[...], axis=0, keepdims=True)
    sums_ref[3:4, :] = jnp.sum(residual, axis=0, keepdims=True)
    sums_ref[4:5, :] = jnp.sum(dpre[...].astype(F32), axis=0, keepdims=True)
    gafter_ref[...] = back[...]

    def output_part(t, carry):
        cols = pl.ds(pl.multiple_of(t * 256, 256), 256)
        for k, dz in enumerate((1, -1, 2)):
            outs_ref[k, :, cols] = nt(act[block(dz), :], wmlp[cols, 1024:2048]).astype(BF)
        res_ref[:, cols] = (
            after[:, cols] + vec_ref[5:6, cols] + nt(act[block(0), :], wmlp[cols, 1024:2048])
        )
        return carry

    lax.fori_loop(0, 4, output_part, 0)
    for copy in swaps[3:]:
        copy.wait_recv()
    save.wait()
    copies.finish()


N3_COPIES = 6 + 4 + 6


def call_middle(*operands):
    shape = jax.ShapeDtypeStruct
    return pl.pallas_call(
        middle_kernel,
        out_shape=(
            shape((BLOCK, D), F32),
            shape((BLOCK, D), BF),
            shape((GROUP, 256), BF),
            shape((8, D), F32),
            shape((BLOCK, D), F32),
            shape((3, BLOCK, D), BF),
            shape((D, 2048), BF),
        ),
        in_specs=vm(3) + far_memory(3),
        out_specs=tuple(vm(6) + far_memory(1)),
        scratch_shapes=[
            pltpu.VMEM((4 * D, 256), BF),
            pltpu.VMEM((D, 2048), BF),
            pltpu.VMEM((GROUP, D), BF),
            pltpu.VMEM((4, BLOCK, 256), BF),
            pltpu.VMEM((GROUP, D), BF),
            pltpu.VMEM((GROUP, D), BF),
            pltpu.VMEM((GROUP, D), BF),
            pltpu.VMEM((GROUP, D), F32),
            pltpu.VMEM((BLOCK, D), F32),
            pltpu.VMEM((BLOCK, D), F32),
            pltpu.VMEM((BLOCK, D), F32),
            pltpu.VMEM((D, 2048), BF),
            pltpu.VMEM((4, BLOCK, 256), BF),
            pltpu.SemaphoreType.DMA((4,)),
            pltpu.SemaphoreType.DMA((N3_COPIES,)),
            pltpu.SemaphoreType.DMA((N3_COPIES,)),
            *RingReturn.scratch(),
        ],
        compiler_params=pltpu.CompilerParams(
            collective_id=2, has_side_effects=True, vmem_limit_bytes=VMEM_LIMIT
        ),
        name="mlp_both_ways",
    )(*operands)


def last_kernel(
    dq_ref, dkv_ref, x_ref, vec_ref, gafter_ref, gaf_ref, ctx_ref, sums_ref, res_ref, outs_ref,
    n1_any, xg_any, wqkv_any, dw_any,
    gin_ref, out_ref, early_ref, late_ref, small_ref,
    n1, xg, wqkv, gafg, part, cross, hand, land, mid, fin, dqkv, early, late, own, zsum, ysum, csum,
    io_sem, send_sem, recv_sem, *scratch,
):
    p = Place()
    loads = [
        pltpu.make_async_copy(source, target, io_sem.at[i])
        for i, (source, target) in enumerate(
            ((dw_any, early.at[:, 0:2048]), (n1_any, n1), (wqkv_any, wqkv), (xg_any, xg))
        )
    ]
    for load in loads:
        load.start()
    gafg[rows(p.z * BLOCK, BLOCK), :] = gaf_ref[...]
    greet(
        [p.at(dz=1), p.at(dz=-1), p.at(dz=2), p.at(dx=1), p.at(dx=-1), p.at(dx=2),
         p.at(dy=1), p.at(dy=-1), p.at(dy=2), p.at(flip=True), p.linear(1), p.linear(-1),
         p.beside(-1, -2), p.beside_source(-2, 1)]
    )
    copies = Copies(send_sem, recv_sem)
    scatter = RingScatter(copies, p, scratch[0:3])
    outs = RingReturn(copies, p, (outs_ref,) + scratch[3:6])
    plane = PlaneScatter(copies, p, early, scratch[6:14])
    quick = QuickScatter(copies, p, late, scratch[14:20])
    sibling = p.at(flip=True)
    even = p.c == 0

    def start_of(k):
        return lax.rem(p.z + k, 4) * BLOCK

    def block(k):
        return rows(start_of(k), BLOCK)

    order = (2, 1, 3, 0)
    crossing = []
    for k in order:
        for side in range(2):
            source = dkv_ref.at[rows((1 + 2 * side) * GROUP + start_of(k), BLOCK)]
            crossing.append(copies.put(source, cross.at[side, block(k)], sibling))
    ring = RingGather(copies, p, gafg)
    ring.start()
    outs.send_above()
    outs.send_below()
    outs.send_far()
    for load in loads:
        load.wait()
    weight_grad(n1, dq_ref, early, 2048)
    plane.start()
    dqkv[:, 0:256] = dq_ref[...]
    far, near = {}, {}
    for k in (3, 2, 0, 1):
        i = order.index(k)
        crossing[2 * i].wait_recv()
        crossing[2 * i + 1].wait_recv()
        low = cross[0, block(k)].astype(F32)
        high = cross[1, block(k)].astype(F32)
        hand[0, block(k)] = (
            dkv_ref[rows(start_of(k), BLOCK), :].astype(F32) + jnp.where(even, 0.0, low)
        ).astype(BF)
        if i < 2:
            far[k] = copies.put(hand.at[0, block(k)], mid.at[i], p.at(dy=1))
        else:
            far[k] = copies.put(hand.at[0, block(k)], land.at[0, block(k)], p.linear(-1))
        part[0, block(k)] = dkv_ref[rows(2 * GROUP + start_of(k), BLOCK), :].astype(F32) + jnp.where(even, low, high)
        part[1, block(k)] = dkv_ref[rows(4 * GROUP + start_of(k), BLOCK), :].astype(F32) + jnp.where(even, high, 0.0)
    for k in order[:2]:
        hand[1, block(k)] = part[0, block(k)].astype(BF)
        near[k] = copies.put(hand.at[1, block(k)], land.at[1, block(k)], p.linear(-1))
    for i, k in enumerate(order[:2]):
        far[k].wait_recv()
        far[k] = copies.put(mid.at[i], fin.at[i], p.beside(-1, -2))
    for k in order[2:]:
        far[k].wait_recv()
        hand[1, block(k)] = (part[0, block(k)] + land[0, block(k)].astype(F32)).astype(BF)
        near[k] = copies.put(hand.at[1, block(k)], land.at[1, block(k)], p.linear(-1))
    ring.below()
    ring.above()
    outs.pass_on()
    plane.step1()
    ring.far()
    weight_grad(gafg, ctx_ref, late, 512)
    small_ref[...] = jnp.zeros_like(small_ref)
    small_ref[8:9, :] = sums_ref[4:5, :]
    small_ref[9:10, 0:256] = jnp.sum(dq_ref[...].astype(F32), axis=0, keepdims=True)
    small_ref[1:2, :] = sums_ref[0:1, :]
    small_ref[3:6, :] = sums_ref[1:4, :]
    out_ref[...] = res_ref[...] + outs.received()
    plane.step2()

    for k in order:
        near[k].wait_recv()
        value = part[1, block(k)] + land[1, block(k)].astype(F32)
        if k in order[:2]:
            far[k].wait_recv()
            value = value + fin[order.index(k)].astype(F32)
        dqkv[block(k), 256:768] = value.astype(BF)
    weight_grad(n1, dqkv.at[:, 256:768], late, 0)
    quick.start()

    def grad_part(k):
        return nt(dqkv[block(k), :], wqkv[...])

    def tally(k, grad):
        hat, _ = normalised(xg[block(k), :].astype(F32))
        small_ref[0:1, :] += jnp.sum(grad * hat, axis=0, keepdims=True)
        small_ref[2:3, :] += jnp.sum(grad, axis=0, keepdims=True)

    grad = grad_part(2)
    scatter.part[2] = grad.astype(BF)
    scatter.send_far()
    tally(2, grad)
    above = grad_part(1)
    scatter.part[0] = above.astype(BF)
    below = grad_part(3)
    scatter.part[1] = below.astype(BF)
    scatter.send_above()
    scatter.send_below()
    plane.step3()
    quick.step1()
    tally(1, above)
    tally(3, below)
    own[...] = grad_part(0)
    tally(0, own[...])
    top = small_ref.at[0:8]
    sends = [copies.put(top, zsum.at[i], p.at(dz=dz)) for i, dz in enumerate((1, -1, 2))]
    small_ref[10:11, 0:256] = jnp.sum(dqkv[:, 512:768].astype(F32), axis=0, keepdims=True)
    plane.step4()
    for copy in sends:
        copy.wait_recv()
    copies.settle(*sends)
    small_ref[0:8, :] = small_ref[0:8, :] + zsum[0] + zsum[1] + zsum[2]
    send = copies.put(small_ref, csum.at[0], sibling)
    quick.step2()
    hat, scale = normalised(x_ref[...].astype(F32))
    back, _, _ = norm_back(hat, scale, own[...] + scatter.received(), vec_ref[0:1, :])
    gin_ref[...] = gafter_ref[...] + back
    send.wait_recv()
    csum[1] = small_ref[...] + csum[0]
    sends = [copies.put(csum.at[1], ysum.at[i], p.at(dy=dy)) for i, dy in enumerate((1, -1, 2))]
    plane.step5()
    quick.step3()
    for copy in sends:
        copy.wait_recv()
    csum[2] = csum[1] + ysum[0] + ysum[1] + ysum[2]
    sends = [copies.put(csum.at[2], ysum.at[3 + i], p.at(dx=dx)) for i, dx in enumerate((1, -1, 2))]
    plane.step6(early_ref)
    quick.step4(late_ref)
    for copy in sends:
        copy.wait_recv()
    copies.settle(send)
    small_ref[...] = csum[2] + ysum[3] + ysum[4] + ysum[5]
    copies.finish()


N5_COPIES = 8 + 4 + 6 + 4 + 4 + 2 + 4 + 18 + 17 + 3 + 1 + 3 + 3


def call_last(*operands):
    shape = jax.ShapeDtypeStruct
    return pl.pallas_call(
        last_kernel,
        out_shape=(
            shape((BLOCK, D), F32),
            shape((BLOCK, D), F32),
            shape((32, 2304), F32),
            shape((32, 768), F32),
            shape((16, D), F32),
        ),
        in_specs=vm(10) + far_memory(4),
        out_specs=tuple(vm(5)),
        scratch_shapes=[
            pltpu.VMEM((GROUP, D), BF),
            pltpu.VMEM((GROUP, D), BF),
            pltpu.VMEM((D, 768), BF),
            pltpu.VMEM((GROUP, D), BF),
            pltpu.VMEM((2, GROUP, 512), F32),
            pltpu.VMEM((2, GROUP, 512), BF),
            pltpu.VMEM((2, GROUP, 512), BF),
            pltpu.VMEM((2, GROUP, 512), BF),
            pltpu.VMEM((2, BLOCK, 512), BF),
            pltpu.VMEM((2, BLOCK, 512), BF),
            pltpu.VMEM((GROUP, 768), BF),
            pltpu.VMEM((D, 2304), BF),
            pltpu.VMEM((D, 768), BF),
            pltpu.VMEM((BLOCK, D), F32),
            pltpu.VMEM((3, 8, D), F32),
            pltpu.VMEM((6, 16, D), F32),
            pltpu.VMEM((3, 16, D), F32),
            pltpu.SemaphoreType.DMA((4,)),
            pltpu.SemaphoreType.DMA((N5_COPIES,)),
            pltpu.SemaphoreType.DMA((N5_COPIES,)),
            *RingScatter.scratch(),
            *RingReturn.scratch()[1:],
            *PlaneScatter.scratch(2304),
            *QuickScatter.scratch(768),
        ],
        compiler_params=pltpu.CompilerParams(
            collective_id=3, has_side_effects=True, vmem_limit_bytes=VMEM_LIMIT
        ),
        name="project_back",
    )(*operands)


def finish_kernel(
    out_ref, gin_ref, early_ref, late_ref, small_ref,
    out, gin, wqkv, wout, wfc, wproj, bqv, bfc, gains, shifts,
):
    dp, z = lax.axis_index("dp"), lax.axis_index("tensor")
    out[...] = out_ref[...]
    gin[...] = gin_ref[...]
    wqkv[0] = early_ref[:, 2048:2304]
    wqkv[1] = late_ref[:, 0:256]
    wqkv[2] = late_ref[:, 256:512]
    wout[...] = late_ref[:, 512:768]
    wfc[...] = early_ref[:, 0:1024]
    wproj[...] = early_ref[:, 1024:2048]

    def pick(first, offset, width):
        lanes = pl.ds(pl.multiple_of(offset // 128 * 128, 128), 128)
        row = lax.broadcasted_iota(jnp.int32, (128, 128), 0)
        lane = lax.broadcasted_iota(jnp.int32, (128, 128), 1)
        chosen = jnp.where(row == lane + lax.rem(offset, 128), 1.0, 0.0).astype(F32)
        return exact(small_ref[first:first + 8, lanes], chosen)[:, 0:width]

    eight = pick(0, (dp * 4 + z) * 8, 8)
    gains[...] = eight[0:2]
    shifts[...] = eight[2:6]
    bqv[...] = pick(8, dp * 8, 8)[1:3]
    bfc[...] = pick(8, dp * 32, 32)[0:1]


def call_finish(*operands):
    shape = jax.ShapeDtypeStruct
    return pl.pallas_call(
        finish_kernel,
        out_shape=(
            shape((BLOCK, D), F32),
            shape((BLOCK, D), F32),
            shape((3, 32, 256), F32),
            shape((32, 256), F32),
            shape((32, 1024), F32),
            shape((32, 1024), F32),
            shape((2, 8), F32),
            shape((1, 32), F32),
            shape((2, 8), F32),
            shape((4, 8), F32),
        ),
        in_specs=vm(5),
        out_specs=tuple(vm(10)),
        compiler_params=pltpu.CompilerParams(vmem_limit_bytes=VMEM_LIMIT),
        name="lay_out",
    )(*operands)


def on_device(inputs, lengths, w_qkv, w_out, w_fc, w_proj, b_qv, b_fc, gains, shifts, cotangent):
    q, kv, vec, n1, xg, cotg, wqkv, wo, wmlp = call_first(
        inputs, cotangent, w_qkv[0].transpose(1, 0, 2), w_out[0].T, w_fc[0], w_proj[0].T,
        gains[0], shifts[0], b_qv[0], b_fc,
    )
    ctx, lse = call_attend(lengths, q, kv)
    gafter, gaf, dctx, sums, res, outs, dw_mlp = call_middle(inputs, ctx, vec, wo, wmlp, cotg)
    dq, dkv = call_attend_back(lengths, q, kv, ctx, lse, dctx)
    gin, out, early, late, small = call_last(
        dq, dkv, inputs, vec, gafter, gaf, ctx, sums, res, outs, n1, xg, wqkv, dw_mlp
    )
    out, gin, g_qkv, g_out, g_fc, g_proj, g_bqv, g_bfc, g_gains, g_shifts = call_finish(
        out, gin, early, late, small
    )
    return (
        out, gin, g_qkv.transpose(1, 0, 2)[None], g_out.T[None], g_fc[None], g_proj.T[None],
        g_bqv[None], g_bfc, g_gains[None], g_shifts[None],
    )


def solution(mesh):
    return jax.shard_map(
        on_device,
        mesh=mesh,
        in_specs=(
            P(("dp", "tensor"), None),
            P(),
            P(None, "dp", None, "tensor"),
            P(None, "tensor", "dp"),
            P(None, "dp", "tensor"),
            P(None, "tensor", "dp"),
            P(None, None, ("tensor", "dp")),
            P(None, ("tensor", "dp")),
            P(None, None, ("dp", "tensor")),
            P(None, None, ("dp", "tensor")),
            P(("dp", "tensor"), None),
        ),
        out_specs=(
            P(("dp", "tensor"), None),
            P(("dp", "tensor"), None),
            P(None, "dp", None, "tensor"),
            P(None, "tensor", "dp"),
            P(None, "dp", "tensor"),
            P(None, "tensor", "dp"),
            P(None, None, ("tensor", "dp")),
            P(None, ("tensor", "dp")),
            P(None, None, ("dp", "tensor")),
            P(None, None, ("dp", "tensor")),
        ),
        check_vma=False,
    )
```

time: 282 us -> 196 us (0.70); the launches traced: 284 us -> 193 us
  Pallas kernels: 267 us -> 192 us
  local copies, waits for them, and re-layouts: 11.3 us -> 0 us
  other arithmetic: 5.24 us -> 0 us
    pallas_call x3 -> x4, Pallas kernels: 249 us -> 178 us  [the longest x1 72.2 us: call_last(): pl.pallas_call(last_kernel, out_shape=(shape((BLOCK, D), F32), shape((BLO...]
    broadcast_in_dim x5 -> x0, local copies, waits for them, and re-layouts: 3.99 us -> none  [the longest x1 1.37 us: on_device(): dw_attn[:, 768:].T[None]]
    unnamed x11 -> x0, local copies, waits for them, and re-layouts: 3.11 us -> none
    concatenate x3 -> x0, other arithmetic: 3 us -> none  [the longest x1 1.57 us: pack_weights(): jnp.concatenate([w_qkv[0].reshape(32, 768), w_out[0].T, w_fc[0], w_proj[0...]
where the time goes in v3:
time: 196 us; the launch traced here: 193 us
  Pallas kernels  192 us (98%)
    pallas_call x1, Pallas kernels, call_last(): pl.pallas_call(last_kernel, out_shape=(shape((BLOCK, D), F32), shape((BLO...  72.2 us
    pallas_call x1, Pallas kernels, call_first(): pl.pallas_call(first_kernel, out_shape=(shape((GROUP, 256), BF), shape((5...  58.2 us
    pallas_call x1, Pallas kernels, call_middle(): pl.pallas_call(middle_kernel, out_shape=(shape((BLOCK, D), F32), shape((B...  45.2 us
    pallas_call x1, Pallas kernels, call_attend_back(): pl.pallas_call(attend_back_kernel, out_shape=(jax.ShapeDtypeStruct((GROUP...  8.3 us
    pallas_call x1, Pallas kernels, call_attend(): pl.pallas_call(attend_kernel, out_shape=(jax.ShapeDtypeStruct((GROUP, 256...  5.61 us

profile of v3, /device:TPU:0, one launch (start us, length us, event | category | flops | bytes accessed | tf_op | source)
XLA Modules:
  0.0 192.9 jit_solution(405558266505099102)
XLA Ops:
  0.6 58.2 %gather_and_project.1 = (bf16[512,256]{1,0:T(8,128)(2,1)}, bf16[2560,512]{1,0:T(8,128)(2,1)}, f32[16,1024]{1,0:T(8,128)}, bf16[512,1024]{1,0:T(8,128)(2,1)}, bf1...) custom-call(bf16[128,1024]{1,0:T(8,128)(2,1)} %x_ref.5, ...), custom_call_target="tpu_custom_call" | custom-call | tf_op jit(solution)/shard_map/gather_and_project/pallas_call | solution.py:453
  58.8 5.6 %attend.1 = (bf16[512,256]{1,0:T(8,128)(2,1)}, f32[4,512,128]{2,1,0:T(8,128)}) custom-call(s32[32]{0:T(128)} %lengths_ref.3, bf16[512,256]{1,0:T(8,128)(2,1)} %get-tuple-element.45.q_ref, bf16[2560,512]{1,0:T(8,128)(2,1)} %get-tuple-element.46.kv_ref), custom_call_target="tpu_custom_call" | custom-call | tf_op jit(solution)/shard_map/attend/pallas_call | solution.py:588
  64.5 45.2 %mlp_both_ways.1 = (f32[128,1024]{1,0:T(8,128)}, bf16[128,1024]{1,0:T(8,128)(2,1)}, bf16[512,256]{1,0:T(8,128)(2,1)}, f32[8,1024]{1,0:T(8,128)}, f32[128,1024]{1...) custom-call(bf16[128,1024]{1,0:T(8,128)(2,1)} %x_ref.5, ...), custom_call_target="tpu_custom_call" | custom-call | tf_op jit(solution)/shard_map/mlp_both_ways/pallas_call | solution.py:1143
  109.7 8.3 %attend_back.1 = (bf16[512,256]{1,0:T(8,128)(2,1)}, bf16[2560,512]{1,0:T(8,128)(2,1)}) custom-call(s32[32]{0:T(128)} %lengths_ref.3, bf16[512,256]{1,0:T(8,128)(2,1)} %get-tuple-element.45.q_ref, bf16[2560,512]{1,0:T(8,128)(2,1)} %get-tuple-element.46.kv_ref, bf16[512,256]{1,0:T(8,128)(2,1)} %get-tuple-element.47.ctx_ref, ...), custom_call_target="tpu_custom_call" | custom-call | tf_op jit(solution)/shard_map/attend_back/pallas_call | solution.py:677
  118.0 72.2 %project_back.1 = (f32[128,1024]{1,0:T(8,128)}, f32[128,1024]{1,0:T(8,128)}, f32[32,2304]{1,0:T(8,128)}, f32[32,768]{1,0:T(8,128)}, f32[16,1024]{1,0:T(8,128)}) custom-call(bf16[512,256]{1,0:T(8,128)(2,1)} %get-tuple-element.54.dq_ref, bf16[2560,512]{1,0:T(8,128)(2,1)} %get-tuple-element.55.dkv_ref, bf16[128,1024]{1,0:T(8,128)(2,1)} %x_ref.5, ...), custom_call_target="tpu_custom_call" | custom-call | tf_op jit(solution)/shard_map/project_back/pallas_call | solution.py:1344
  190.2 2.6 %lay_out.1 = (f32[128,1024]{1,0:T(8,128)}, f32[128,1024]{1,0:T(8,128)}, f32[3,32,256]{2,1,0:T(8,128)}, f32[32,256]{1,0:T(8,128)}, f32[32,1024]{1,0:T(8,128)}, /*...) custom-call(f32[128,1024]{1,0:T(8,128)} %get-tuple-element.65.out_ref, ...), custom_call_target="tpu_custom_call" | custom-call | tf_op jit(solution)/shard_map/lay_out/pallas_call | solution.py:1418
